TPU v7x, 512 devices: a whole 4x4x16 slice. The times are simulated.
512 devices in a mesh: dp: 128 (over x_hi, z, y), fsdp: 4 (over x_lo, core).
Axes of the slice: x: 4 (x_hi: 2, x_lo: 2; x = x_hi * 2 + x_lo), y: 4, z: 16, core: 2. Of those that a mesh axis runs over, the one named last changes fastest.
Arguments:
- caption_encoder_outputs: bfloat16 [24576, 1152], P(('dp', 'fsdp')), may hold values from -6 to 6
- picture_vectors: bfloat16 [24576, 1152], P(('dp', 'fsdp')), may hold values from -6 to 6
- caption_mapping_weights: bfloat16 [1152, 1152], P('fsdp'), may hold values from -0.1875 to 0.1875
- natural_exponent_coldness: float32 [1], replicated, may hold values from 4.3 to 4.7
- offset_constant: float32 [1], replicated, may hold values from -8 to -5
- objective_weighting: float32 [1], replicated, may hold values from 4096 to 16384
Outputs:
- feat_grad: bfloat16 [24576, 1152], P(('dp', 'fsdp'))
- head_grad: float32 [128, 1152, 1152], P('dp', 'fsdp')
All inputs are finite; a program needn't handle non-finite values.
Results may differ from a plain program's by a relative error of at most 0.035.
Values may be sent and summed in bfloat16 or wider, within the bound.
No kernel may reach another device: no remote copies, remote signals or barrier semaphores. Data moves between devices by JAX's collectives and lax.ppermute only.
A program may use at most 64 MiB of HBM per device.

v0:
```python
import jax
import jax.numpy as jnp
from jax import lax
from jax.sharding import PartitionSpec as P

D = 1152


epsilon = 1e-06


def body(
    caption_encoder_outputs,
    picture_vectors,
    caption_mapping_weights,
    natural_exponent_coldness,
    offset_constant,
    objective_weighting,
):
    fsdp_size = lax.axis_size("fsdp")
    cycle_size = lax.axis_size("dp")
    fsdp_index = lax.axis_index("fsdp")
    cycle_index = lax.axis_index("dp")
    local_rows = caption_encoder_outputs.shape[0]
    group_rows = fsdp_size * local_rows
    example_total_number = group_rows * cycle_size
    columns = caption_encoder_outputs
    projected = jnp.dot(
        columns,
        lax.all_gather(caption_mapping_weights, "fsdp", axis=0, tiled=True),
        preferred_element_type=jnp.float32,
    )
    text_norm = jnp.sqrt(jnp.sum(projected * projected, axis=-1, keepdims=True) + epsilon)
    unit_text = projected / text_norm
    text_embed = unit_text.astype(jnp.bfloat16)
    group_text = lax.all_gather(text_embed, "fsdp", axis=0, tiled=True)
    image_vals = picture_vectors.astype(jnp.float32)
    image_norm = jnp.sqrt(jnp.sum(image_vals * image_vals, axis=-1, keepdims=True) + epsilon)
    image_embed = (image_vals / image_norm).astype(jnp.bfloat16)
    sharpness_factor = jnp.exp(natural_exponent_coldness[0])
    added_offset_entry = offset_constant[0]
    derivative_factor = sharpness_factor * objective_weighting[0] / example_total_number
    text_ids = cycle_index * group_rows + jnp.arange(group_rows, dtype=jnp.int32)
    image_rows = lax.all_gather(image_embed, "dp", axis=0, tiled=True)
    positions = jnp.arange(image_rows.shape[0], dtype=jnp.int32)
    image_ids = (
        positions // local_rows * fsdp_size + fsdp_index
    ) * local_rows + positions % local_rows
    cosine_agreement = lax.dot_general(
        group_text, image_rows, (((1,), (1,)), ((), ())), preferred_element_type=jnp.float32
    )
    cross_affinity_table = sharpness_factor * cosine_agreement + added_offset_entry
    labels = jnp.where(text_ids[:, None] == image_ids[None, :], 1.0, -1.0).astype(jnp.float32)
    weights = (-labels * jax.nn.sigmoid(-labels * cross_affinity_table) * derivative_factor).astype(
        jnp.bfloat16
    )
    embed_grad = jnp.dot(weights, image_rows, preferred_element_type=jnp.float32)
    own_grad = lax.psum_scatter(
        embed_grad.astype(jnp.bfloat16), "fsdp", scatter_dimension=0, tiled=True
    ).astype(jnp.float32)
    radial = jnp.sum(unit_text * own_grad, axis=-1, keepdims=True)
    proj_grad = ((own_grad - unit_text * radial) / text_norm).astype(jnp.bfloat16)
    feat_grad = lax.dot_general(
        proj_grad,
        lax.all_gather(caption_mapping_weights, "fsdp", axis=0, tiled=True),
        (((1,), (1,)), ((), ())),
        preferred_element_type=jnp.float32,
    )
    rows_owned = D // fsdp_size
    columns = caption_encoder_outputs
    head_grad = lax.psum_scatter(
        lax.dot_general(
            columns, proj_grad, (((0,), (0,)), ((), ())), preferred_element_type=jnp.float32
        ).astype(jnp.bfloat16),
        "fsdp",
        scatter_dimension=0,
        tiled=True,
    ).astype(jnp.float32)
    return (feat_grad.astype(jnp.bfloat16), head_grad.reshape(1, rows_owned, D))


def solution(mesh):
    return jax.shard_map(
        body,
        mesh=mesh,
        in_specs=(P(("dp", "fsdp"), None), P(("dp", "fsdp"), None), P("fsdp", None), P(), P(), P()),
        out_specs=(P(("dp", "fsdp"), None), P("dp", "fsdp", None)),
        check_vma=False,
    )
```

profile of v0, /device:TPU:1, one launch (start us, length us, event | category | flops | bytes accessed | tf_op | source)
XLA Modules:
  0.0 437.8 jit_solution(14766095887421989676)
XLA Ops:
  7.2 0.0 copy-start
  7.2 0.0 all-gather.3.cloned.1.call-start
  7.2 0.7 all-gather.3.cloned.1.call-update
  7.9 0.0 all-gather.5.cloned.1.call-start
  8.0 1.0 fusion.10
  9.0 1.6 fusion.11
  10.6 0.0 all-gather.5.cloned.1.call-update
  10.7 0.0 reduce-scatter.5.cloned.1.call-start
  12.7 44.5 %all-gather.3.cloned.1.call-done = bf16[1152,1152]{1,0:T(8,128)(2,1)} async-done(((bf16[288,1152]{1,0:T(8,128)(2,1)}), bf16[1152,1152]{1,0:T(8,128)(2,1)}) %all-gather.3.cloned.1.call-update) | async-done | bytes 2654224 | tf_op jit(solution)/shard_map/all_gather | solution.py:30
  57.3 0.0 copy-done
  57.3 2.4 multiply_reduce_fusion
  59.7 0.1 fusion.28
  59.8 6.8 %all_gather.11 = bf16[192,1152]{1,0:T(8,128)(2,1)S(1)} all-gather(bf16[48,1152]{1,0:T(8,128)(2,1)S(1)} %fusion.28), channel_id=1, replica_groups=mesh['dp'=128,'fsdp'=4] {'fsdp'}, dimensions={0}, use_global_device_ids=true | all-gather | bytes 552960 | tf_op jit(solution)/shard_map/all_gather | solution.py:36
  66.7 267.7 %all-gather.5.cloned.1.call-done = bf16[6144,1152]{1,0:T(8,128)(2,1)} async-done(((bf16[48,1152]{1,0:T(8,128)(2,1)}), bf16[6144,1152]{1,0:T(8,128)(2,1)}) %all-gather.5.cloned.1.call-update) | async-done | bytes 14155792 | tf_op jit(solution)/shard_map/all_gather | solution.py:44
  334.4 17.9 %convolution_convert_fusion.1 = bf16[192,1152]{1,0:T(8,128)(2,1)} fusion(bf16[6144,1152]{1,0:T(8,128)(2,1)} %all-gather.5.cloned.1.call-done, bf16[192,1152]{1,0:T(8,128)(2,1)S(1)} %all_gather.11, f32[]{:T(128)S(6)} %div.44, f32[]{:T(128)} %bitcast.16, f32[]{:T(128)} %bitcast, s32[6144]{0:T(1024)S(1)} %fusion.24, s32[192]{0:T(256)S(1)} %iota_add_fusion), kind=kOutput, calls=%fused_computation.12 | convolution fusion | flops 5450194944 | bytes 15065868 | tf_op jit(solution)/shard_map/dot_general | solution.py:57
  352.3 0.0 reduce-scatter.5.cloned.1.call-update
  352.3 0.0 reduce-scatter.7.cloned.1.call-start
  352.4 28.0 %reduce-scatter.5.cloned.1.call-done = bf16[48,1152]{1,0:T(8,128)(2,1)} async-done(((bf16[192,1152]{1,0:T(8,128)(2,1)}), bf16[48,1152]{1,0:T(8,128)(2,1)}) %reduce-scatter.5.cloned.1.call-update) | async-done | bytes 110608 | tf_op jit(solution)/shard_map/reduce_scatter | solution.py:58
  380.4 1.1 fusion.12
  381.5 1.9 fusion.9
  383.3 0.0 copy-start.1
  383.3 3.3 copy.10
  386.6 0.0 reduce-scatter.7.cloned.1.call-update
  386.7 0.0 copy-done.1
  386.7 3.3 convolution_convert_fusion.2
  390.0 38.1 %reduce-scatter.7.cloned.1.call-done = bf16[288,1152]{1,0:T(8,128)(2,1)} async-done(((bf16[1152,1152]{1,0:T(8,128)(2,1)}), bf16[288,1152]{1,0:T(8,128)(2,1)}) %reduce-scatter.7.cloned.1.call-update) | async-done | bytes 663568
  428.1 1.5 copy.11
  429.6 0.1 bitcast_convert_fusion
  429.7 1.6 copy.9
  (4 shorter events, 0.0 us)
Async XLA Ops:
  7.2 50.1 %copy-start = (bf16[48,1152]{1,0:T(8,128)(2,1)S(1)}, bf16[48,1152]{1,0:T(8,128)(2,1)}, u32[]{:S(2)}) copy-start(bf16[48,1152]{1,0:T(8,128)(2,1)} %param.6) | copy-start | bytes 331780
  7.2 50.1 %all-gather.3.cloned.1.call-start = ((), (), s32[]{:S(2)}) async-start(), calls=%async_computation.2 | async-start | bytes 3317760 | tf_op jit(solution)/shard_map/all_gather | solution.py:30
  7.9 326.4 %all-gather.5.cloned.1.call-start = ((), (), s32[]{:S(2)}) async-start(), calls=%async_computation.3 | async-start | bytes 14266368 | tf_op jit(solution)/shard_map/all_gather | solution.py:44
  10.7 369.7 %reduce-scatter.5.cloned.1.call-start = ((), (), s32[]{:S(2)}) async-start(), calls=%async_computation.4 | async-start | bytes 552960 | tf_op jit(solution)/shard_map/reduce_scatter | solution.py:58
  352.3 75.8 %reduce-scatter.7.cloned.1.call-start = ((), (), s32[]{:S(2)}) async-start(), calls=%async_computation.5 | async-start | bytes 3317760
  383.3 3.3 copy-start.1
Sparse Core Ops, SparseCore 0:
  10.1 47.1 all-gather.2
  62.4 271.8 all-gather.4
  352.4 27.8 reduce-scatter.4
  386.8 41.2 reduce-scatter.6
where the time goes:
time: 438 us
  waiting for transfers between devices  379 us (87%)
  matrix products  25.6 us (6%)
  between operations  15.8 us (4%)
  blocking collectives  6.85 us (2%)
  local copies, waits for them, and re-layouts  6.36 us (1%)
    all_gather x1, waiting for transfers between devices, body(): image_rows = lax.all_gather(image_embed, 'dp', axis=0, tiled=True)  268 us
    all_gather x1, waiting for transfers between devices, body(): lax.all_gather(caption_mapping_weights, 'fsdp', axis=0, tiled=True)  44.5 us
    unnamed x5, waiting for transfers between devices  38.8 us
    reduce_scatter x1, waiting for transfers between devices, body(): lax.psum_scatter(embed_grad.astype(jnp.bfloat16), 'fsdp', scatter_dimensi...  28 us
    dot_general x1, matrix products, body(): jnp.dot(weights, image_rows, preferred_element_type=jnp.float32)  17.9 us
  transfers between devices with their start and end apart: 4, of which 4 were waited for; matrix products, arithmetic and copies ran while one was open for 2% of the time, Pallas kernels for 0%

commit v1 on v0

v1 whole, which is shorter than its diff:
```python
import jax
import jax.numpy as jnp
from jax import lax
from jax.sharding import Mesh, PartitionSpec as P

AXES = ("xh", "z", "y", "xl", "c")
SIZES = (2, 16, 4, 2, 2)
PLANE = ("xh", "y", "xl")
LINE = ("z", "c")
RING = ("xh", "xl")
FSDP = ("xl", "c")

epsilon = 1e-06


def shift(step, size):
    return [(i, (i + step) % size) for i in range(size)]


def whole_head(rows):
    half = rows.shape[0] // 2
    other = jnp.concatenate(
        [
            lax.ppermute(rows[:half], RING, shift(1, 4)),
            lax.ppermute(rows[half:], RING, shift(3, 4)),
        ]
    )
    mine = jnp.stack([rows, other])
    theirs = lax.ppermute(mine, "c", shift(1, 2))
    chip, core = lax.axis_index("xl"), lax.axis_index("c")
    low = jnp.where(core == 0, mine, theirs)
    high = jnp.where(core == 0, theirs, mine)
    first = jnp.concatenate([low[0], high[0]])
    second = jnp.concatenate([low[1], high[1]])
    return jnp.where(
        chip == 0, jnp.concatenate([first, second]), jnp.concatenate([second, first])
    )


def body(features, pictures, head_rows, coldness, offset, weighting):
    rows, width = features.shape
    xh, z, y, xl, c = (lax.axis_index(a) for a in AXES)
    total_rows = rows * 512

    image_vals = pictures.astype(jnp.float32)
    image_norm = jnp.sqrt(jnp.sum(image_vals * image_vals, axis=-1, keepdims=True) + epsilon)
    image_embed = (image_vals / image_norm).astype(jnp.bfloat16)
    images = lax.all_gather(image_embed, LINE, axis=0, tiled=True)

    head = whole_head(head_rows)
    columns = lax.all_to_all(features, FSDP, 1, 0, tiled=True)
    plane_features = lax.all_to_all(jnp.tile(features, (16, 1)), PLANE, 0, 0, tiled=True)

    projected = jnp.dot(plane_features, head, preferred_element_type=jnp.float32)
    plane_norm = jnp.sqrt(jnp.sum(projected * projected, axis=-1, keepdims=True) + epsilon)
    plane_unit = projected / plane_norm
    plane_text = plane_unit.astype(jnp.bfloat16)
    place = ((xh * 4 + y) * 2 + xl) * rows
    unit_text = lax.dynamic_slice_in_dim(plane_unit, place, rows)
    text_norm = lax.dynamic_slice_in_dim(plane_norm, place, rows)

    sharpness = jnp.exp(coldness[0])
    factor = sharpness * weighting[0] / total_rows

    r = jnp.arange(rows, dtype=jnp.int32)
    plane_at = jnp.arange(16, dtype=jnp.int32)
    text_at = (((plane_at // 8) * 16 + z) * 4 + plane_at // 2 % 4) * 4 + plane_at % 2 * 2 + c
    line_at = jnp.arange(32, dtype=jnp.int32)
    image_at = ((xh * 16 + line_at // 2) * 4 + y) * 4 + xl * 2 + line_at % 2
    text_ids = (text_at[:, None] * rows + r[None, :]).reshape(-1)
    image_ids = (image_at[:, None] * rows + r[None, :]).reshape(-1)

    cosine = lax.dot_general(
        plane_text, images, (((1,), (1,)), ((), ())), preferred_element_type=jnp.float32
    )
    logits = sharpness * cosine + offset[0]
    labels = jnp.where(text_ids[:, None] == image_ids[None, :], 1.0, -1.0).astype(jnp.float32)
    weights = (-labels * jax.nn.sigmoid(-labels * logits) * factor).astype(jnp.bfloat16)
    partial = jnp.dot(weights, images, preferred_element_type=jnp.float32).astype(jnp.bfloat16)

    parts = lax.all_to_all(partial, PLANE, 0, 0, tiled=True).reshape(16, rows, width)
    own_grad = jnp.sum(parts.astype(jnp.float32), axis=0)
    radial = jnp.sum(unit_text * own_grad, axis=-1, keepdims=True)
    proj_grad = ((own_grad - unit_text * radial) / text_norm).astype(jnp.bfloat16)
    feat_grad = lax.dot_general(
        proj_grad, head, (((1,), (1,)), ((), ())), preferred_element_type=jnp.float32
    )
    group_grad = lax.all_gather(proj_grad, FSDP, axis=0, tiled=True)
    head_grad = lax.dot_general(
        columns, group_grad, (((0,), (0,)), ((), ())), preferred_element_type=jnp.float32
    )
    return feat_grad.astype(jnp.bfloat16), head_grad[None]


def solution(mesh):
    fine = Mesh(mesh.devices.reshape(SIZES), AXES)
    return jax.shard_map(
        body,
        mesh=fine,
        in_specs=(P(AXES, None), P(AXES, None), P(FSDP, None), P(), P(), P()),
        out_specs=(P(AXES, None), P(("xh", "z", "y"), FSDP, None)),
        check_vma=False,
    )
```

time: 438 us -> 161 us (0.37)
  waiting for transfers between devices: 379 us -> 70.5 us
  starting transfers between devices: 0.16 us -> 32.1 us
  other arithmetic: 4.02 us -> 11.5 us
  matrix products: 25.6 us -> 19.4 us
    all_gather x2 -> x1, waiting for transfers between devices: 312 us -> 18.3 us  [body(): images = lax.all_gather(image_embed, LINE, axis=0, tiled=True)]
    all_to_all x0 -> x3, waiting for transfers between devices: none -> 47.5 us  [the longest x1 25.6 us: body(): lax.all_to_all(partial, PLANE, 0, 0, tiled=True).reshape(16, rows, width)]
    unnamed x5 -> x1, waiting for transfers between devices: 38.8 us -> 0.02 us
    reduce_scatter x1 -> x0, waiting for transfers between devices: 28 us -> none  [body(): lax.psum_scatter(embed_grad.astype(jnp.bfloat16), 'fsdp', scatter_dimensi...]
    all_to_all x0 -> x3, starting transfers between devices: none -> 16.3 us  [the longest x1 6.8 us: body(): lax.all_to_all(partial, PLANE, 0, 0, tiled=True).reshape(16, rows, width)]
    ppermute x0 -> x3, starting transfers between devices: none -> 15.8 us  [the longest x1 8.65 us: whole_head(): theirs = lax.ppermute(mine, 'c', shift(1, 2))]
    unnamed x7 -> x4, local copies, waits for them, and re-layouts: 6.36 us -> 0.01 us
    dot_general x4, matrix products: 25.6 us -> 19.4 us  [the longest x1 12.1 us: body(): jnp.dot(weights, images, preferred_element_type=jnp.float32)]
  transfers between devices with their start and end apart: 4 -> 7, of which waited for: 4 -> 5; matrix products, arithmetic and copies ran while one was open for 2% -> 11% of each run, Pallas kernels for 0% -> 0%
where the time goes in v1:
time: 161 us
  waiting for transfers between devices  70.5 us (44%)
  starting transfers between devices  32.1 us (20%)
  matrix products  19.4 us (12%)
  between operations  16.2 us (10%)
  other arithmetic  11.5 us (7%)
  blocking collectives  7.08 us (4%)
  local copies, waits for them, and re-layouts  3.8 us (2%)
    all_to_all x1, waiting for transfers between devices, body(): lax.all_to_all(partial, PLANE, 0, 0, tiled=True).reshape(16, rows, width)  25.6 us
    all_to_all x1, waiting for transfers between devices, body(): lax.all_to_all(jnp.tile(features, (16, 1)), PLANE, 0, 0, tiled=True)  21.9 us
    all_gather x1, waiting for transfers between devices, body(): images = lax.all_gather(image_embed, LINE, axis=0, tiled=True)  18.3 us
    dot_general x1, matrix products, body(): jnp.dot(weights, images, preferred_element_type=jnp.float32)  12.1 us
    ppermute x1, starting transfers between devices, whole_head(): theirs = lax.ppermute(mine, 'c', shift(1, 2))  8.65 us
    all_gather x1, blocking collectives, body(): group_grad = lax.all_gather(proj_grad, FSDP, axis=0, tiled=True)  7.08 us
    all_to_all x1, starting transfers between devices, body(): lax.all_to_all(partial, PLANE, 0, 0, tiled=True).reshape(16, rows, width)  6.8 us
    all_to_all x1, starting transfers between devices, body(): lax.all_to_all(jnp.tile(features, (16, 1)), PLANE, 0, 0, tiled=True)  4.84 us
  transfers between devices with their start and end apart: 7, of which 5 were waited for; matrix products, arithmetic and copies ran while one was open for 11% of the time, Pallas kernels for 0%

profile of v1, /device:TPU:1, one launch (start us, length us, event | category | flops | bytes accessed | tf_op | source)
XLA Modules:
  0.0 160.5 jit_solution(14963537573960099067)
XLA Ops:
  7.2 1.1 fusion.2
  8.3 1.6 %fusion.3 = bf16[48,1152]{1,0:T(8,128)(2,1)} fusion(bf16[48,1152]{1,0:T(8,128)(2,1)} %param.7, f32[48]{0:T(128)S(1)} %add_sqrt_fusion.1), kind=kLoop, calls=%fused_computation.20 | loop fusion | flops 165888 | bytes 221376 | tf_op jit(solution)/shard_map/convert_element_type | solution.py:47
  10.0 1.1 fusion.27
  11.1 3.9 %collective-permute-start = (bf16[144,1152]{1,0:T(8,128)(2,1)S(1)}, bf16[144,1152]{1,0:T(8,128)(2,1)S(1)}, u32[]{:S(2)}, u32[]{:S(2)}) collective-permute-start(bf16[144,1152]{1,0:T(8,128)(2,1)S(1)} %get-tuple-element.8), channel_id=1, source_target_pairs={{0,2},{2,256},{256,258},{258,0},{1,3},{3,257},{257,259},{259,1},{4... | collective-permute-start | bytes 995336 | tf_op jit(solution)/shard_map/ppermute | solution.py:24
  15.1 3.2 %collective-permute-start.1 = (bf16[144,1152]{1,0:T(8,128)(2,1)S(1)}, bf16[144,1152]{1,0:T(8,128)(2,1)S(1)}, u32[]{:S(2)}, u32[]{:S(2)}) collective-permute-start(bf16[144,1152]{1,0:T(8,128)(2,1)S(1)} %get-tuple-element.9), channel_id=1, source_target_pairs={{0,258},{2,0},{256,2},{258,256},{1,259},{3,1},{257,3},{259,257},{4... | collective-permute-start | bytes 995336 | tf_op jit(solution)/shard_map/ppermute | solution.py:25
  18.3 2.6 %collective-permute-done = bf16[144,1152]{1,0:T(8,128)(2,1)S(1)} collective-permute-done((bf16[144,1152]{1,0:T(8,128)(2,1)S(1)}, bf16[144,1152]{1,0:T(8,128)(2,1)S(1)}, u32[]{:S(2)}, u32[]{:S(2)}) %collective-permute-start) | collective-permute-done | bytes 331808 | tf_op jit(solution)/shard_map/ppermute | solution.py:24
  20.8 2.1 %collective-permute-done.1 = bf16[144,1152]{1,0:T(8,128)(2,1)S(1)} collective-permute-done((bf16[144,1152]{1,0:T(8,128)(2,1)S(1)}, bf16[144,1152]{1,0:T(8,128)(2,1)S(1)}, u32[]{:S(2)}, u32[]{:S(2)}) %collective-permute-start.1) | collective-permute-done | bytes 331808 | tf_op jit(solution)/shard_map/ppermute | solution.py:25
  23.0 0.1 pad_maximum_fusion
  23.2 8.7 %collective-permute-start.2 = (bf16[2,288,1152]{2,1,0:T(8,128)(2,1)S(1)}, bf16[2,288,1152]{2,1,0:T(8,128)(2,1)}, u32[]{:S(2)}, u32[]{:S(2)}) collective-permute-start(bf16[2,288,1152]{2,1,0:T(8,128)(2,1)S(1)} %pad_maximum_fusion), channel_id=1, source_target_pairs={{0,1},{1,0},{2,3},{3,2},{4,5},{5,4},{6,7},{7,6},{8,9},{9,8},{10,11... | collective-permute-start | bytes 3981320 | tf_op jit(solution)/shard_map/ppermute | solution.py:29
  31.8 1.4 tile.2
  33.2 4.8 %all-to-all-start = ((bf16[16,48,1152]{2,1,0:T(8,128)(2,1)}), bf16[16,48,1152]{2,1,0:T(8,128)(2,1)}, u32[]{:S(2)}, u32[]{:S(2)}) async-start(bf16[16,48,1152]{2,1,0:T(8,128)(2,1)} %tile.2), calls=%async_computation | async-start | bytes 3538944 | tf_op jit(solution)/shard_map/all_to_all | solution.py:52
  38.1 0.1 add.223
  38.3 0.1 add.211
  40.4 1.6 %broadcast_select_fusion.1 = (bf16[2,288,1152]{2,1,0:T(8,128)(2,1)S(1)}, bf16[2,288,1152]{2,1,0:T(8,128)(2,1)S(1)}) fusion(bf16[2,288,1152]{2,1,0:T(8,128)(2,1)} %collective-permute-done.2, pred[]{:T(512)S(6)} %eq.29, bf16[1,288,1152]{2,1,0:T(8,128)(2,1)S(1)} %maximum_bitcast_fusion, bf16[1,288,1152]{2,1,0:T(8,128)(2,1)S(1)} %bitcast.45), kind=kLoop, calls=%fused_computation.11 | loop fusion | flops 1990656 | bytes 5308417 | tf_op jit(solution)/shard_map/jit(_where)/select_n | solution.py:31
  42.0 0.2 slice_bitcast_fusion.2
  42.3 0.7 maximum_select_fusion
  43.0 21.9 %all-to-all-done = bf16[16,48,1152]{2,1,0:T(8,128)(2,1)} async-done(((bf16[16,48,1152]{2,1,0:T(8,128)(2,1)}), bf16[16,48,1152]{2,1,0:T(8,128)(2,1)}, u32[]{:S(2)}, u32[]{:S(2)}) %all-to-all-start) | async-done | bytes 1769504 | tf_op jit(solution)/shard_map/all_to_all | solution.py:52
  64.8 4.3 %multiply_reduce_fusion = (f32[768]{0:T(1024)S(1)}, f32[1152,768]{0,1:T(8,128)S(1)}) fusion(bf16[768,1152]{1,0:T(8,128)(2,1)} %bitcast.7, bf16[1152,1152]{1,0:T(8,128)(2,1)S(1)} %maximum_select_fusion), kind=kOutput, calls=%fused_computation.2 | convolution fusion | flops 2040200448 | bytes 7965696 | tf_op jit(solution)/shard_map/dot_general | solution.py:54
  69.2 2.1 %broadcast_divide_fusion = f32[1152,768]{0,1:T(8,128)} fusion(f32[1152,768]{0,1:T(8,128)S(1)} %get-tuple-element.11, f32[768]{0:T(1024)S(1)} %add_sqrt_fusion), kind=kLoop, calls=%fused_computation.8 | loop fusion | flops 884736 | bytes 7080960 | tf_op jit(solution)/shard_map/div | solution.py:56
  71.3 18.3 %all-gather.2.cloned.1.call-done = bf16[1536,1152]{1,0:T(8,128)(2,1)} async-done(((bf16[48,1152]{1,0:T(8,128)(2,1)}), bf16[1536,1152]{1,0:T(8,128)(2,1)}) %all-gather.2.cloned.1.call-update) | async-done | bytes 3538960 | tf_op jit(solution)/shard_map/all_gather | solution.py:48
  89.6 12.1 %convolution_convert_fusion = bf16[768,1152]{1,0:T(8,128)(2,1)} fusion(bf16[1536,1152]{1,0:T(8,128)(2,1)} %all-gather.2.cloned.1.call-done, f32[]{:T(128)S(6)} %div.58, f32[]{:T(128)} %bitcast.42, f32[]{:T(128)} %bitcast, s32[1536]{0:T(1024)S(1)} %add.223, s32[768]{0:T(1024)S(1)} %add.211, f32[1152,768]{0,1:T(8,128)} %broadcast_divide_fusion), kind=kOutput, calls=%fused_computation.3 | convolution fusion | flops 5451743232 | bytes 8856588 | tf_op jit(solution)/shard_map/dot_general | solution.py:79
  101.7 6.8 %all-to-all-start.1 = ((bf16[16,48,1152]{2,1,0:T(8,128)(2,1)}), bf16[16,48,1152]{2,1,0:T(8,128)(2,1)}, u32[]{:S(2)}, u32[]{:S(2)}) async-start(bf16[16,48,1152]{2,1,0:T(8,128)(2,1)} %bitcast.46), calls=%async_computation.1 | async-start | bytes 3538944 | tf_op jit(solution)/shard_map/all_to_all | solution.py:81
  108.5 0.2 all_to_all.30
  108.7 0.7 copy.9
  109.4 25.6 %all-to-all-done.1 = bf16[16,48,1152]{2,1,0:T(8,128)(2,1)} async-done(((bf16[16,48,1152]{2,1,0:T(8,128)(2,1)}), bf16[16,48,1152]{2,1,0:T(8,128)(2,1)}, u32[]{:S(2)}, u32[]{:S(2)}) %all-to-all-start.1) | async-done | bytes 1769504 | tf_op jit(solution)/shard_map/all_to_all | solution.py:81
  135.0 4.7 %all-to-all-start.2 = ((bf16[48,4,288]{2,0,1:T(8,128)(2,1)}), bf16[48,4,288]{2,0,1:T(8,128)(2,1)S(1)}, u32[]{:S(2)}, u32[]{:S(2)}) async-start(bf16[48,4,288]{2,0,1:T(8,128)(2,1)} %copy.9), calls=%async_computation.2 | async-start | bytes 294912 | tf_op jit(solution)/shard_map/all_to_all | solution.py:51
  139.7 1.7 %convert_reduce_fusion = f32[48,1152]{1,0:T(8,128)S(1)} fusion(bf16[16,48,1152]{2,1,0:T(8,128)(2,1)} %all-to-all-done.1), kind=kLoop, calls=%fused_computation.1 | loop fusion | flops 1714176 | bytes 1990656 | tf_op jit(solution)/shard_map/reduce_sum | solution.py:82
  141.5 1.1 fusion.4
  142.5 1.0 fusion.7
  143.6 1.6 convolution_convert_fusion.1
  145.1 7.1 %all_gather.7 = bf16[192,1152]{1,0:T(8,128)(2,1)S(1)} all-gather(bf16[48,1152]{1,0:T(8,128)(2,1)S(1)} %fusion.7), channel_id=1, replica_groups=mesh['xh'=2,'z'=16,'y'=4,'xl'=2,'c'=2] {'xl','c'}, dimensions={0}, use_global_device_ids=true | all-gather | bytes 552960 | tf_op jit(solution)/shard_map/all_gather | solution.py:88
  152.2 1.5 convolution_bitcast_fusion
  (16 shorter events, 0.4 us)
Async XLA Ops:
  7.2 15.8 %copy-start = (bf16[288,1152]{1,0:T(8,128)(2,1)S(1)}, bf16[288,1152]{1,0:T(8,128)(2,1)}, u32[]{:S(2)}) copy-start(bf16[288,1152]{1,0:T(8,128)(2,1)} %param.8) | copy-start | bytes 1990660
  7.2 24.6 %copy-start.1 = (bf16[48,1152]{1,0:T(8,128)(2,1)S(1)}, bf16[48,1152]{1,0:T(8,128)(2,1)}, u32[]{:S(2)}) copy-start(bf16[48,1152]{1,0:T(8,128)(2,1)} %param.6) | copy-start | bytes 331780
  7.2 82.4 %all-gather.2.cloned.1.call-start = ((), (), s32[]{:S(2)}) async-start(), calls=%async_computation.3 | async-start | bytes 3649536 | tf_op jit(solution)/shard_map/all_gather | solution.py:48
  11.1 9.7 %collective-permute-start = (bf16[144,1152]{1,0:T(8,128)(2,1)S(1)}, bf16[144,1152]{1,0:T(8,128)(2,1)S(1)}, u32[]{:S(2)}, u32[]{:S(2)}) collective-permute-start(bf16[144,1152]{1,0:T(8,128)(2,1)S(1)} %get-tuple-element.8), channel_id=1, source_target_pairs={{0,2},{2,256},{256,258},{258,0},{1,3},{3,257},{257,259},{259,1},{4... | collective-permute-start | bytes 995336 | tf_op jit(solution)/shard_map/ppermute | solution.py:24
  15.1 7.9 %collective-permute-start.1 = (bf16[144,1152]{1,0:T(8,128)(2,1)S(1)}, bf16[144,1152]{1,0:T(8,128)(2,1)S(1)}, u32[]{:S(2)}, u32[]{:S(2)}) collective-permute-start(bf16[144,1152]{1,0:T(8,128)(2,1)S(1)} %get-tuple-element.9), channel_id=1, source_target_pairs={{0,258},{2,0},{256,2},{258,256},{1,259},{3,1},{257,3},{259,257},{4... | collective-permute-start | bytes 995336 | tf_op jit(solution)/shard_map/ppermute | solution.py:25
  23.2 17.2 %collective-permute-start.2 = (bf16[2,288,1152]{2,1,0:T(8,128)(2,1)S(1)}, bf16[2,288,1152]{2,1,0:T(8,128)(2,1)}, u32[]{:S(2)}, u32[]{:S(2)}) collective-permute-start(bf16[2,288,1152]{2,1,0:T(8,128)(2,1)S(1)} %pad_maximum_fusion), channel_id=1, source_target_pairs={{0,1},{1,0},{2,3},{3,2},{4,5},{5,4},{6,7},{7,6},{8,9},{9,8},{10,11... | collective-permute-start | bytes 3981320 | tf_op jit(solution)/shard_map/ppermute | solution.py:29
  33.2 31.6 %all-to-all-start = ((bf16[16,48,1152]{2,1,0:T(8,128)(2,1)}), bf16[16,48,1152]{2,1,0:T(8,128)(2,1)}, u32[]{:S(2)}, u32[]{:S(2)}) async-start(bf16[16,48,1152]{2,1,0:T(8,128)(2,1)} %tile.2), calls=%async_computation | async-start | bytes 3538944 | tf_op jit(solution)/shard_map/all_to_all | solution.py:52
  101.7 33.4 %all-to-all-start.1 = ((bf16[16,48,1152]{2,1,0:T(8,128)(2,1)}), bf16[16,48,1152]{2,1,0:T(8,128)(2,1)}, u32[]{:S(2)}, u32[]{:S(2)}) async-start(bf16[16,48,1152]{2,1,0:T(8,128)(2,1)} %bitcast.46), calls=%async_computation.1 | async-start | bytes 3538944 | tf_op jit(solution)/shard_map/all_to_all | solution.py:81
  135.0 17.2 %all-to-all-start.2 = ((bf16[48,4,288]{2,0,1:T(8,128)(2,1)}), bf16[48,4,288]{2,0,1:T(8,128)(2,1)S(1)}, u32[]{:S(2)}, u32[]{:S(2)}) async-start(bf16[48,4,288]{2,0,1:T(8,128)(2,1)} %copy.9), calls=%async_computation.2 | async-start | bytes 294912 | tf_op jit(solution)/shard_map/all_to_all | solution.py:51
Sparse Core Ops, SparseCore 0:
  10.7 78.8 all-gather.1

commit v2 on v1

v2 whole, which is shorter than its diff:
```python
import functools

import jax
import jax.numpy as jnp
from jax import lax
from jax.experimental import pallas as pl
from jax.experimental.pallas import tpu as pltpu
from jax.sharding import Mesh, PartitionSpec as P

AXES = ("xh", "za", "zb", "y", "xl", "c")
SIZES = (2, 4, 4, 4, 2, 2)
LINE = ("za", "zb")
PLANE = ("xh", "y", "xl")
RING = ("xh", "xl")
FSDP = ("xl", "c")

epsilon = 1e-06
LOG2E = 1.4426950408889634
WIDE = 256
VMEM_BYTES = 18 * 2**20
BY_COLUMNS = (((1,), (1,)), ((), ()))

IN_VMEM = pl.BlockSpec(memory_space=pltpu.VMEM)
IN_SMEM = pl.BlockSpec(memory_space=pltpu.SMEM)
ANYWHERE = pl.BlockSpec(memory_space=pl.ANY)


def shift(step, size):
    return [(i, (i + step) % size) for i in range(size)]


def along_z(array, step):
    return lax.ppermute(array, LINE, shift(step % 16, 16))


def other_core(array):
    return lax.ppermute(array, "c", shift(1, 2))


def lay(pieces, whole_ref, sems, starts):
    copies = [
        pltpu.make_async_copy(piece, whole_ref.at[pl.ds(start, piece.shape[0])], sems.at[k])
        for k, (piece, start) in enumerate(zip(pieces, starts))
    ]
    for copy in copies:
        copy.start()
    for copy in copies:
        copy.wait()


def unit_kernel(rows_ref, out_ref):
    values = rows_ref[...].astype(jnp.float32)
    norm = jnp.sqrt(jnp.sum(values * values, axis=-1, keepdims=True) + epsilon)
    out_ref[...] = (values / norm).astype(out_ref.dtype)


def unit_rows(rows):
    return pl.pallas_call(
        unit_kernel,
        out_shape=jax.ShapeDtypeStruct(rows.shape, rows.dtype),
        in_specs=[IN_VMEM],
        out_specs=IN_VMEM,
        compiler_params=pltpu.CompilerParams(vmem_limit_bytes=2**21),
    )(rows)


def project_kernel(block, place_ref, from_ref, *refs):
    pieces, (text_ref, head_ref, pair_ref, rows_ref, sems, rows_sem) = refs[:-6], refs[-6:]
    copy = pltpu.make_async_copy(from_ref, rows_ref, rows_sem)
    copy.start()
    depth = pieces[0].shape[0]
    starts = [pl.multiple_of(place_ref[k] * depth, 32) for k in range(len(pieces))]
    lay(pieces, head_ref, sems, starts)
    copy.wait()
    for start in range(0, rows_ref.shape[0], block):
        at = pl.ds(start, block)
        projected = jnp.dot(rows_ref[at], head_ref[...], preferred_element_type=jnp.float32)
        norm = jnp.sqrt(jnp.sum(projected * projected, axis=-1, keepdims=True) + epsilon)
        text_ref[at] = (projected * (1.0 / norm)).astype(text_ref.dtype)
    count = pair_ref.shape[0]
    pair_ref[...] = rows_ref[pl.ds(pl.multiple_of(place_ref[len(pieces)] * count, 32), count)]


def project(place, rows, pieces, pair):
    count, width = rows.shape
    return pl.pallas_call(
        functools.partial(project_kernel, count // 2),
        out_shape=[
            jax.ShapeDtypeStruct((count, width), jnp.bfloat16),
            jax.ShapeDtypeStruct((width, width), jnp.bfloat16),
            jax.ShapeDtypeStruct((pair, width), jnp.bfloat16),
        ],
        in_specs=[IN_SMEM] + [ANYWHERE] * (1 + len(pieces)),
        out_specs=[IN_VMEM] * 3,
        scratch_shapes=[
            pltpu.VMEM((count, width), jnp.bfloat16),
            pltpu.SemaphoreType.DMA((len(pieces),)),
            pltpu.SemaphoreType.DMA,
        ],
        compiler_params=pltpu.CompilerParams(vmem_limit_bytes=VMEM_BYTES),
        cost_estimate=pl.CostEstimate(
            flops=2 * count * width * width,
            bytes_accessed=4 * width * (count + width),
            transcendentals=0,
        ),
    )(place, rows, *pieces)


def meet_kernel(block, own_rows, added, scalars_ref, place_ref, text_ref, *refs):
    pieces, (out_ref, images_ref, sems) = refs[:-3], refs[-3:]
    if added:
        pieces, sum_ref = pieces[:-1], pieces[-1]
    starts = [sum(p.shape[0] for p in pieces[:k]) for k in range(len(pieces))]
    lay(pieces, images_ref, sems, starts)
    scale, plus, minus, rest = (scalars_ref[k] for k in range(4))
    for start in range(0, text_ref.shape[0], block):
        at = pl.ds(start, block)
        cosine = lax.dot_general(
            text_ref[at], images_ref[...], BY_COLUMNS, preferred_element_type=jnp.float32
        )
        weights = 1.0 / (jnp.exp2(plus - cosine * scale) + rest)
        if own_rows:
            text = lax.broadcasted_iota(jnp.int32, (block, WIDE), 0) + (start - place_ref[0])
            image = lax.broadcasted_iota(jnp.int32, (block, WIDE), 1) - place_ref[1]
            paired = -1.0 / (jnp.exp2(cosine[:, :WIDE] * scale + minus) + rest)
            own = (text == image) & (text >= 0) & (text < own_rows)
            first = jnp.where(own, paired, weights[:, :WIDE])
            weights = jnp.concatenate([first, weights[:, WIDE:]], axis=1)
        grad = jnp.dot(
            weights.astype(jnp.bfloat16), images_ref[...], preferred_element_type=jnp.float32
        )
        if added:
            grad = sum_ref[at] + grad
        out_ref[at] = grad.astype(out_ref.dtype)


def meet(scalars, place, text, pieces, total=None, own_rows=0, dtype=jnp.float32):
    count, width = text.shape
    images = sum(p.shape[0] for p in pieces)
    given = () if total is None else (total,)
    return pl.pallas_call(
        functools.partial(meet_kernel, count // 2, own_rows, len(given)),
        out_shape=jax.ShapeDtypeStruct((count, width), dtype),
        in_specs=[IN_SMEM, IN_SMEM, IN_VMEM]
        + [ANYWHERE] * len(pieces)
        + [IN_VMEM] * len(given),
        out_specs=IN_VMEM,
        scratch_shapes=[
            pltpu.VMEM((images, width), jnp.bfloat16),
            pltpu.SemaphoreType.DMA((len(pieces),)),
        ],
        compiler_params=pltpu.CompilerParams(vmem_limit_bytes=VMEM_BYTES),
        cost_estimate=pl.CostEstimate(
            flops=4 * count * images * width,
            bytes_accessed=2 * width * (3 * count + images),
            transcendentals=2 * count * images,
        ),
    )(scalars, place, text, *pieces, *given)


def join_kernel(*refs):
    pieces, (out_ref, sems) = refs[:-3], refs[-2:]
    lay(pieces, out_ref, sems, [sum(p.shape[0] for p in pieces[:k]) for k in range(len(pieces))])


def join(pieces, after):
    count, width = sum(p.shape[0] for p in pieces), pieces[0].shape[1]
    return pl.pallas_call(
        join_kernel,
        out_shape=jax.ShapeDtypeStruct((count, width), jnp.bfloat16),
        in_specs=[ANYWHERE] * (len(pieces) + 1),
        out_specs=ANYWHERE,
        scratch_shapes=[pltpu.SemaphoreType.DMA((len(pieces),))],
        compiler_params=pltpu.CompilerParams(vmem_limit_bytes=2**20),
        cost_estimate=pl.CostEstimate(
            flops=0, bytes_accessed=4 * count * width, transcendentals=0
        ),
    )(*pieces, after)


def finish_kernel(parts_ref, projected_ref, out_ref):
    projected = projected_ref[...]
    norm = jnp.sqrt(jnp.sum(projected * projected, axis=-1, keepdims=True) + epsilon)
    unit = projected / norm
    grad = parts_ref[0].astype(jnp.float32)
    for k in range(1, parts_ref.shape[0]):
        grad = grad + parts_ref[k].astype(jnp.float32)
    radial = jnp.sum(unit * grad, axis=-1, keepdims=True)
    out_ref[...] = ((grad - unit * radial) / norm).astype(out_ref.dtype)


def finish(parts, projected):
    return pl.pallas_call(
        finish_kernel,
        out_shape=jax.ShapeDtypeStruct(projected.shape, jnp.bfloat16),
        in_specs=[IN_VMEM, IN_VMEM],
        out_specs=IN_VMEM,
        compiler_params=pltpu.CompilerParams(vmem_limit_bytes=VMEM_BYTES // 2),
    )(parts, projected)


def body(features, pictures, head_rows, coldness, offset, weighting):
    rows, width = features.shape
    xh, za, zb, y, xl, c = (lax.axis_index(a) for a in AXES)
    plane = 16
    place = (((xh * 4 + y) * 2 + xl) * rows).astype(jnp.int32)

    plane_features = lax.all_to_all(jnp.tile(features, (plane, 1)), PLANE, 0, 0, tiled=True)

    crossed = lax.ppermute(head_rows, "xl", shift(1, 2))
    head_pieces = [head_rows, crossed, other_core(head_rows), other_core(crossed)]
    at = [(xl * 2 + c), ((1 - xl) * 2 + c), (xl * 2 + 1 - c), ((1 - xl) * 2 + 1 - c), xh * 4 + y]
    head_place = jnp.stack([a.astype(jnp.int32) for a in at])

    own = unit_rows(pictures)
    quarter = lax.all_gather(own, "za", axis=0, tiled=True)
    half = quarter.shape[0] // 2
    late = [
        along_z(quarter, 1),
        along_z(quarter, -1),
        along_z(quarter[:half], 2),
        along_z(quarter[half:], -2),
    ]
    early = [quarter, other_core(quarter)]

    text, head, pair = project(head_place, plane_features, head_pieces, 2 * rows)

    sharpness = jnp.exp(coldness[0])
    factor = sharpness * weighting[0] / (rows * 512)
    log_factor = jnp.log2(factor)
    shift_up = offset[0] * LOG2E
    scalars = jnp.stack(
        [sharpness * LOG2E, -shift_up - log_factor, shift_up - log_factor, 1.0 / factor]
    )
    places = jnp.stack([place, (za * rows).astype(jnp.int32)])
    total = meet(scalars, places, text, early, own_rows=rows)
    late = join(late, total)
    late_other = other_core(late)
    total = meet(scalars, places, text, [late], total)
    partial = meet(scalars, places, text, [late_other], total, dtype=jnp.bfloat16)

    parts = lax.all_to_all(partial, PLANE, 0, 0, tiled=True).reshape(plane, rows, width)

    projected = jnp.dot(features, head, preferred_element_type=jnp.float32)
    other = other_core(pair)
    low, high = jnp.where(c == 0, pair, other), jnp.where(c == 0, other, pair)
    group = jnp.stack([low.reshape(2, rows, width), high.reshape(2, rows, width)], axis=1)
    columns = lax.dynamic_slice_in_dim(
        group.reshape(4 * rows, width), (xl * 2 + c) * (width // 4), width // 4, axis=1
    )

    proj_grad = finish(parts, projected)
    feat_grad = lax.dot_general(proj_grad, head, BY_COLUMNS, preferred_element_type=jnp.float32)
    group_grad = lax.all_gather(proj_grad, FSDP, axis=0, tiled=True)
    head_grad = lax.dot_general(
        columns, group_grad, (((0,), (0,)), ((), ())), preferred_element_type=jnp.float32
    )
    return feat_grad.astype(jnp.bfloat16), head_grad[None]


def solution(mesh):
    fine = Mesh(mesh.devices.reshape(SIZES), AXES)
    return jax.shard_map(
        body,
        mesh=fine,
        in_specs=(P(AXES, None), P(AXES, None), P(FSDP, None), P(), P(), P()),
        out_specs=(P(AXES, None), P(("xh", "za", "zb", "y"), FSDP, None)),
        check_vma=False,
    )
```

time: 161 us -> 147 us (0.913)
  waiting for transfers between devices: 70.5 us -> 23.9 us
  blocking collectives: 7.08 us -> 35.7 us
  Pallas kernels: 0 us -> 21.8 us
  starting transfers between devices: 32.1 us -> 48.6 us
  matrix products: 19.4 us -> 3.67 us
  between operations: 16.2 us -> 3.01 us
  other arithmetic: 11.5 us -> 0.25 us
  local copies, waits for them, and re-layouts: 3.8 us -> 8.97 us
    all_gather x0 -> x1, blocking collectives: none -> 27.2 us  [body(): quarter = lax.all_gather(own, 'za', axis=0, tiled=True)]
    all_to_all x3 -> x2, waiting for transfers between devices: 47.5 us -> 23.3 us  [the longest x1 23.3 us: body(): lax.all_to_all(partial, PLANE, 0, 0, tiled=True).reshape(plane, rows, width)]
    pallas_call x0 -> x7, Pallas kernels: none -> 21.8 us  [the longest x3 12.8 us: meet(): pl.pallas_call(functools.partial(meet_kernel, count // 2, own_rows, len(g...]
    ppermute x3 -> x10, starting transfers between devices: 15.8 us -> 34.8 us  [the longest x5 17.6 us: other_core(): return lax.ppermute(array, 'c', shift(1, 2))]
    all_gather x1 -> x0, waiting for transfers between devices: 18.3 us -> none  [body(): images = lax.all_gather(image_embed, LINE, axis=0, tiled=True)]
    dot_general x3 -> x2, matrix products: 17.9 us -> 2.12 us  [the longest x1 1.55 us: body(): lax.dot_general(proj_grad, head, BY_COLUMNS, preferred_element_type=jnp.f...]
    unnamed x4 -> x18, local copies, waits for them, and re-layouts: 0.01 us -> 5.72 us
    ppermute x3 -> x10, waiting for transfers between devices: 4.67 us -> 0.61 us  [the longest x5 0.59 us: other_core(): return lax.ppermute(array, 'c', shift(1, 2))]
  transfers between devices with their start and end apart: 7 -> 12, of which waited for: 5 -> 2; matrix products, arithmetic and copies ran while one was open for 11% -> 1% of each run, Pallas kernels for 0% -> 10%
where the time goes in v2:
time: 147 us; the launch traced here: 146 us
  starting transfers between devices  48.6 us (33%)
  blocking collectives  35.7 us (24%)
  waiting for transfers between devices  23.9 us (16%)
  Pallas kernels  21.8 us (15%)
  local copies, waits for them, and re-layouts  8.97 us (6%)
  matrix products  3.67 us (2%)
  between operations  3.01 us (2%)
    all_gather x1, blocking collectives, body(): quarter = lax.all_gather(own, 'za', axis=0, tiled=True)  27.2 us
    all_to_all x1, waiting for transfers between devices, body(): lax.all_to_all(partial, PLANE, 0, 0, tiled=True).reshape(plane, rows, width)  23.3 us
    ppermute x5, starting transfers between devices, other_core(): return lax.ppermute(array, 'c', shift(1, 2))  17.6 us
    ppermute x4, starting transfers between devices, along_z(): return lax.ppermute(array, LINE, shift(step % 16, 16))  13.9 us
    pallas_call x3, Pallas kernels, meet(): pl.pallas_call(functools.partial(meet_kernel, count // 2, own_rows, len(g...  12.8 us
    all_gather x1, blocking collectives, body(): group_grad = lax.all_gather(proj_grad, FSDP, axis=0, tiled=True)  8.45 us
    all_to_all x1, starting transfers between devices, body(): lax.all_to_all(jnp.tile(features, (plane, 1)), PLANE, 0, 0, tiled=True)  7.58 us
    all_to_all x1, starting transfers between devices, body(): lax.all_to_all(partial, PLANE, 0, 0, tiled=True).reshape(plane, rows, width)  6.27 us
  transfers between devices with their start and end apart: 12, of which 2 were waited for; matrix products, arithmetic and copies ran while one was open for 1% of the time, Pallas kernels for 10%

profile of v2, /device:TPU:1, one launch (start us, length us, event | category | flops | bytes accessed | tf_op | source)
XLA Modules:
  0.0 145.9 jit_solution(1022333045750416591)
XLA Ops:
  0.7 2.3 %tile.2 = bf16[16,48,1152]{2,1,0:T(8,128)(2,1)} broadcast(bf16[48,1152]{1,0:T(8,128)(2,1)} %param.6), dimensions={1,2} | broadcast | bytes 1880064 | tf_op jit(solution)/shard_map/tile | solution.py:208
  3.0 7.6 %all-to-all-start = ((bf16[16,48,1152]{2,1,0:T(8,128)(2,1)}), bf16[16,48,1152]{2,1,0:T(8,128)(2,1)S(1)}, u32[]{:S(2)}, u32[]{:S(2)}) async-start(bf16[16,48,1152]{2,1,0:T(8,128)(2,1)} %tile.2), calls=%async_computation | async-start | bytes 3538944 | tf_op jit(solution)/shard_map/all_to_all | solution.py:208
  10.6 3.3 %collective-permute-start = (bf16[288,1152]{1,0:T(8,128)(2,1)S(1)}, bf16[288,1152]{1,0:T(8,128)(2,1)}, u32[]{:S(2)}, u32[]{:S(2)}) collective-permute-start(bf16[288,1152]{1,0:T(8,128)(2,1)S(1)} %copy-done.6), channel_id=1, source_target_pairs={{0,2},{2,0},{1,3},{3,1},{4,6},{6,4},{5,7},{7,5},{8,10},{10,8},{9,1... | collective-permute-start | bytes 1990664 | tf_op jit(solution)/shard_map/ppermute | solution.py:210
  13.9 5.4 %collective-permute-start.1 = (bf16[288,1152]{1,0:T(8,128)(2,1)S(1)}, bf16[288,1152]{1,0:T(8,128)(2,1)}, u32[]{:S(2)}, u32[]{:S(2)}) collective-permute-start(bf16[288,1152]{1,0:T(8,128)(2,1)S(1)} %copy-done.6), channel_id=1, source_target_pairs={{0,1},{1,0},{2,3},{3,2},{4,5},{5,4},{6,7},{7,6},{8,9},{9,8},{10,11... | collective-permute-start | bytes 1990664 | tf_op jit(solution)/shard_map/ppermute | solution.py:37
  19.4 27.2 %all_gather.6.refs_0_ = bf16[192,1152]{1,0:T(8,128)(2,1)S(1)} all-gather(bf16[48,1152]{1,0:T(8,128)(2,1)S(1)} %shard_map.78), channel_id=1, replica_groups=mesh['xh'=2,'za'=4,'zb'=4,'y'=4,'xl'=2,'c'=2] {'za'}, dimensions={0}, use_global_device_ids=true | all-gather | bytes 552960 | tf_op jit(solution)/shard_map/all_gather | solution.py:216
  46.6 5.1 %collective-permute-start.7 = (bf16[192,1152]{1,0:T(8,128)(2,1)S(1)}, bf16[192,1152]{1,0:T(8,128)(2,1)}, u32[]{:S(2)}, u32[]{:S(2)}) collective-permute-start(bf16[192,1152]{1,0:T(8,128)(2,1)S(1)} %all_gather.6.refs_0_), channel_id=1, source_target_pairs={{0,1},{1,0},{2,3},{3,2},{4,5},{5,4},{6,7},{7,6},{8,9},{9,8},{10,11... | collective-permute-start | bytes 1327112 | tf_op jit(solution)/shard_map/ppermute | solution.py:37
  51.7 1.9 %collective-permute-start.3 = (bf16[192,1152]{1,0:T(8,128)(2,1)S(1)}, bf16[192,1152]{1,0:T(8,128)(2,1)S(1)}, u32[]{:S(2)}, u32[]{:S(2)}) collective-permute-start(bf16[192,1152]{1,0:T(8,128)(2,1)S(1)} %all_gather.6.refs_0_), channel_id=1, source_target_pairs={{0,16},{16,32},{32,48},{48,64},{64,80},{80,96},{96,112},{112,128},... | collective-permute-start | bytes 1327112 | tf_op jit(solution)/shard_map/ppermute | solution.py:33
  53.6 4.6 %collective-permute-start.4 = (bf16[192,1152]{1,0:T(8,128)(2,1)S(1)}, bf16[192,1152]{1,0:T(8,128)(2,1)}, u32[]{:S(2)}, u32[]{:S(2)}) collective-permute-start(bf16[192,1152]{1,0:T(8,128)(2,1)S(1)} %all_gather.6.refs_0_), channel_id=1, source_target_pairs={{0,240},{16,0},{32,16},{48,32},{64,48},{80,64},{96,80},{112,96},{1... | collective-permute-start | bytes 1327112 | tf_op jit(solution)/shard_map/ppermute | solution.py:33
  58.2 2.5 %collective-permute-start.2 = (bf16[288,1152]{1,0:T(8,128)(2,1)}, bf16[288,1152]{1,0:T(8,128)(2,1)}, u32[]{:S(2)}, u32[]{:S(2)}) collective-permute-start(bf16[288,1152]{1,0:T(8,128)(2,1)} %collective-permute-done.refs_1_), channel_id=1, source_target_pairs={{0,1},{1,0},{2,3},{3,2},{4,5},{5,4},{6,7},{7,6},{8,9},{9,8},{10,11... | collective-permute-start | bytes 1990664 | tf_op jit(solution)/shard_map/ppermute | solution.py:37
  60.7 0.8 fusion.2
  63.9 1.9 %collective-permute-start.5 = (bf16[96,1152]{1,0:T(8,128)(2,1)}, bf16[96,1152]{1,0:T(8,128)(2,1)}, u32[]{:S(2)}, u32[]{:S(2)}) collective-permute-start(bf16[96,1152]{1,0:T(8,128)(2,1)} %get-tuple-element.11), channel_id=1, source_target_pairs={{0,32},{16,48},{32,64},{48,80},{64,96},{80,112},{96,128},{112,144}... | collective-permute-start | bytes 663560 | tf_op jit(solution)/shard_map/ppermute | solution.py:33
  65.8 5.5 %collective-permute-start.6 = (bf16[96,1152]{1,0:T(8,128)(2,1)}, bf16[96,1152]{1,0:T(8,128)(2,1)}, u32[]{:S(2)}, u32[]{:S(2)}) collective-permute-start(bf16[96,1152]{1,0:T(8,128)(2,1)} %get-tuple-element.10), channel_id=1, source_target_pairs={{0,224},{16,240},{32,0},{48,16},{64,32},{80,48},{96,64},{112,80},{... | collective-permute-start | bytes 663560 | tf_op jit(solution)/shard_map/ppermute | solution.py:33
  71.3 1.2 copy-done.1
  72.5 1.5 %copy-done.2 = bf16[16,48,1152]{2,1,0:T(8,128)(2,1)S(1)} copy-done((bf16[16,48,1152]{2,1,0:T(8,128)(2,1)S(1)}, bf16[16,48,1152]{2,1,0:T(8,128)(2,1)}, u32[]{:S(2)}) %copy-start.2) | copy-done | bytes 1769496
  74.0 1.1 copy-done.7
  75.1 5.6 %shard_map.77 = (bf16[768,1152]{1,0:T(8,128)(2,1)S(1)}, bf16[1152,1152]{1,0:T(8,128)(2,1)S(1)}, bf16[96,1152]{1,0:T(8,128)(2,1)S(1)}) custom-call(s32[5]{0:T(128)S(1)} %stack.52.place_ref, bf16[768,1152]{1,0:T(8,128)(2,1)S(1)} %bitcast.30, bf16[288,1152]{1,0:T(8,128)(2,1)S(1)} %copy-done.7, bf16[288,1152]{1,0:T(8,128)(2,1)} %collective-permute-done.refs_1_, ...), custom_call_target="tpu_custom_call" | custom-call | flops 2038431744 | bytes 8847360 | tf_op jit(solution)/shard_map/pallas_call | solution.py:86
  80.7 0.7 copy-done.3
  81.4 4.4 %shard_map.79.refs_4_.refs_1_ = f32[768,1152]{1,0:T(8,128)S(1)} custom-call(f32[4]{0:T(128)S(1)} %pad_maximum_fusion.1.scalars_ref, s32[2]{0:T(128)S(1)} %pad_add_fusion.place_ref, bf16[768,1152]{1,0:T(8,128)(2,1)S(1)} %get-tuple-element.5.text_ref, bf16[192,1152]{1,0:T(8,128)(2,1)S(1)} %all_gather.6.refs_0_, bf16[192,1152]{1,0:T(8,128)(2,1)} %collective-permute-done.7.refs_1_), custom_call_target="tpu_custom_call" | custom-call | flops 1358954496 | bytes 6193152 | tf_op jit(solution)/shard_map/pallas_call | solution.py:141
  85.8 1.5 %shard_map.80.refs_0_ = bf16[576,1152]{1,0:T(8,128)(2,1)S(1)} custom-call(bf16[192,1152]{1,0:T(8,128)(2,1)S(1)} %collective-permute-done.3.refs_0_, bf16[192,1152]{1,0:T(8,128)(2,1)} %collective-permute-done.4.refs_1_, bf16[96,1152]{1,0:T(8,128)(2,1)} %collective-permute-done.5.refs_2_, bf16[96,1152]{1,0:T(8,128)(2,1)} %collective-permute-done.6.refs_3_, ...), custom_call_target="tpu_custom_call" | custom-call | bytes 2654208 | tf_op jit(solution)/shard_map/pallas_call | solution.py:168
  87.3 2.5 %collective-permute-start.8 = (bf16[576,1152]{1,0:T(8,128)(2,1)S(1)}, bf16[576,1152]{1,0:T(8,128)(2,1)S(1)}, u32[]{:S(2)}, u32[]{:S(2)}) collective-permute-start(bf16[576,1152]{1,0:T(8,128)(2,1)S(1)} %shard_map.80.refs_0_), channel_id=1, source_target_pairs={{0,1},{1,0},{2,3},{3,2},{4,5},{5,4},{6,7},{7,6},{8,9},{9,8},{10,11... | collective-permute-start | bytes 3981320 | tf_op jit(solution)/shard_map/ppermute | solution.py:37
  89.8 4.2 %shard_map.81.refs_1_ = f32[768,1152]{1,0:T(8,128)S(1)} custom-call(f32[4]{0:T(128)S(1)} %pad_maximum_fusion.1.scalars_ref, s32[2]{0:T(128)S(1)} %pad_add_fusion.place_ref, bf16[768,1152]{1,0:T(8,128)(2,1)S(1)} %get-tuple-element.5.text_ref, bf16[576,1152]{1,0:T(8,128)(2,1)S(1)} %shard_map.80.refs_0_, f32[768,1152]{1,0:T(8,128)S(1)} %shard_map.79.refs_4_.refs_1_), custom_call_target="tpu_custom_call" | custom-call | flops 2038431744 | bytes 6635520 | tf_op jit(solution)/shard_map/pallas_call | solution.py:141
  94.0 4.2 %shard_map.82 = bf16[768,1152]{1,0:T(8,128)(2,1)S(1)} custom-call(f32[4]{0:T(128)S(1)} %pad_maximum_fusion.1.scalars_ref, s32[2]{0:T(128)S(1)} %pad_add_fusion.place_ref, bf16[768,1152]{1,0:T(8,128)(2,1)S(1)} %get-tuple-element.5.text_ref, bf16[576,1152]{1,0:T(8,128)(2,1)S(1)} %collective-permute-done.8.refs_0_, f32[768,1152]{1,0:T(8,128)S(1)} %shard_map.81.refs_1_), custom_call_target="tpu_custom_call" | custom-call | flops 2038431744 | bytes 6635520 | tf_op jit(solution)/shard_map/pallas_call | solution.py:141
  98.2 1.2 copy-done
  99.4 6.3 %all-to-all-start.1 = ((bf16[16,48,1152]{2,1,0:T(8,128)(2,1)}), bf16[16,48,1152]{2,1,0:T(8,128)(2,1)}, u32[]{:S(2)}, u32[]{:S(2)}) async-start(bf16[16,48,1152]{2,1,0:T(8,128)(2,1)} %bitcast.29), calls=%async_computation.1 | async-start | bytes 3538944 | tf_op jit(solution)/shard_map/all_to_all | solution.py:242
  105.7 2.2 %collective-permute-start.9 = (bf16[96,1152]{1,0:T(8,128)(2,1)S(1)}, bf16[96,1152]{1,0:T(8,128)(2,1)S(1)}, u32[]{:S(2)}, u32[]{:S(2)}) collective-permute-start(bf16[96,1152]{1,0:T(8,128)(2,1)S(1)} %copy-done.4), channel_id=1, source_target_pairs={{0,1},{1,0},{2,3},{3,2},{4,5},{5,4},{6,7},{7,6},{8,9},{9,8},{10,11... | collective-permute-start | bytes 663560 | tf_op jit(solution)/shard_map/ppermute | solution.py:37
  107.9 0.6 convolution_bitcast_fusion.1.projected_ref
  108.5 0.6 collective-permute-done.9
  109.2 23.3 %all-to-all-done.1.parts_ref = bf16[16,48,1152]{2,1,0:T(8,128)(2,1)} async-done(((bf16[16,48,1152]{2,1,0:T(8,128)(2,1)}), bf16[16,48,1152]{2,1,0:T(8,128)(2,1)}, u32[]{:S(2)}, u32[]{:S(2)}) %all-to-all-start.1) | async-done | bytes 1769504 | tf_op jit(solution)/shard_map/all_to_all | solution.py:242
  132.5 1.8 %shard_map.83 = bf16[48,1152]{1,0:T(8,128)(2,1)S(1)} custom-call(bf16[16,48,1152]{2,1,0:T(8,128)(2,1)} %all-to-all-done.1.parts_ref, f32[48,1152]{1,0:T(8,128)S(1)} %convolution_bitcast_fusion.1.projected_ref), custom_call_target="tpu_custom_call" | custom-call | tf_op jit(solution)/shard_map/pallas_call | solution.py:193
  134.3 8.4 %all_gather.7 = bf16[192,1152]{1,0:T(8,128)(2,1)S(1)} all-gather(bf16[48,1152]{1,0:T(8,128)(2,1)S(1)} %shard_map.83), channel_id=1, replica_groups=mesh['xh'=2,'za'=4,'zb'=4,'y'=4,'xl'=2,'c'=2] {'xl','c'}, dimensions={0}, use_global_device_ids=true | all-gather | bytes 552960 | tf_op jit(solution)/shard_map/all_gather | solution.py:254
  142.8 1.6 %convolution_convert_fusion = bf16[48,1152]{1,0:T(8,128)(2,1)} fusion(bf16[48,1152]{1,0:T(8,128)(2,1)S(1)} %shard_map.83, bf16[1152,1152]{1,0:T(8,128)(2,1)S(1)} %get-tuple-element.6), kind=kOutput, calls=%fused_computation.2 | convolution fusion | flops 127457280 | bytes 2875392 | tf_op jit(solution)/shard_map/dot_general | solution.py:253
  144.3 1.5 %convolution_bitcast_fusion = f32[1,288,1152]{2,1,0:T(8,128)} fusion(bf16[192,1152]{1,0:T(8,128)(2,1)S(1)} %all_gather.7, bf16[192,1152]{1,0:T(8,128)(2,1)S(1)} %bitcast.33, s32[]{:T(128)S(6)} %select_n.18), kind=kOutput, calls=%fused_computation | convolution fusion | flops 127401984 | bytes 1916932 | tf_op jit(solution)/shard_map/dot_general | solution.py:255
  (29 shorter events, 0.5 us)
Async XLA Ops:
  0.6 10.0 %copy-start.6 = (bf16[288,1152]{1,0:T(8,128)(2,1)S(1)}, bf16[288,1152]{1,0:T(8,128)(2,1)}, u32[]{:S(2)}) copy-start(bf16[288,1152]{1,0:T(8,128)(2,1)} %refs_0_.1) | copy-start | bytes 1990660
  0.6 18.6 %copy-start.5 = (bf16[48,1152]{1,0:T(8,128)(2,1)S(1)}, bf16[48,1152]{1,0:T(8,128)(2,1)}, u32[]{:S(2)}) copy-start(bf16[48,1152]{1,0:T(8,128)(2,1)} %rows_ref.1) | copy-start | bytes 331780
  3.0 68.3 %all-to-all-start = ((bf16[16,48,1152]{2,1,0:T(8,128)(2,1)}), bf16[16,48,1152]{2,1,0:T(8,128)(2,1)S(1)}, u32[]{:S(2)}, u32[]{:S(2)}) async-start(bf16[16,48,1152]{2,1,0:T(8,128)(2,1)} %tile.2), calls=%async_computation | async-start | bytes 3538944 | tf_op jit(solution)/shard_map/all_to_all | solution.py:208
  10.6 47.6 %collective-permute-start = (bf16[288,1152]{1,0:T(8,128)(2,1)S(1)}, bf16[288,1152]{1,0:T(8,128)(2,1)}, u32[]{:S(2)}, u32[]{:S(2)}) collective-permute-start(bf16[288,1152]{1,0:T(8,128)(2,1)S(1)} %copy-done.6), channel_id=1, source_target_pairs={{0,2},{2,0},{1,3},{3,1},{4,6},{6,4},{5,7},{7,5},{8,10},{10,8},{9,1... | collective-permute-start | bytes 1990664 | tf_op jit(solution)/shard_map/ppermute | solution.py:210
  13.9 50.0 %collective-permute-start.1 = (bf16[288,1152]{1,0:T(8,128)(2,1)S(1)}, bf16[288,1152]{1,0:T(8,128)(2,1)}, u32[]{:S(2)}, u32[]{:S(2)}) collective-permute-start(bf16[288,1152]{1,0:T(8,128)(2,1)S(1)} %copy-done.6), channel_id=1, source_target_pairs={{0,1},{1,0},{2,3},{3,2},{4,5},{5,4},{6,7},{7,6},{8,9},{9,8},{10,11... | collective-permute-start | bytes 1990664 | tf_op jit(solution)/shard_map/ppermute | solution.py:37
  46.6 34.8 %collective-permute-start.7 = (bf16[192,1152]{1,0:T(8,128)(2,1)S(1)}, bf16[192,1152]{1,0:T(8,128)(2,1)}, u32[]{:S(2)}, u32[]{:S(2)}) collective-permute-start(bf16[192,1152]{1,0:T(8,128)(2,1)S(1)} %all_gather.6.refs_0_), channel_id=1, source_target_pairs={{0,1},{1,0},{2,3},{3,2},{4,5},{5,4},{6,7},{7,6},{8,9},{9,8},{10,11... | collective-permute-start | bytes 1327112 | tf_op jit(solution)/shard_map/ppermute | solution.py:37
  51.7 34.1 %collective-permute-start.3 = (bf16[192,1152]{1,0:T(8,128)(2,1)S(1)}, bf16[192,1152]{1,0:T(8,128)(2,1)S(1)}, u32[]{:S(2)}, u32[]{:S(2)}) collective-permute-start(bf16[192,1152]{1,0:T(8,128)(2,1)S(1)} %all_gather.6.refs_0_), channel_id=1, source_target_pairs={{0,16},{16,32},{32,48},{48,64},{64,80},{80,96},{96,112},{112,128},... | collective-permute-start | bytes 1327112 | tf_op jit(solution)/shard_map/ppermute | solution.py:33
  53.6 32.2 %collective-permute-start.4 = (bf16[192,1152]{1,0:T(8,128)(2,1)S(1)}, bf16[192,1152]{1,0:T(8,128)(2,1)}, u32[]{:S(2)}, u32[]{:S(2)}) collective-permute-start(bf16[192,1152]{1,0:T(8,128)(2,1)S(1)} %all_gather.6.refs_0_), channel_id=1, source_target_pairs={{0,240},{16,0},{32,16},{48,32},{64,48},{80,64},{96,80},{112,96},{1... | collective-permute-start | bytes 1327112 | tf_op jit(solution)/shard_map/ppermute | solution.py:33
  58.2 7.6 %collective-permute-start.2 = (bf16[288,1152]{1,0:T(8,128)(2,1)}, bf16[288,1152]{1,0:T(8,128)(2,1)}, u32[]{:S(2)}, u32[]{:S(2)}) collective-permute-start(bf16[288,1152]{1,0:T(8,128)(2,1)} %collective-permute-done.refs_1_), channel_id=1, source_target_pairs={{0,1},{1,0},{2,3},{3,2},{4,5},{5,4},{6,7},{7,6},{8,9},{9,8},{10,11... | collective-permute-start | bytes 1990664 | tf_op jit(solution)/shard_map/ppermute | solution.py:37
  63.9 21.9 %collective-permute-start.5 = (bf16[96,1152]{1,0:T(8,128)(2,1)}, bf16[96,1152]{1,0:T(8,128)(2,1)}, u32[]{:S(2)}, u32[]{:S(2)}) collective-permute-start(bf16[96,1152]{1,0:T(8,128)(2,1)} %get-tuple-element.11), channel_id=1, source_target_pairs={{0,32},{16,48},{32,64},{48,80},{64,96},{80,112},{96,128},{112,144}... | collective-permute-start | bytes 663560 | tf_op jit(solution)/shard_map/ppermute | solution.py:33
  65.8 20.0 %collective-permute-start.6 = (bf16[96,1152]{1,0:T(8,128)(2,1)}, bf16[96,1152]{1,0:T(8,128)(2,1)}, u32[]{:S(2)}, u32[]{:S(2)}) collective-permute-start(bf16[96,1152]{1,0:T(8,128)(2,1)} %get-tuple-element.10), channel_id=1, source_target_pairs={{0,224},{16,240},{32,0},{48,16},{64,32},{80,48},{96,64},{112,80},{... | collective-permute-start | bytes 663560 | tf_op jit(solution)/shard_map/ppermute | solution.py:33
  71.3 1.2 copy-start.1
  72.5 1.5 %copy-start.2 = (bf16[16,48,1152]{2,1,0:T(8,128)(2,1)S(1)}, bf16[16,48,1152]{2,1,0:T(8,128)(2,1)}, u32[]{:S(2)}) copy-start(bf16[16,48,1152]{2,1,0:T(8,128)(2,1)} %copy-done.1) | copy-start | bytes 5308420
  74.0 1.1 copy-start.7
  80.7 0.7 copy-start.3
  87.3 6.7 %collective-permute-start.8 = (bf16[576,1152]{1,0:T(8,128)(2,1)S(1)}, bf16[576,1152]{1,0:T(8,128)(2,1)S(1)}, u32[]{:S(2)}, u32[]{:S(2)}) collective-permute-start(bf16[576,1152]{1,0:T(8,128)(2,1)S(1)} %shard_map.80.refs_0_), channel_id=1, source_target_pairs={{0,1},{1,0},{2,3},{3,2},{4,5},{5,4},{6,7},{7,6},{8,9},{9,8},{10,11... | collective-permute-start | bytes 3981320 | tf_op jit(solution)/shard_map/ppermute | solution.py:37
  98.2 1.2 copy-start
  99.4 6.3 %copy-start.4 = (bf16[96,1152]{1,0:T(8,128)(2,1)S(1)}, bf16[96,1152]{1,0:T(8,128)(2,1)}, u32[]{:S(2)}) copy-start(bf16[96,1152]{1,0:T(8,128)(2,1)} %copy-done.3) | copy-start | bytes 663556
  99.4 8.5 %copy-start.8 = (bf16[48,1152]{1,0:T(8,128)(2,1)S(1)}, bf16[48,1152]{1,0:T(8,128)(2,1)}, u32[]{:S(2)}) copy-start(bf16[48,1152]{1,0:T(8,128)(2,1)} %param.6) | copy-start | bytes 331780
  99.4 33.1 %all-to-all-start.1 = ((bf16[16,48,1152]{2,1,0:T(8,128)(2,1)}), bf16[16,48,1152]{2,1,0:T(8,128)(2,1)}, u32[]{:S(2)}, u32[]{:S(2)}) async-start(bf16[16,48,1152]{2,1,0:T(8,128)(2,1)} %bitcast.29), calls=%async_computation.1 | async-start | bytes 3538944 | tf_op jit(solution)/shard_map/all_to_all | solution.py:242
  105.7 3.4 %collective-permute-start.9 = (bf16[96,1152]{1,0:T(8,128)(2,1)S(1)}, bf16[96,1152]{1,0:T(8,128)(2,1)S(1)}, u32[]{:S(2)}, u32[]{:S(2)}) collective-permute-start(bf16[96,1152]{1,0:T(8,128)(2,1)S(1)} %copy-done.4), channel_id=1, source_target_pairs={{0,1},{1,0},{2,3},{3,2},{4,5},{5,4},{6,7},{7,6},{8,9},{9,8},{10,11... | collective-permute-start | bytes 663560 | tf_op jit(solution)/shard_map/ppermute | solution.py:37

commit v3 on v2

--- a/solution.py
+++ b/solution.py
@@ -16,13 +16,14 @@
 
 epsilon = 1e-06
 LOG2E = 1.4426950408889634
-WIDE = 256
+TOTAL_ROWS = 24576
 VMEM_BYTES = 18 * 2**20
 BY_COLUMNS = (((1,), (1,)), ((), ()))
 
 IN_VMEM = pl.BlockSpec(memory_space=pltpu.VMEM)
 IN_SMEM = pl.BlockSpec(memory_space=pltpu.SMEM)
 ANYWHERE = pl.BlockSpec(memory_space=pl.ANY)
+IN_HBM = pl.BlockSpec(memory_space=pltpu.HBM)
 
 
 def shift(step, size):
@@ -65,7 +66,8 @@
 
 
 def project_kernel(block, place_ref, from_ref, *refs):
-    pieces, (text_ref, head_ref, pair_ref, rows_ref, sems, rows_sem) = refs[:-6], refs[-6:]
+    settings, pieces, refs = refs[:3], refs[3:-7], refs[-7:]
+    text_ref, head_ref, pair_ref, scalars_ref, rows_ref, sems, rows_sem = refs
     copy = pltpu.make_async_copy(from_ref, rows_ref, rows_sem)
     copy.start()
     depth = pieces[0].shape[0]
@@ -77,11 +79,18 @@
         projected = jnp.dot(rows_ref[at], head_ref[...], preferred_element_type=jnp.float32)
         norm = jnp.sqrt(jnp.sum(projected * projected, axis=-1, keepdims=True) + epsilon)
         text_ref[at] = (projected * (1.0 / norm)).astype(text_ref.dtype)
+    coldness, offset, weighting = (setting[...] for setting in settings)
+    sharpness = jnp.exp(coldness)
+    factor = sharpness * weighting * (1.0 / TOTAL_ROWS)
+    raised, log_factor = offset * LOG2E, jnp.log2(factor)
+    scalars = [sharpness * LOG2E, -raised - log_factor, raised - log_factor, 1.0 / factor]
+    for k, scalar in enumerate(scalars):
+        scalars_ref[k : k + 1] = jnp.broadcast_to(scalar, (1, scalars_ref.shape[1]))
     count = pair_ref.shape[0]
     pair_ref[...] = rows_ref[pl.ds(pl.multiple_of(place_ref[len(pieces)] * count, 32), count)]
 
 
-def project(place, rows, pieces, pair):
+def project(place, rows, settings, pieces, pair):
     count, width = rows.shape
     return pl.pallas_call(
         functools.partial(project_kernel, count // 2),
@@ -89,73 +98,92 @@
             jax.ShapeDtypeStruct((count, width), jnp.bfloat16),
             jax.ShapeDtypeStruct((width, width), jnp.bfloat16),
             jax.ShapeDtypeStruct((pair, width), jnp.bfloat16),
+            jax.ShapeDtypeStruct((8, 128), jnp.float32),
         ],
-        in_specs=[IN_SMEM] + [ANYWHERE] * (1 + len(pieces)),
-        out_specs=[IN_VMEM] * 3,
+        in_specs=[IN_SMEM, IN_HBM] + [IN_VMEM] * 3 + [ANYWHERE] * len(pieces),
+        out_specs=[IN_VMEM] * 4,
         scratch_shapes=[
             pltpu.VMEM((count, width), jnp.bfloat16),
             pltpu.SemaphoreType.DMA((len(pieces),)),
             pltpu.SemaphoreType.DMA,
         ],
-        compiler_params=pltpu.CompilerParams(vmem_limit_bytes=VMEM_BYTES),
-        cost_estimate=pl.CostEstimate(
-            flops=2 * count * width * width,
-            bytes_accessed=4 * width * (count + width),
-            transcendentals=0,
-        ),
-    )(place, rows, *pieces)
-
-
-def meet_kernel(block, own_rows, added, scalars_ref, place_ref, text_ref, *refs):
-    pieces, (out_ref, images_ref, sems) = refs[:-3], refs[-3:]
-    if added:
-        pieces, sum_ref = pieces[:-1], pieces[-1]
-    starts = [sum(p.shape[0] for p in pieces[:k]) for k in range(len(pieces))]
-    lay(pieces, images_ref, sems, starts)
-    scale, plus, minus, rest = (scalars_ref[k] for k in range(4))
-    for start in range(0, text_ref.shape[0], block):
-        at = pl.ds(start, block)
+        compiler_params=pltpu.CompilerParams(vmem_limit_bytes=46 * 2**20),
+    )(place, rows, *settings, *pieces)
+
+
+def meet_kernel(block, own_rows, last, place_ref, text_ref, *refs):
+    scalars_ref, refs = refs[0], refs[1:]
+    if last:
+        pieces, (sum_ref, _, into_ref, images_ref, sems, out_ref, out_sems) = refs[:-7], refs[-7:]
+    else:
+        pieces, (out_ref, images_ref, sems) = refs[:-3], refs[-3:]
+        if not own_rows:
+            pieces, sum_ref = pieces[:-1], pieces[-1]
+    lay(pieces, images_ref, sems, [sum(p.shape[0] for p in pieces[:k]) for k in range(len(pieces))])
+    scale, plus, minus, rest = (scalars_ref[k : k + 1, :1] for k in range(4))
+
+    def result(k):
+        at = pl.ds(pl.multiple_of(k * block, block), block)
+        return pltpu.make_async_copy(out_ref.at[at], into_ref.at[at], out_sems.at[k])
+
+    def step(k, _):
+        at = pl.ds(pl.multiple_of(k * block, block), block)
         cosine = lax.dot_general(
             text_ref[at], images_ref[...], BY_COLUMNS, preferred_element_type=jnp.float32
         )
         weights = 1.0 / (jnp.exp2(plus - cosine * scale) + rest)
-        if own_rows:
-            text = lax.broadcasted_iota(jnp.int32, (block, WIDE), 0) + (start - place_ref[0])
-            image = lax.broadcasted_iota(jnp.int32, (block, WIDE), 1) - place_ref[1]
-            paired = -1.0 / (jnp.exp2(cosine[:, :WIDE] * scale + minus) + rest)
-            own = (text == image) & (text >= 0) & (text < own_rows)
-            first = jnp.where(own, paired, weights[:, :WIDE])
-            weights = jnp.concatenate([first, weights[:, WIDE:]], axis=1)
         grad = jnp.dot(
             weights.astype(jnp.bfloat16), images_ref[...], preferred_element_type=jnp.float32
         )
-        if added:
+        if not own_rows:
             grad = sum_ref[at] + grad
         out_ref[at] = grad.astype(out_ref.dtype)
-
-
-def meet(scalars, place, text, pieces, total=None, own_rows=0, dtype=jnp.float32):
+        if last:
+            result(k).start()
+        return 0
+
+    steps = text_ref.shape[0] // block
+    lax.fori_loop(0, steps, step, 0)
+    if own_rows:
+        own = pl.ds(pl.multiple_of(place_ref[5], 16), own_rows)
+        image = images_ref[pl.ds(pl.multiple_of(place_ref[6], 16), own_rows)].astype(jnp.float32)
+        cosine = jnp.sum(text_ref[own].astype(jnp.float32) * image, axis=-1, keepdims=True)
+        apart = 1.0 / (jnp.exp2(plus - cosine * scale) + rest)
+        paired = -1.0 / (jnp.exp2(cosine * scale + minus) + rest)
+        change = paired.astype(jnp.bfloat16).astype(jnp.float32)
+        change = change - apart.astype(jnp.bfloat16).astype(jnp.float32)
+        out_ref[own] = out_ref[own] + change * image
+    if last:
+        for k in range(steps):
+            result(k).wait()
+
+
+def meet(scalars, place, text, pieces, total=None, into=None, own_rows=0):
     count, width = text.shape
     images = sum(p.shape[0] for p in pieces)
-    given = () if total is None else (total,)
-    return pl.pallas_call(
-        functools.partial(meet_kernel, count // 2, own_rows, len(given)),
-        out_shape=jax.ShapeDtypeStruct((count, width), dtype),
-        in_specs=[IN_SMEM, IN_SMEM, IN_VMEM]
+    last = into is not None
+    given = [a for a in (total, into) if a is not None]
+    return pl.pallas_call(
+        functools.partial(meet_kernel, count // 2, own_rows, last),
+        out_shape=jax.ShapeDtypeStruct((count, width), jnp.bfloat16 if last else jnp.float32),
+        in_specs=[IN_SMEM, IN_VMEM]
+        + [IN_VMEM]
         + [ANYWHERE] * len(pieces)
-        + [IN_VMEM] * len(given),
-        out_specs=IN_VMEM,
+        + [IN_VMEM, IN_HBM][: len(given)],
+        out_specs=IN_HBM if last else IN_VMEM,
         scratch_shapes=[
             pltpu.VMEM((images, width), jnp.bfloat16),
             pltpu.SemaphoreType.DMA((len(pieces),)),
-        ],
+        ]
+        + ([pltpu.VMEM((count, width), jnp.bfloat16), pltpu.SemaphoreType.DMA((2,))] if last else []),
+        input_output_aliases={4 + len(pieces): 0} if last else {},
         compiler_params=pltpu.CompilerParams(vmem_limit_bytes=VMEM_BYTES),
         cost_estimate=pl.CostEstimate(
             flops=4 * count * images * width,
             bytes_accessed=2 * width * (3 * count + images),
             transcendentals=2 * count * images,
         ),
-    )(scalars, place, text, *pieces, *given)
+    )(place, text, scalars, *pieces, *given)
 
 
 def join_kernel(*refs):
@@ -208,9 +236,9 @@
     plane_features = lax.all_to_all(jnp.tile(features, (plane, 1)), PLANE, 0, 0, tiled=True)
 
     crossed = lax.ppermute(head_rows, "xl", shift(1, 2))
-    head_pieces = [head_rows, crossed, other_core(head_rows), other_core(crossed)]
-    at = [(xl * 2 + c), ((1 - xl) * 2 + c), (xl * 2 + 1 - c), ((1 - xl) * 2 + 1 - c), xh * 4 + y]
-    head_place = jnp.stack([a.astype(jnp.int32) for a in at])
+    at = [xl * 2 + c, (1 - xl) * 2 + c, xl * 2 + 1 - c, (1 - xl) * 2 + 1 - c]
+    at += [xh * 4 + y, place, za * rows]
+    places = jnp.stack([a.astype(jnp.int32) for a in at])
 
     own = unit_rows(pictures)
     quarter = lax.all_gather(own, "za", axis=0, tiled=True)
@@ -221,23 +249,14 @@
         along_z(quarter[:half], 2),
         along_z(quarter[half:], -2),
     ]
-    early = [quarter, other_core(quarter)]
-
-    text, head, pair = project(head_place, plane_features, head_pieces, 2 * rows)
-
-    sharpness = jnp.exp(coldness[0])
-    factor = sharpness * weighting[0] / (rows * 512)
-    log_factor = jnp.log2(factor)
-    shift_up = offset[0] * LOG2E
-    scalars = jnp.stack(
-        [sharpness * LOG2E, -shift_up - log_factor, shift_up - log_factor, 1.0 / factor]
-    )
-    places = jnp.stack([place, (za * rows).astype(jnp.int32)])
-    total = meet(scalars, places, text, early, own_rows=rows)
-    late = join(late, total)
-    late_other = other_core(late)
-    total = meet(scalars, places, text, [late], total)
-    partial = meet(scalars, places, text, [late_other], total, dtype=jnp.bfloat16)
+    head_pieces = [head_rows, crossed, other_core(head_rows), other_core(crossed)]
+    settings = [setting.reshape(1, 1) for setting in (coldness, offset, weighting)]
+    text, head, pair, scalars = project(places, plane_features, settings, head_pieces, 2 * rows)
+
+    line = join([quarter] + late, text)
+    other_line = other_core(line)
+    total = meet(scalars, places, text, [line], own_rows=rows)
+    partial = meet(scalars, places, text, [other_line], total, plane_features)
 
     parts = lax.all_to_all(partial, PLANE, 0, 0, tiled=True).reshape(plane, rows, width)
 
@@ -250,8 +269,9 @@
     )
 
     proj_grad = finish(parts, projected)
+    group_grad = lax.all_gather(proj_grad, FSDP, axis=0, tiled=True)
+    proj_grad, _ = lax.optimization_barrier((proj_grad, group_grad))
     feat_grad = lax.dot_general(proj_grad, head, BY_COLUMNS, preferred_element_type=jnp.float32)
-    group_grad = lax.all_gather(proj_grad, FSDP, axis=0, tiled=True)
     head_grad = lax.dot_general(
         columns, group_grad, (((0,), (0,)), ((), ())), preferred_element_type=jnp.float32
     )

time: 147 us -> 140 us (0.952)
  local copies, waits for them, and re-layouts: 8.97 us -> 3.18 us
  Pallas kernels: 21.8 us -> 18.2 us
  matrix products: 3.67 us -> 7.15 us
  blocking collectives: 35.7 us -> 33.5 us
  waiting for transfers between devices: 23.9 us -> 25.6 us
    unnamed x18 -> x10, local copies, waits for them, and re-layouts: 5.72 us -> 0.02 us
    ppermute x4, waiting for transfers between devices: 0.01 us -> 3.66 us  [along_z(): return lax.ppermute(array, LINE, shift(step % 16, 16))]
    pallas_call x3 -> x2, Pallas kernels: 12.8 us -> 11 us  [meet(): pl.pallas_call(functools.partial(meet_kernel, count // 2, own_rows, last)...]
    dot_general x1, matrix products: 0.57 us -> 2.32 us  [body(): projected = jnp.dot(features, head, preferred_element_type=jnp.float32)]
    dot_general x1, matrix products: 1.55 us -> 3.29 us  [body(): lax.dot_general(proj_grad, head, BY_COLUMNS, preferred_element_type=jnp.f...]
    all_gather x1, blocking collectives: 27.2 us -> 25.6 us  [body(): quarter = lax.all_gather(own, 'za', axis=0, tiled=True)]
    pallas_call x1, Pallas kernels: 1.83 us -> 0.36 us  [finish(): pl.pallas_call(finish_kernel, out_shape=jax.ShapeDtypeStruct(projected.sh...]
    ppermute x5 -> x4, starting transfers between devices: 17.6 us -> 17.6 us  [other_core(): return lax.ppermute(array, 'c', shift(1, 2))]
  transfers between devices with their start and end apart: 12 -> 11, of which waited for: 2 -> 3; matrix products, arithmetic and copies ran while one was open for 1% -> 2% of each run, Pallas kernels for 10% -> 7%
where the time goes in v3:
time: 140 us
  starting transfers between devices  49.1 us (35%)
  blocking collectives  33.5 us (24%)
  waiting for transfers between devices  25.6 us (18%)
  Pallas kernels  18.2 us (13%)
  matrix products  7.15 us (5%)
  local copies, waits for them, and re-layouts  3.18 us (2%)
  between operations  2.84 us (2%)
    all_gather x1, blocking collectives, body(): quarter = lax.all_gather(own, 'za', axis=0, tiled=True)  25.6 us
    all_to_all x1, waiting for transfers between devices, body(): lax.all_to_all(partial, PLANE, 0, 0, tiled=True).reshape(plane, rows, width)  22 us
    ppermute x4, starting transfers between devices, other_core(): return lax.ppermute(array, 'c', shift(1, 2))  17.6 us
    ppermute x4, starting transfers between devices, along_z(): return lax.ppermute(array, LINE, shift(step % 16, 16))  13.9 us
    pallas_call x2, Pallas kernels, meet(): pl.pallas_call(functools.partial(meet_kernel, count // 2, own_rows, last)...  11 us
    all_gather x1, blocking collectives, body(): group_grad = lax.all_gather(proj_grad, FSDP, axis=0, tiled=True)  7.97 us
    all_to_all x1, starting transfers between devices, body(): lax.all_to_all(jnp.tile(features, (plane, 1)), PLANE, 0, 0, tiled=True)  7.76 us
    all_to_all x1, starting transfers between devices, body(): lax.all_to_all(partial, PLANE, 0, 0, tiled=True).reshape(plane, rows, width)  6.62 us
  transfers between devices with their start and end apart: 11, of which 3 were waited for; matrix products, arithmetic and copies ran while one was open for 2% of the time, Pallas kernels for 7%

profile of v3, /device:TPU:1, one launch (start us, length us, event | category | flops | bytes accessed | tf_op | source)
XLA Modules:
  0.0 139.7 jit_solution(10678289536973623883)
XLA Ops:
  0.6 2.3 %tile.2 = bf16[16,48,1152]{2,1,0:T(8,128)(2,1)} broadcast(bf16[48,1152]{1,0:T(8,128)(2,1)} %param.6), dimensions={1,2} | broadcast | bytes 1880064 | tf_op jit(solution)/shard_map/tile | solution.py:236
  2.9 7.8 %all-to-all-start = ((bf16[16,48,1152]{2,1,0:T(8,128)(2,1)}), bf16[16,48,1152]{2,1,0:T(8,128)(2,1)}, u32[]{:S(2)}, u32[]{:S(2)}) async-start(bf16[16,48,1152]{2,1,0:T(8,128)(2,1)} %tile.2), calls=%async_computation | async-start | bytes 3538944 | tf_op jit(solution)/shard_map/all_to_all | solution.py:236
  10.7 3.2 %collective-permute-start = (bf16[288,1152]{1,0:T(8,128)(2,1)S(1)}, bf16[288,1152]{1,0:T(8,128)(2,1)S(1)}, u32[]{:S(2)}, u32[]{:S(2)}) collective-permute-start(bf16[288,1152]{1,0:T(8,128)(2,1)S(1)} %copy-done), channel_id=1, source_target_pairs={{0,2},{2,0},{1,3},{3,1},{4,6},{6,4},{5,7},{7,5},{8,10},{10,8},{9,1... | collective-permute-start | bytes 1990664 | tf_op jit(solution)/shard_map/ppermute | solution.py:238
  13.9 6.0 %collective-permute-start.1 = (bf16[288,1152]{1,0:T(8,128)(2,1)S(1)}, bf16[288,1152]{1,0:T(8,128)(2,1)S(1)}, u32[]{:S(2)}, u32[]{:S(2)}) collective-permute-start(bf16[288,1152]{1,0:T(8,128)(2,1)S(1)} %copy-done), channel_id=1, source_target_pairs={{0,1},{1,0},{2,3},{3,2},{4,5},{5,4},{6,7},{7,6},{8,9},{9,8},{10,11... | collective-permute-start | bytes 1990664 | tf_op jit(solution)/shard_map/ppermute | solution.py:38
  19.9 0.1 shard_map.78
  20.1 25.6 %all_gather.6.refs_0_ = bf16[192,1152]{1,0:T(8,128)(2,1)S(1)} all-gather(bf16[48,1152]{1,0:T(8,128)(2,1)S(1)} %shard_map.78), channel_id=1, replica_groups=mesh['xh'=2,'za'=4,'zb'=4,'y'=4,'xl'=2,'c'=2] {'za'}, dimensions={0}, use_global_device_ids=true | all-gather | bytes 552960 | tf_op jit(solution)/shard_map/all_gather | solution.py:244
  45.6 4.6 %collective-permute-start.3 = (bf16[192,1152]{1,0:T(8,128)(2,1)S(1)}, bf16[192,1152]{1,0:T(8,128)(2,1)S(1)}, u32[]{:S(2)}, u32[]{:S(2)}) collective-permute-start(bf16[192,1152]{1,0:T(8,128)(2,1)S(1)} %all_gather.6.refs_0_), channel_id=1, source_target_pairs={{0,16},{16,32},{32,48},{48,64},{64,80},{80,96},{96,112},{112,128},... | collective-permute-start | bytes 1327112 | tf_op jit(solution)/shard_map/ppermute | solution.py:34
  50.2 1.9 %collective-permute-start.4 = (bf16[192,1152]{1,0:T(8,128)(2,1)S(1)}, bf16[192,1152]{1,0:T(8,128)(2,1)}, u32[]{:S(2)}, u32[]{:S(2)}) collective-permute-start(bf16[192,1152]{1,0:T(8,128)(2,1)S(1)} %all_gather.6.refs_0_), channel_id=1, source_target_pairs={{0,240},{16,0},{32,16},{48,32},{64,48},{80,64},{96,80},{112,96},{1... | collective-permute-start | bytes 1327112 | tf_op jit(solution)/shard_map/ppermute | solution.py:34
  52.1 0.0 collective-permute-done.refs_4_
  52.1 7.0 %collective-permute-start.2 = (bf16[288,1152]{1,0:T(8,128)(2,1)S(1)}, bf16[288,1152]{1,0:T(8,128)(2,1)S(1)}, u32[]{:S(2)}, u32[]{:S(2)}) collective-permute-start(bf16[288,1152]{1,0:T(8,128)(2,1)S(1)} %collective-permute-done.refs_4_), channel_id=1, source_target_pairs={{0,1},{1,0},{2,3},{3,2},{4,5},{5,4},{6,7},{7,6},{8,9},{9,8},{10,11... | collective-permute-start | bytes 1990664 | tf_op jit(solution)/shard_map/ppermute | solution.py:38
  59.2 0.8 fusion.2
  60.0 1.9 %collective-permute-start.5 = (bf16[96,1152]{1,0:T(8,128)(2,1)}, bf16[96,1152]{1,0:T(8,128)(2,1)}, u32[]{:S(2)}, u32[]{:S(2)}) collective-permute-start(bf16[96,1152]{1,0:T(8,128)(2,1)} %get-tuple-element.15), channel_id=1, source_target_pairs={{0,32},{16,48},{32,64},{48,80},{64,96},{80,112},{96,128},{112,144}... | collective-permute-start | bytes 663560 | tf_op jit(solution)/shard_map/ppermute | solution.py:34
  61.9 0.0 collective-permute-done.1.refs_5_
  61.9 5.5 %collective-permute-start.6 = (bf16[96,1152]{1,0:T(8,128)(2,1)}, bf16[96,1152]{1,0:T(8,128)(2,1)}, u32[]{:S(2)}, u32[]{:S(2)}) collective-permute-start(bf16[96,1152]{1,0:T(8,128)(2,1)} %get-tuple-element.14), channel_id=1, source_target_pairs={{0,224},{16,240},{32,0},{48,16},{64,32},{80,48},{96,64},{112,80},{... | collective-permute-start | bytes 663560 | tf_op jit(solution)/shard_map/ppermute | solution.py:34
  69.3 0.1 stack.34.place_ref
  69.4 5.0 %shard_map.77 = (bf16[768,1152]{1,0:T(8,128)(2,1)S(1)}, bf16[1152,1152]{1,0:T(8,128)(2,1)}, bf16[96,1152]{1,0:T(8,128)(2,1)S(1)}, f32[8,128]{1,0:T(8,128)S(1)}) custom-call(s32[7]{0:T(128)S(1)} %stack.34.place_ref, bf16[768,1152]{1,0:T(8,128)(2,1)} %bitcast.7.from_ref.refs_3_, f32[1,1]{1,0:T(1,128)} %bitcast.28.refs_0_, f32[1,1]{1,0:T(1,128)} %bitcast.29.refs_1_, ...), custom_call_target="tpu_custom_call" | custom-call | tf_op jit(solution)/shard_map/pallas_call | solution.py:95
  74.4 0.7 collective-permute-done.5.refs_3_
  75.2 2.9 %collective-permute-done.6.refs_4_ = bf16[96,1152]{1,0:T(8,128)(2,1)} collective-permute-done((bf16[96,1152]{1,0:T(8,128)(2,1)}, bf16[96,1152]{1,0:T(8,128)(2,1)}, u32[]{:S(2)}, u32[]{:S(2)}) %collective-permute-start.6) | collective-permute-done | bytes 221216 | tf_op jit(solution)/shard_map/ppermute | solution.py:34
  78.1 0.0 collective-permute-done.3.refs_1_
  78.1 1.7 %shard_map.79.refs_1_ = bf16[768,1152]{1,0:T(8,128)(2,1)S(1)} custom-call(bf16[192,1152]{1,0:T(8,128)(2,1)S(1)} %all_gather.6.refs_0_, bf16[192,1152]{1,0:T(8,128)(2,1)S(1)} %collective-permute-done.3.refs_1_, bf16[192,1152]{1,0:T(8,128)(2,1)} %collective-permute-done.4.refs_2_, bf16[96,1152]{1,0:T(8,128)(2,1)} %collective-permute-done.5.refs_3_, ...), custom_call_target="tpu_custom_call" | custom-call | bytes 3538944 | tf_op jit(solution)/shard_map/pallas_call | solution.py:196
  79.8 2.3 %collective-permute-start.7 = (bf16[768,1152]{1,0:T(8,128)(2,1)S(1)}, bf16[768,1152]{1,0:T(8,128)(2,1)S(1)}, u32[]{:S(2)}, u32[]{:S(2)}) collective-permute-start(bf16[768,1152]{1,0:T(8,128)(2,1)S(1)} %shard_map.79.refs_1_), channel_id=1, source_target_pairs={{0,1},{1,0},{2,3},{3,2},{4,5},{5,4},{6,7},{7,6},{8,9},{9,8},{10,11... | collective-permute-start | bytes 5308424 | tf_op jit(solution)/shard_map/ppermute | solution.py:38
  82.2 4.9 %shard_map.80.refs_2_ = f32[768,1152]{1,0:T(8,128)S(1)} custom-call(s32[7]{0:T(128)S(1)} %stack.34.place_ref, bf16[768,1152]{1,0:T(8,128)(2,1)S(1)} %get-tuple-element.7.refs_5_.text_ref, f32[8,128]{1,0:T(8,128)S(1)} %get-tuple-element.8.refs_0_, bf16[768,1152]{1,0:T(8,128)(2,1)S(1)} %shard_map.79.refs_1_), custom_call_target="tpu_custom_call" | custom-call | flops 2717908992 | bytes 7077888 | tf_op jit(solution)/shard_map/pallas_call | solution.py:166
  87.1 6.1 %shard_map.81 = bf16[768,1152]{1,0:T(8,128)(2,1)} custom-call(s32[7]{0:T(128)S(1)} %stack.34.place_ref, bf16[768,1152]{1,0:T(8,128)(2,1)S(1)} %get-tuple-element.7.refs_5_.text_ref, f32[8,128]{1,0:T(8,128)S(1)} %get-tuple-element.8.refs_0_, bf16[768,1152]{1,0:T(8,128)(2,1)S(1)} %collective-permute-done.7.refs_1_, ...), custom_call_target="tpu_custom_call", output_to_operand_aliasing={{}: (5, {})} | custom-call | flops 2717908992 | bytes 7077888 | tf_op jit(solution)/shard_map/pallas_call | solution.py:166
  93.3 0.0 copy-start.4
  93.3 6.6 %all-to-all-start.1 = ((bf16[16,48,1152]{2,1,0:T(8,128)(2,1)}), bf16[16,48,1152]{2,1,0:T(8,128)(2,1)S(1)}, u32[]{:S(2)}, u32[]{:S(2)}) async-start(bf16[16,48,1152]{2,1,0:T(8,128)(2,1)} %bitcast.11), calls=%async_computation.1 | async-start | bytes 3538944 | tf_op jit(solution)/shard_map/all_to_all | solution.py:261
  99.9 2.3 %collective-permute-start.8 = (bf16[96,1152]{1,0:T(8,128)(2,1)S(1)}, bf16[96,1152]{1,0:T(8,128)(2,1)S(1)}, u32[]{:S(2)}, u32[]{:S(2)}) collective-permute-start(bf16[96,1152]{1,0:T(8,128)(2,1)S(1)} %copy-done.2), channel_id=1, source_target_pairs={{0,1},{1,0},{2,3},{3,2},{4,5},{5,4},{6,7},{7,6},{8,9},{9,8},{10,11... | collective-permute-start | bytes 663560 | tf_op jit(solution)/shard_map/ppermute | solution.py:38
  102.2 2.3 %convolution_bitcast_fusion.1.projected_ref = f32[48,1152]{1,0:T(8,128)S(1)} fusion(bf16[48,1152]{1,0:T(8,128)(2,1)S(1)} %copy-done.4, bf16[1152,1152]{1,0:T(8,128)(2,1)} %get-tuple-element.9), kind=kOutput, calls=%fused_computation.1 | convolution fusion | flops 127401984 | bytes 2985984 | tf_op jit(solution)/shard_map/dot_general | solution.py:263
  104.6 22.0 %all-to-all-done.1.parts_ref = bf16[16,48,1152]{2,1,0:T(8,128)(2,1)S(1)} async-done(((bf16[16,48,1152]{2,1,0:T(8,128)(2,1)}), bf16[16,48,1152]{2,1,0:T(8,128)(2,1)S(1)}, u32[]{:S(2)}, u32[]{:S(2)}) %all-to-all-start.1) | async-done | bytes 1769504 | tf_op jit(solution)/shard_map/all_to_all | solution.py:261
  126.6 0.4 shard_map.82
  126.9 8.0 %all_gather.7 = bf16[192,1152]{1,0:T(8,128)(2,1)S(1)} all-gather(bf16[48,1152]{1,0:T(8,128)(2,1)S(1)} %shard_map.82), channel_id=1, replica_groups=mesh['xh'=2,'za'=4,'zb'=4,'y'=4,'xl'=2,'c'=2] {'xl','c'}, dimensions={0}, use_global_device_ids=true | all-gather | bytes 552960 | tf_op jit(solution)/shard_map/all_gather | solution.py:272
  134.9 3.3 %convolution_convert_fusion = bf16[48,1152]{1,0:T(8,128)(2,1)} fusion(bf16[48,1152]{1,0:T(8,128)(2,1)S(1)} %shard_map.82, bf16[1152,1152]{1,0:T(8,128)(2,1)} %get-tuple-element.9), kind=kOutput, calls=%fused_computation.2 | convolution fusion | flops 127457280 | bytes 2875392 | tf_op jit(solution)/shard_map/dot_general | solution.py:274
  138.2 1.5 %convolution_bitcast_fusion = f32[1,288,1152]{2,1,0:T(8,128)} fusion(bf16[192,1152]{1,0:T(8,128)(2,1)S(1)} %all_gather.7, bf16[192,1152]{1,0:T(8,128)(2,1)S(1)} %bitcast.33, s32[]{:T(128)S(6)} %select_n.18), kind=kOutput, calls=%fused_computation | convolution fusion | flops 127401984 | bytes 1916932 | tf_op jit(solution)/shard_map/dot_general | solution.py:275
  (16 shorter events, 0.1 us)
Async XLA Ops:
  2.9 7.8 %copy-start = (bf16[288,1152]{1,0:T(8,128)(2,1)S(1)}, bf16[288,1152]{1,0:T(8,128)(2,1)}, u32[]{:S(2)}) copy-start(bf16[288,1152]{1,0:T(8,128)(2,1)} %refs_3_.1) | copy-start | bytes 1990660
  2.9 17.0 %copy-start.3 = (bf16[48,1152]{1,0:T(8,128)(2,1)S(1)}, bf16[48,1152]{1,0:T(8,128)(2,1)}, u32[]{:S(2)}) copy-start(bf16[48,1152]{1,0:T(8,128)(2,1)} %rows_ref.1) | copy-start | bytes 331780
  2.9 66.5 %all-to-all-start = ((bf16[16,48,1152]{2,1,0:T(8,128)(2,1)}), bf16[16,48,1152]{2,1,0:T(8,128)(2,1)}, u32[]{:S(2)}, u32[]{:S(2)}) async-start(bf16[16,48,1152]{2,1,0:T(8,128)(2,1)} %tile.2), calls=%async_computation | async-start | bytes 3538944 | tf_op jit(solution)/shard_map/all_to_all | solution.py:236
  10.7 41.4 %collective-permute-start = (bf16[288,1152]{1,0:T(8,128)(2,1)S(1)}, bf16[288,1152]{1,0:T(8,128)(2,1)S(1)}, u32[]{:S(2)}, u32[]{:S(2)}) collective-permute-start(bf16[288,1152]{1,0:T(8,128)(2,1)S(1)} %copy-done), channel_id=1, source_target_pairs={{0,2},{2,0},{1,3},{3,1},{4,6},{6,4},{5,7},{7,5},{8,10},{10,8},{9,1... | collective-permute-start | bytes 1990664 | tf_op jit(solution)/shard_map/ppermute | solution.py:238
  13.9 48.0 %collective-permute-start.1 = (bf16[288,1152]{1,0:T(8,128)(2,1)S(1)}, bf16[288,1152]{1,0:T(8,128)(2,1)S(1)}, u32[]{:S(2)}, u32[]{:S(2)}) collective-permute-start(bf16[288,1152]{1,0:T(8,128)(2,1)S(1)} %copy-done), channel_id=1, source_target_pairs={{0,1},{1,0},{2,3},{3,2},{4,5},{5,4},{6,7},{7,6},{8,9},{9,8},{10,11... | collective-permute-start | bytes 1990664 | tf_op jit(solution)/shard_map/ppermute | solution.py:38
  45.6 32.5 %collective-permute-start.3 = (bf16[192,1152]{1,0:T(8,128)(2,1)S(1)}, bf16[192,1152]{1,0:T(8,128)(2,1)S(1)}, u32[]{:S(2)}, u32[]{:S(2)}) collective-permute-start(bf16[192,1152]{1,0:T(8,128)(2,1)S(1)} %all_gather.6.refs_0_), channel_id=1, source_target_pairs={{0,16},{16,32},{32,48},{48,64},{64,80},{80,96},{96,112},{112,128},... | collective-permute-start | bytes 1327112 | tf_op jit(solution)/shard_map/ppermute | solution.py:34
  50.2 27.9 %collective-permute-start.4 = (bf16[192,1152]{1,0:T(8,128)(2,1)S(1)}, bf16[192,1152]{1,0:T(8,128)(2,1)}, u32[]{:S(2)}, u32[]{:S(2)}) collective-permute-start(bf16[192,1152]{1,0:T(8,128)(2,1)S(1)} %all_gather.6.refs_0_), channel_id=1, source_target_pairs={{0,240},{16,0},{32,16},{48,32},{64,48},{80,64},{96,80},{112,96},{1... | collective-permute-start | bytes 1327112 | tf_op jit(solution)/shard_map/ppermute | solution.py:34
  52.1 17.3 %collective-permute-start.2 = (bf16[288,1152]{1,0:T(8,128)(2,1)S(1)}, bf16[288,1152]{1,0:T(8,128)(2,1)S(1)}, u32[]{:S(2)}, u32[]{:S(2)}) collective-permute-start(bf16[288,1152]{1,0:T(8,128)(2,1)S(1)} %collective-permute-done.refs_4_), channel_id=1, source_target_pairs={{0,1},{1,0},{2,3},{3,2},{4,5},{5,4},{6,7},{7,6},{8,9},{9,8},{10,11... | collective-permute-start | bytes 1990664 | tf_op jit(solution)/shard_map/ppermute | solution.py:38
  60.0 15.2 %collective-permute-start.5 = (bf16[96,1152]{1,0:T(8,128)(2,1)}, bf16[96,1152]{1,0:T(8,128)(2,1)}, u32[]{:S(2)}, u32[]{:S(2)}) collective-permute-start(bf16[96,1152]{1,0:T(8,128)(2,1)} %get-tuple-element.15), channel_id=1, source_target_pairs={{0,32},{16,48},{32,64},{48,80},{64,96},{80,112},{96,128},{112,144}... | collective-permute-start | bytes 663560 | tf_op jit(solution)/shard_map/ppermute | solution.py:34
  61.9 16.2 %collective-permute-start.6 = (bf16[96,1152]{1,0:T(8,128)(2,1)}, bf16[96,1152]{1,0:T(8,128)(2,1)}, u32[]{:S(2)}, u32[]{:S(2)}) collective-permute-start(bf16[96,1152]{1,0:T(8,128)(2,1)} %get-tuple-element.14), channel_id=1, source_target_pairs={{0,224},{16,240},{32,0},{48,16},{64,32},{80,48},{96,64},{112,80},{... | collective-permute-start | bytes 663560 | tf_op jit(solution)/shard_map/ppermute | solution.py:34
  74.4 5.4 %copy-start.1 = (bf16[96,1152]{1,0:T(8,128)(2,1)}, bf16[96,1152]{1,0:T(8,128)(2,1)S(1)}, u32[]{:S(2)}) copy-start(bf16[96,1152]{1,0:T(8,128)(2,1)S(1)} %get-tuple-element.11) | copy-start | bytes 663556
  79.8 7.3 %collective-permute-start.7 = (bf16[768,1152]{1,0:T(8,128)(2,1)S(1)}, bf16[768,1152]{1,0:T(8,128)(2,1)S(1)}, u32[]{:S(2)}, u32[]{:S(2)}) collective-permute-start(bf16[768,1152]{1,0:T(8,128)(2,1)S(1)} %shard_map.79.refs_1_), channel_id=1, source_target_pairs={{0,1},{1,0},{2,3},{3,2},{4,5},{5,4},{6,7},{7,6},{8,9},{9,8},{10,11... | collective-permute-start | bytes 5308424 | tf_op jit(solution)/shard_map/ppermute | solution.py:38
  93.2 6.7 %copy-start.2 = (bf16[96,1152]{1,0:T(8,128)(2,1)S(1)}, bf16[96,1152]{1,0:T(8,128)(2,1)}, u32[]{:S(2)}) copy-start(bf16[96,1152]{1,0:T(8,128)(2,1)} %copy-done.1) | copy-start | bytes 663556
  93.3 8.9 %copy-start.4 = (bf16[48,1152]{1,0:T(8,128)(2,1)S(1)}, bf16[48,1152]{1,0:T(8,128)(2,1)}, u32[]{:S(2)}) copy-start(bf16[48,1152]{1,0:T(8,128)(2,1)} %param.6) | copy-start | bytes 331780
  93.3 33.3 %all-to-all-start.1 = ((bf16[16,48,1152]{2,1,0:T(8,128)(2,1)}), bf16[16,48,1152]{2,1,0:T(8,128)(2,1)S(1)}, u32[]{:S(2)}, u32[]{:S(2)}) async-start(bf16[16,48,1152]{2,1,0:T(8,128)(2,1)} %bitcast.11), calls=%async_computation.1 | async-start | bytes 3538944 | tf_op jit(solution)/shard_map/all_to_all | solution.py:261
  99.9 4.6 %collective-permute-start.8 = (bf16[96,1152]{1,0:T(8,128)(2,1)S(1)}, bf16[96,1152]{1,0:T(8,128)(2,1)S(1)}, u32[]{:S(2)}, u32[]{:S(2)}) collective-permute-start(bf16[96,1152]{1,0:T(8,128)(2,1)S(1)} %copy-done.2), channel_id=1, source_target_pairs={{0,1},{1,0},{2,3},{3,2},{4,5},{5,4},{6,7},{7,6},{8,9},{9,8},{10,11... | collective-permute-start | bytes 663560 | tf_op jit(solution)/shard_map/ppermute | solution.py:38

commit v4 on v3

--- a/solution.py
+++ b/solution.py
@@ -7,9 +7,9 @@
 from jax.experimental.pallas import tpu as pltpu
 from jax.sharding import Mesh, PartitionSpec as P
 
-AXES = ("xh", "za", "zb", "y", "xl", "c")
-SIZES = (2, 4, 4, 4, 2, 2)
-LINE = ("za", "zb")
+AXES = ("xh", "zh", "zl", "y", "xl", "c")
+SIZES = (2, 8, 2, 4, 2, 2)
+LINE = ("zh", "zl")
 PLANE = ("xh", "y", "xl")
 RING = ("xh", "xl")
 FSDP = ("xl", "c")
@@ -19,6 +19,7 @@
 TOTAL_ROWS = 24576
 VMEM_BYTES = 18 * 2**20
 BY_COLUMNS = (((1,), (1,)), ((), ()))
+BY_ROWS = (((0,), (0,)), ((), ()))
 
 IN_VMEM = pl.BlockSpec(memory_space=pltpu.VMEM)
 IN_SMEM = pl.BlockSpec(memory_space=pltpu.SMEM)
@@ -206,12 +207,19 @@
     )(*pieces, after)
 
 
-def finish_kernel(parts_ref, projected_ref, out_ref):
+def finish_kernel(from_ref, projected_ref, out_ref, parts_ref, sems):
+    copies = [
+        pltpu.make_async_copy(from_ref.at[k], parts_ref.at[k], sems.at[k])
+        for k in range(parts_ref.shape[0])
+    ]
+    for copy in copies:
+        copy.start()
     projected = projected_ref[...]
     norm = jnp.sqrt(jnp.sum(projected * projected, axis=-1, keepdims=True) + epsilon)
     unit = projected / norm
-    grad = parts_ref[0].astype(jnp.float32)
-    for k in range(1, parts_ref.shape[0]):
+    grad = jnp.zeros(unit.shape, jnp.float32)
+    for k, copy in enumerate(copies):
+        copy.wait()
         grad = grad + parts_ref[k].astype(jnp.float32)
     radial = jnp.sum(unit * grad, axis=-1, keepdims=True)
     out_ref[...] = ((grad - unit * radial) / norm).astype(out_ref.dtype)
@@ -221,15 +229,54 @@
     return pl.pallas_call(
         finish_kernel,
         out_shape=jax.ShapeDtypeStruct(projected.shape, jnp.bfloat16),
-        in_specs=[IN_VMEM, IN_VMEM],
+        in_specs=[ANYWHERE, IN_VMEM],
         out_specs=IN_VMEM,
+        scratch_shapes=[
+            pltpu.VMEM(parts.shape, parts.dtype),
+            pltpu.SemaphoreType.DMA((parts.shape[0],)),
+        ],
         compiler_params=pltpu.CompilerParams(vmem_limit_bytes=VMEM_BYTES // 2),
     )(parts, projected)
 
 
+def last_kernel(columns_ref, group_ref, own_ref, from_ref, feat_ref, to_ref, head_ref, grad_ref, sem, to_sem):
+    head = pltpu.make_async_copy(from_ref, head_ref, sem)
+    head.start()
+    grad_ref[...] = lax.dot_general(
+        columns_ref[...], group_ref[...], BY_ROWS, preferred_element_type=jnp.float32
+    )
+    result = pltpu.make_async_copy(grad_ref, to_ref, to_sem)
+    result.start()
+    head.wait()
+    feat_ref[...] = lax.dot_general(
+        own_ref[...], head_ref[...], BY_COLUMNS, preferred_element_type=jnp.float32
+    ).astype(feat_ref.dtype)
+    result.wait()
+
+
+def last(columns, group_grad, own_grad, head):
+    width = head.shape[0]
+    return pl.pallas_call(
+        last_kernel,
+        out_shape=[
+            jax.ShapeDtypeStruct(own_grad.shape, jnp.bfloat16),
+            jax.ShapeDtypeStruct((columns.shape[1], width), jnp.float32),
+        ],
+        in_specs=[IN_VMEM] * 3 + [ANYWHERE],
+        out_specs=[IN_VMEM, ANYWHERE],
+        scratch_shapes=[
+            pltpu.VMEM(head.shape, jnp.bfloat16),
+            pltpu.VMEM((columns.shape[1], width), jnp.float32),
+            pltpu.SemaphoreType.DMA,
+            pltpu.SemaphoreType.DMA,
+        ],
+        compiler_params=pltpu.CompilerParams(vmem_limit_bytes=VMEM_BYTES),
+    )(columns, group_grad, own_grad, head)
+
+
 def body(features, pictures, head_rows, coldness, offset, weighting):
     rows, width = features.shape
-    xh, za, zb, y, xl, c = (lax.axis_index(a) for a in AXES)
+    xh, zh, zl, y, xl, c = (lax.axis_index(a) for a in AXES)
     plane = 16
     place = (((xh * 4 + y) * 2 + xl) * rows).astype(jnp.int32)
 
@@ -237,23 +284,18 @@
 
     crossed = lax.ppermute(head_rows, "xl", shift(1, 2))
     at = [xl * 2 + c, (1 - xl) * 2 + c, xl * 2 + 1 - c, (1 - xl) * 2 + 1 - c]
-    at += [xh * 4 + y, place, za * rows]
+    at += [xh * 4 + y, place, zh * rows]
     places = jnp.stack([a.astype(jnp.int32) for a in at])
 
     own = unit_rows(pictures)
-    quarter = lax.all_gather(own, "za", axis=0, tiled=True)
-    half = quarter.shape[0] // 2
-    late = [
-        along_z(quarter, 1),
-        along_z(quarter, -1),
-        along_z(quarter[:half], 2),
-        along_z(quarter[half:], -2),
-    ]
+    even = lax.all_gather(own, "zh", axis=0, tiled=True)
+    half = even.shape[0] // 2
+    late = [along_z(even[:half], 1), along_z(even[half:], -1)]
     head_pieces = [head_rows, crossed, other_core(head_rows), other_core(crossed)]
     settings = [setting.reshape(1, 1) for setting in (coldness, offset, weighting)]
     text, head, pair, scalars = project(places, plane_features, settings, head_pieces, 2 * rows)
 
-    line = join([quarter] + late, text)
+    line = join([even] + late, text)
     other_line = other_core(line)
     total = meet(scalars, places, text, [line], own_rows=rows)
     partial = meet(scalars, places, text, [other_line], total, plane_features)
@@ -270,12 +312,8 @@
 
     proj_grad = finish(parts, projected)
     group_grad = lax.all_gather(proj_grad, FSDP, axis=0, tiled=True)
-    proj_grad, _ = lax.optimization_barrier((proj_grad, group_grad))
-    feat_grad = lax.dot_general(proj_grad, head, BY_COLUMNS, preferred_element_type=jnp.float32)
-    head_grad = lax.dot_general(
-        columns, group_grad, (((0,), (0,)), ((), ())), preferred_element_type=jnp.float32
-    )
-    return feat_grad.astype(jnp.bfloat16), head_grad[None]
+    feat_grad, head_grad = last(columns, group_grad, proj_grad, head)
+    return feat_grad, head_grad[None]
 
 
 def solution(mesh):
@@ -284,6 +322,6 @@
         body,
         mesh=fine,
         in_specs=(P(AXES, None), P(AXES, None), P(FSDP, None), P(), P(), P()),
-        out_specs=(P(AXES, None), P(("xh", "za", "zb", "y"), FSDP, None)),
+        out_specs=(P(AXES, None), P(("xh", "zh", "zl", "y"), FSDP, None)),
         check_vma=False,
     )

time: 140 us -> 139 us (level)
  blocking collectives: 33.5 us -> 41.3 us
  starting transfers between devices: 49.1 us -> 41.7 us
  matrix products: 7.15 us -> 0.57 us
  Pallas kernels: 18.2 us -> 21.6 us
  waiting for transfers between devices: 25.6 us -> 27.1 us
    ppermute x4 -> x2, starting transfers between devices: 13.9 us -> 6.48 us  [along_z(): return lax.ppermute(array, LINE, shift(step % 16, 16))]
    all_gather x1, blocking collectives: 25.6 us -> 32.9 us  [body(): even = lax.all_gather(own, 'zh', axis=0, tiled=True)]
    dot_general x2 -> x0, matrix products: 4.83 us -> none  [the longest x1 3.29 us: body(): lax.dot_general(proj_grad, head, BY_COLUMNS, preferred_element_type=jnp.f...]
    pallas_call x0 -> x1, Pallas kernels: none -> 2.4 us  [last(): pl.pallas_call(last_kernel, out_shape=[jax.ShapeDtypeStruct(own_grad.shap...]
    dot_general x1, matrix products: 2.32 us -> 0.57 us  [body(): projected = jnp.dot(features, head, preferred_element_type=jnp.float32)]
    pallas_call x1, Pallas kernels: 0.36 us -> 1.76 us  [finish(): pl.pallas_call(finish_kernel, out_shape=jax.ShapeDtypeStruct(projected.sh...]
    ppermute x4 -> x2, waiting for transfers between devices: 3.66 us -> 3.38 us  [along_z(): return lax.ppermute(array, LINE, shift(step % 16, 16))]
  transfers between devices with their start and end apart: 11 -> 9, of which waited for: 3 -> 4; matrix products, arithmetic and copies ran while one was open for 2% -> 1% of each run, Pallas kernels for 7% -> 7%
where the time goes in v4:
time: 139 us
  starting transfers between devices  41.7 us (30%)
  blocking collectives  41.3 us (30%)
  waiting for transfers between devices  27.1 us (19%)
  Pallas kernels  21.6 us (16%)
  local copies, waits for them, and re-layouts  3.5 us (3%)
  between operations  2.84 us (2%)
    all_gather x1, blocking collectives, body(): even = lax.all_gather(own, 'zh', axis=0, tiled=True)  32.9 us
    all_to_all x1, waiting for transfers between devices, body(): lax.all_to_all(partial, PLANE, 0, 0, tiled=True).reshape(plane, rows, width)  23.2 us
    ppermute x4, starting transfers between devices, other_core(): return lax.ppermute(array, 'c', shift(1, 2))  17.7 us
    pallas_call x2, Pallas kernels, meet(): pl.pallas_call(functools.partial(meet_kernel, count // 2, own_rows, last)...  11 us
    all_gather x1, blocking collectives, body(): group_grad = lax.all_gather(proj_grad, FSDP, axis=0, tiled=True)  8.4 us
    all_to_all x1, starting transfers between devices, body(): lax.all_to_all(jnp.tile(features, (plane, 1)), PLANE, 0, 0, tiled=True)  7.76 us
    all_to_all x1, starting transfers between devices, body(): lax.all_to_all(partial, PLANE, 0, 0, tiled=True).reshape(plane, rows, width)  6.53 us
    ppermute x2, starting transfers between devices, along_z(): return lax.ppermute(array, LINE, shift(step % 16, 16))  6.48 us
  transfers between devices with their start and end apart: 9, of which 4 were waited for; matrix products, arithmetic and copies ran while one was open for 1% of the time, Pallas kernels for 7%

profile of v4, /device:TPU:1, one launch (start us, length us, event | category | flops | bytes accessed | tf_op | source)
XLA Modules:
  0.0 138.7 jit_solution(2697620893216470040)
XLA Ops:
  0.6 2.3 %tile.2 = bf16[16,48,1152]{2,1,0:T(8,128)(2,1)} broadcast(bf16[48,1152]{1,0:T(8,128)(2,1)} %param.6), dimensions={1,2} | broadcast | bytes 1880064 | tf_op jit(solution)/shard_map/tile | solution.py:283
  2.9 7.8 %all-to-all-start = ((bf16[16,48,1152]{2,1,0:T(8,128)(2,1)}), bf16[16,48,1152]{2,1,0:T(8,128)(2,1)}, u32[]{:S(2)}, u32[]{:S(2)}) async-start(bf16[16,48,1152]{2,1,0:T(8,128)(2,1)} %tile.2), calls=%async_computation | async-start | bytes 3538944 | tf_op jit(solution)/shard_map/all_to_all | solution.py:283
  10.7 3.2 %collective-permute-start = (bf16[288,1152]{1,0:T(8,128)(2,1)S(1)}, bf16[288,1152]{1,0:T(8,128)(2,1)S(1)}, u32[]{:S(2)}, u32[]{:S(2)}) collective-permute-start(bf16[288,1152]{1,0:T(8,128)(2,1)S(1)} %copy-done.1), channel_id=1, source_target_pairs={{0,2},{2,0},{1,3},{3,1},{4,6},{6,4},{5,7},{7,5},{8,10},{10,8},{9,1... | collective-permute-start | bytes 1990664 | tf_op jit(solution)/shard_map/ppermute | solution.py:285
  13.9 6.0 %collective-permute-start.1 = (bf16[288,1152]{1,0:T(8,128)(2,1)S(1)}, bf16[288,1152]{1,0:T(8,128)(2,1)S(1)}, u32[]{:S(2)}, u32[]{:S(2)}) collective-permute-start(bf16[288,1152]{1,0:T(8,128)(2,1)S(1)} %copy-done.1), channel_id=1, source_target_pairs={{0,1},{1,0},{2,3},{3,2},{4,5},{5,4},{6,7},{7,6},{8,9},{9,8},{10,11... | collective-permute-start | bytes 1990664 | tf_op jit(solution)/shard_map/ppermute | solution.py:39
  19.9 0.1 shard_map.78
  20.1 32.9 %all_gather.6.refs_0_ = bf16[384,1152]{1,0:T(8,128)(2,1)S(1)} all-gather(bf16[48,1152]{1,0:T(8,128)(2,1)S(1)} %shard_map.78), channel_id=1, replica_groups=mesh['xh'=2,'zh'=8,'zl'=2,'y'=4,'xl'=2,'c'=2] {'zh'}, dimensions={0}, use_global_device_ids=true | all-gather | bytes 995328 | tf_op jit(solution)/shard_map/all_gather | solution.py:291
  52.9 0.0 collective-permute-done.refs_4_
  52.9 6.5 %collective-permute-start.2 = (bf16[288,1152]{1,0:T(8,128)(2,1)S(1)}, bf16[288,1152]{1,0:T(8,128)(2,1)S(1)}, u32[]{:S(2)}, u32[]{:S(2)}) collective-permute-start(bf16[288,1152]{1,0:T(8,128)(2,1)S(1)} %collective-permute-done.refs_4_), channel_id=1, source_target_pairs={{0,1},{1,0},{2,3},{3,2},{4,5},{5,4},{6,7},{7,6},{8,9},{9,8},{10,11... | collective-permute-start | bytes 1990664 | tf_op jit(solution)/shard_map/ppermute | solution.py:39
  59.4 1.0 fusion
  60.4 3.3 %collective-permute-start.4 = (bf16[192,1152]{1,0:T(8,128)(2,1)}, bf16[192,1152]{1,0:T(8,128)(2,1)}, u32[]{:S(2)}, u32[]{:S(2)}) collective-permute-start(bf16[192,1152]{1,0:T(8,128)(2,1)} %get-tuple-element.15), channel_id=1, source_target_pairs={{0,16},{16,32},{32,48},{48,64},{64,80},{80,96},{96,112},{112,128},... | collective-permute-start | bytes 1327112 | tf_op jit(solution)/shard_map/ppermute | solution.py:35
  63.7 3.2 %collective-permute-start.5 = (bf16[192,1152]{1,0:T(8,128)(2,1)}, bf16[192,1152]{1,0:T(8,128)(2,1)}, u32[]{:S(2)}, u32[]{:S(2)}) collective-permute-start(bf16[192,1152]{1,0:T(8,128)(2,1)} %get-tuple-element.14), channel_id=1, source_target_pairs={{0,240},{16,0},{32,16},{48,32},{64,48},{80,64},{96,80},{112,96},{1... | collective-permute-start | bytes 1327112 | tf_op jit(solution)/shard_map/ppermute | solution.py:35
  68.9 0.1 stack.34.place_ref
  68.9 0.0 collective-permute-done.1.refs_5_
  68.9 0.0 collective-permute-done.2.refs_6_
  68.9 0.0 all-to-all-done
  69.0 5.0 %shard_map.77 = (bf16[768,1152]{1,0:T(8,128)(2,1)S(1)}, bf16[1152,1152]{1,0:T(8,128)(2,1)}, bf16[96,1152]{1,0:T(8,128)(2,1)S(1)}, f32[8,128]{1,0:T(8,128)S(1)}) custom-call(s32[7]{0:T(128)S(1)} %stack.34.place_ref, bf16[768,1152]{1,0:T(8,128)(2,1)} %bitcast.7.from_ref.refs_3_, f32[1,1]{1,0:T(1,128)} %bitcast.24.refs_0_, f32[1,1]{1,0:T(1,128)} %bitcast.25.refs_1_, ...), custom_call_target="tpu_custom_call" | custom-call | tf_op jit(solution)/shard_map/pallas_call | solution.py:96
  74.0 1.6 %collective-permute-done.4.refs_1_ = bf16[192,1152]{1,0:T(8,128)(2,1)} collective-permute-done((bf16[192,1152]{1,0:T(8,128)(2,1)}, bf16[192,1152]{1,0:T(8,128)(2,1)}, u32[]{:S(2)}, u32[]{:S(2)}) %collective-permute-start.4) | collective-permute-done | bytes 442400 | tf_op jit(solution)/shard_map/ppermute | solution.py:35
  75.6 1.8 %collective-permute-done.5.refs_2_ = bf16[192,1152]{1,0:T(8,128)(2,1)} collective-permute-done((bf16[192,1152]{1,0:T(8,128)(2,1)}, bf16[192,1152]{1,0:T(8,128)(2,1)}, u32[]{:S(2)}, u32[]{:S(2)}) %collective-permute-start.5) | collective-permute-done | bytes 442400 | tf_op jit(solution)/shard_map/ppermute | solution.py:35
  77.3 1.3 shard_map.79.refs_1_
  78.7 3.0 %collective-permute-start.6 = (bf16[768,1152]{1,0:T(8,128)(2,1)S(1)}, bf16[768,1152]{1,0:T(8,128)(2,1)S(1)}, u32[]{:S(2)}, u32[]{:S(2)}) collective-permute-start(bf16[768,1152]{1,0:T(8,128)(2,1)S(1)} %shard_map.79.refs_1_), channel_id=1, source_target_pairs={{0,1},{1,0},{2,3},{3,2},{4,5},{5,4},{6,7},{7,6},{8,9},{9,8},{10,11... | collective-permute-start | bytes 5308424 | tf_op jit(solution)/shard_map/ppermute | solution.py:39
  81.7 4.9 %shard_map.80.refs_2_ = f32[768,1152]{1,0:T(8,128)S(1)} custom-call(s32[7]{0:T(128)S(1)} %stack.34.place_ref, bf16[768,1152]{1,0:T(8,128)(2,1)S(1)} %get-tuple-element.9.refs_3_.text_ref, f32[8,128]{1,0:T(8,128)S(1)} %get-tuple-element.10.refs_0_, bf16[768,1152]{1,0:T(8,128)(2,1)S(1)} %shard_map.79.refs_1_), custom_call_target="tpu_custom_call" | custom-call | flops 2717908992 | bytes 7077888 | tf_op jit(solution)/shard_map/pallas_call | solution.py:167
  86.7 6.1 %shard_map.81 = bf16[768,1152]{1,0:T(8,128)(2,1)} custom-call(s32[7]{0:T(128)S(1)} %stack.34.place_ref, bf16[768,1152]{1,0:T(8,128)(2,1)S(1)} %get-tuple-element.9.refs_3_.text_ref, f32[8,128]{1,0:T(8,128)S(1)} %get-tuple-element.10.refs_0_, bf16[768,1152]{1,0:T(8,128)(2,1)S(1)} %collective-permute-done.6.refs_1_, ...), custom_call_target="tpu_custom_call", output_to_operand_aliasing={{}: (5, {})} | custom-call | flops 2717908992 | bytes 7077888 | tf_op jit(solution)/shard_map/pallas_call | solution.py:167
  92.8 0.0 copy-start.5
  92.8 6.5 %all-to-all-start.1 = ((bf16[16,48,1152]{2,1,0:T(8,128)(2,1)}), bf16[16,48,1152]{2,1,0:T(8,128)(2,1)}, u32[]{:S(2)}, u32[]{:S(2)}) async-start(bf16[16,48,1152]{2,1,0:T(8,128)(2,1)} %bitcast.16), calls=%async_computation.1 | async-start | bytes 3538944 | tf_op jit(solution)/shard_map/all_to_all | solution.py:303
  99.4 2.2 %collective-permute-start.3 = (bf16[96,1152]{1,0:T(8,128)(2,1)S(1)}, bf16[96,1152]{1,0:T(8,128)(2,1)S(1)}, u32[]{:S(2)}, u32[]{:S(2)}) collective-permute-start(bf16[96,1152]{1,0:T(8,128)(2,1)S(1)} %copy-done.3), channel_id=1, source_target_pairs={{0,1},{1,0},{2,3},{3,2},{4,5},{5,4},{6,7},{7,6},{8,9},{9,8},{10,11... | collective-permute-start | bytes 663560 | tf_op jit(solution)/shard_map/ppermute | solution.py:39
  101.6 0.6 convolution_bitcast_fusion.projected_ref
  102.2 0.6 collective-permute-done.3
  102.8 0.1 constant_dynamic-slice_fusion.columns_ref
  103.0 23.2 %all-to-all-done.1.from_ref = bf16[16,48,1152]{2,1,0:T(8,128)(2,1)} async-done(((bf16[16,48,1152]{2,1,0:T(8,128)(2,1)}), bf16[16,48,1152]{2,1,0:T(8,128)(2,1)}, u32[]{:S(2)}, u32[]{:S(2)}) %all-to-all-start.1) | async-done | bytes 1769504 | tf_op jit(solution)/shard_map/all_to_all | solution.py:303
  126.1 1.8 %shard_map.82.own_ref = bf16[48,1152]{1,0:T(8,128)(2,1)S(1)} custom-call(bf16[16,48,1152]{2,1,0:T(8,128)(2,1)} %all-to-all-done.1.from_ref, f32[48,1152]{1,0:T(8,128)S(1)} %convolution_bitcast_fusion.projected_ref), custom_call_target="tpu_custom_call" | custom-call | tf_op jit(solution)/shard_map/pallas_call | solution.py:229
  127.9 8.4 %all_gather.7.group_ref = bf16[192,1152]{1,0:T(8,128)(2,1)S(1)} all-gather(bf16[48,1152]{1,0:T(8,128)(2,1)S(1)} %shard_map.82.own_ref), channel_id=1, replica_groups=mesh['xh'=2,'zh'=8,'zl'=2,'y'=4,'xl'=2,'c'=2] {'xl','c'}, dimensions={0}, use_global_device_ids=true | all-gather | bytes 552960 | tf_op jit(solution)/shard_map/all_gather | solution.py:314
  136.3 2.4 %shard_map.83 = (bf16[48,1152]{1,0:T(8,128)(2,1)}, f32[288,1152]{1,0:T(8,128)}) custom-call(bf16[192,288]{1,0:T(8,128)(2,1)S(1)} %constant_dynamic-slice_fusion.columns_ref, bf16[192,1152]{1,0:T(8,128)(2,1)S(1)} %all_gather.7.group_ref, bf16[48,1152]{1,0:T(8,128)(2,1)S(1)} %shard_map.82.own_ref, bf16[1152,1152]{1,0:T(8,128)(2,1)S(1)} %copy-done), custom_call_target="tpu_custom_call" | custom-call | tf_op jit(solution)/shard_map/pallas_call | solution.py:259
  (14 shorter events, 0.1 us)
Async XLA Ops:
  2.9 7.8 %copy-start.1 = (bf16[288,1152]{1,0:T(8,128)(2,1)S(1)}, bf16[288,1152]{1,0:T(8,128)(2,1)}, u32[]{:S(2)}) copy-start(bf16[288,1152]{1,0:T(8,128)(2,1)} %refs_3_.1) | copy-start | bytes 1990660
  2.9 17.0 %copy-start.4 = (bf16[48,1152]{1,0:T(8,128)(2,1)S(1)}, bf16[48,1152]{1,0:T(8,128)(2,1)}, u32[]{:S(2)}) copy-start(bf16[48,1152]{1,0:T(8,128)(2,1)} %rows_ref.1) | copy-start | bytes 331780
  2.9 66.0 %all-to-all-start = ((bf16[16,48,1152]{2,1,0:T(8,128)(2,1)}), bf16[16,48,1152]{2,1,0:T(8,128)(2,1)}, u32[]{:S(2)}, u32[]{:S(2)}) async-start(bf16[16,48,1152]{2,1,0:T(8,128)(2,1)} %tile.2), calls=%async_computation | async-start | bytes 3538944 | tf_op jit(solution)/shard_map/all_to_all | solution.py:283
  10.7 42.2 %collective-permute-start = (bf16[288,1152]{1,0:T(8,128)(2,1)S(1)}, bf16[288,1152]{1,0:T(8,128)(2,1)S(1)}, u32[]{:S(2)}, u32[]{:S(2)}) collective-permute-start(bf16[288,1152]{1,0:T(8,128)(2,1)S(1)} %copy-done.1), channel_id=1, source_target_pairs={{0,2},{2,0},{1,3},{3,1},{4,6},{6,4},{5,7},{7,5},{8,10},{10,8},{9,1... | collective-permute-start | bytes 1990664 | tf_op jit(solution)/shard_map/ppermute | solution.py:285
  13.9 55.0 %collective-permute-start.1 = (bf16[288,1152]{1,0:T(8,128)(2,1)S(1)}, bf16[288,1152]{1,0:T(8,128)(2,1)S(1)}, u32[]{:S(2)}, u32[]{:S(2)}) collective-permute-start(bf16[288,1152]{1,0:T(8,128)(2,1)S(1)} %copy-done.1), channel_id=1, source_target_pairs={{0,1},{1,0},{2,3},{3,2},{4,5},{5,4},{6,7},{7,6},{8,9},{9,8},{10,11... | collective-permute-start | bytes 1990664 | tf_op jit(solution)/shard_map/ppermute | solution.py:39
  52.9 16.0 %collective-permute-start.2 = (bf16[288,1152]{1,0:T(8,128)(2,1)S(1)}, bf16[288,1152]{1,0:T(8,128)(2,1)S(1)}, u32[]{:S(2)}, u32[]{:S(2)}) collective-permute-start(bf16[288,1152]{1,0:T(8,128)(2,1)S(1)} %collective-permute-done.refs_4_), channel_id=1, source_target_pairs={{0,1},{1,0},{2,3},{3,2},{4,5},{5,4},{6,7},{7,6},{8,9},{9,8},{10,11... | collective-permute-start | bytes 1990664 | tf_op jit(solution)/shard_map/ppermute | solution.py:39
  60.4 15.2 %collective-permute-start.4 = (bf16[192,1152]{1,0:T(8,128)(2,1)}, bf16[192,1152]{1,0:T(8,128)(2,1)}, u32[]{:S(2)}, u32[]{:S(2)}) collective-permute-start(bf16[192,1152]{1,0:T(8,128)(2,1)} %get-tuple-element.15), channel_id=1, source_target_pairs={{0,16},{16,32},{32,48},{48,64},{64,80},{80,96},{96,112},{112,128},... | collective-permute-start | bytes 1327112 | tf_op jit(solution)/shard_map/ppermute | solution.py:35
  63.7 13.7 %collective-permute-start.5 = (bf16[192,1152]{1,0:T(8,128)(2,1)}, bf16[192,1152]{1,0:T(8,128)(2,1)}, u32[]{:S(2)}, u32[]{:S(2)}) collective-permute-start(bf16[192,1152]{1,0:T(8,128)(2,1)} %get-tuple-element.14), channel_id=1, source_target_pairs={{0,240},{16,0},{32,16},{48,32},{64,48},{80,64},{96,80},{112,96},{1... | collective-permute-start | bytes 1327112 | tf_op jit(solution)/shard_map/ppermute | solution.py:35
  74.0 4.8 %copy-start.2 = (bf16[96,1152]{1,0:T(8,128)(2,1)}, bf16[96,1152]{1,0:T(8,128)(2,1)S(1)}, u32[]{:S(2)}) copy-start(bf16[96,1152]{1,0:T(8,128)(2,1)S(1)} %get-tuple-element.8) | copy-start | bytes 663556
  78.7 7.9 %collective-permute-start.6 = (bf16[768,1152]{1,0:T(8,128)(2,1)S(1)}, bf16[768,1152]{1,0:T(8,128)(2,1)S(1)}, u32[]{:S(2)}, u32[]{:S(2)}) collective-permute-start(bf16[768,1152]{1,0:T(8,128)(2,1)S(1)} %shard_map.79.refs_1_), channel_id=1, source_target_pairs={{0,1},{1,0},{2,3},{3,2},{4,5},{5,4},{6,7},{7,6},{8,9},{9,8},{10,11... | collective-permute-start | bytes 5308424 | tf_op jit(solution)/shard_map/ppermute | solution.py:39
  92.8 6.6 %copy-start.3 = (bf16[96,1152]{1,0:T(8,128)(2,1)S(1)}, bf16[96,1152]{1,0:T(8,128)(2,1)}, u32[]{:S(2)}) copy-start(bf16[96,1152]{1,0:T(8,128)(2,1)} %copy-done.2) | copy-start | bytes 663556
  92.8 8.8 %copy-start = (bf16[1152,1152]{1,0:T(8,128)(2,1)S(1)}, bf16[1152,1152]{1,0:T(8,128)(2,1)}, u32[]{:S(2)}) copy-start(bf16[1152,1152]{1,0:T(8,128)(2,1)} %get-tuple-element.11.from_ref) | copy-start | bytes 7962628
  92.8 8.8 %copy-start.5 = (bf16[48,1152]{1,0:T(8,128)(2,1)S(1)}, bf16[48,1152]{1,0:T(8,128)(2,1)}, u32[]{:S(2)}) copy-start(bf16[48,1152]{1,0:T(8,128)(2,1)} %param.6) | copy-start | bytes 331780
  92.8 33.3 %all-to-all-start.1 = ((bf16[16,48,1152]{2,1,0:T(8,128)(2,1)}), bf16[16,48,1152]{2,1,0:T(8,128)(2,1)}, u32[]{:S(2)}, u32[]{:S(2)}) async-start(bf16[16,48,1152]{2,1,0:T(8,128)(2,1)} %bitcast.16), calls=%async_computation.1 | async-start | bytes 3538944 | tf_op jit(solution)/shard_map/all_to_all | solution.py:303
  99.4 3.4 %collective-permute-start.3 = (bf16[96,1152]{1,0:T(8,128)(2,1)S(1)}, bf16[96,1152]{1,0:T(8,128)(2,1)S(1)}, u32[]{:S(2)}, u32[]{:S(2)}) collective-permute-start(bf16[96,1152]{1,0:T(8,128)(2,1)S(1)} %copy-done.3), channel_id=1, source_target_pairs={{0,1},{1,0},{2,3},{3,2},{4,5},{5,4},{6,7},{7,6},{8,9},{9,8},{10,11... | collective-permute-start | bytes 663560 | tf_op jit(solution)/shard_map/ppermute | solution.py:39

commit v5 on v4

--- a/solution.py
+++ b/solution.py
@@ -295,9 +295,9 @@
     settings = [setting.reshape(1, 1) for setting in (coldness, offset, weighting)]
     text, head, pair, scalars = project(places, plane_features, settings, head_pieces, 2 * rows)
 
-    line = join([even] + late, text)
-    other_line = other_core(line)
-    total = meet(scalars, places, text, [line], own_rows=rows)
+    total = meet(scalars, places, text, [even], own_rows=rows)
+    other_line = other_core(join([even] + late, total))
+    total = meet(scalars, places, text, late, total)
     partial = meet(scalars, places, text, [other_line], total, plane_features)
 
     parts = lax.all_to_all(partial, PLANE, 0, 0, tiled=True).reshape(plane, rows, width)

time: 139 us -> 137 us (0.986)
  waiting for transfers between devices: 27.1 us -> 23.8 us
  Pallas kernels: 21.6 us -> 23.8 us
    ppermute x2, waiting for transfers between devices: 3.38 us -> 0.01 us  [along_z(): return lax.ppermute(array, LINE, shift(step % 16, 16))]
    pallas_call x2 -> x3, Pallas kernels: 11 us -> 13.4 us  [meet(): pl.pallas_call(functools.partial(meet_kernel, count // 2, own_rows, last)...]
  transfers between devices with their start and end apart: 9 -> 9, of which waited for: 4 -> 2; matrix products, arithmetic and copies ran while one was open for 1% -> 1% of each run, Pallas kernels for 7% -> 9%
where the time goes in v5:
time: 137 us
  blocking collectives  41.3 us (30%)
  starting transfers between devices  41.1 us (30%)
  Pallas kernels  23.8 us (17%)
  waiting for transfers between devices  23.8 us (17%)
  local copies, waits for them, and re-layouts  3.49 us (3%)
  between operations  2.83 us (2%)
    all_gather x1, blocking collectives, body(): even = lax.all_gather(own, 'zh', axis=0, tiled=True)  32.8 us
    all_to_all x1, waiting for transfers between devices, body(): lax.all_to_all(partial, PLANE, 0, 0, tiled=True).reshape(plane, rows, width)  23.2 us
    ppermute x4, starting transfers between devices, other_core(): return lax.ppermute(array, 'c', shift(1, 2))  17.2 us
    pallas_call x3, Pallas kernels, meet(): pl.pallas_call(functools.partial(meet_kernel, count // 2, own_rows, last)...  13.4 us
    all_gather x1, blocking collectives, body(): group_grad = lax.all_gather(proj_grad, FSDP, axis=0, tiled=True)  8.43 us
    all_to_all x1, starting transfers between devices, body(): lax.all_to_all(jnp.tile(features, (plane, 1)), PLANE, 0, 0, tiled=True)  7.76 us
    ppermute x2, starting transfers between devices, along_z(): return lax.ppermute(array, LINE, shift(step % 16, 16))  6.48 us
    all_to_all x1, starting transfers between devices, body(): lax.all_to_all(partial, PLANE, 0, 0, tiled=True).reshape(plane, rows, width)  6.45 us
  transfers between devices with their start and end apart: 9, of which 2 were waited for; matrix products, arithmetic and copies ran while one was open for 1% of the time, Pallas kernels for 9%

profile of v5, /device:TPU:1, one launch (start us, length us, event | category | flops | bytes accessed | tf_op | source)
XLA Modules:
  0.0 136.9 jit_solution(2579742612102276116)
XLA Ops:
  0.6 2.3 %tile.2 = bf16[16,48,1152]{2,1,0:T(8,128)(2,1)} broadcast(bf16[48,1152]{1,0:T(8,128)(2,1)} %param.6), dimensions={1,2} | broadcast | bytes 1880064 | tf_op jit(solution)/shard_map/tile | solution.py:283
  2.9 7.8 %all-to-all-start = ((bf16[16,48,1152]{2,1,0:T(8,128)(2,1)}), bf16[16,48,1152]{2,1,0:T(8,128)(2,1)}, u32[]{:S(2)}, u32[]{:S(2)}) async-start(bf16[16,48,1152]{2,1,0:T(8,128)(2,1)} %tile.2), calls=%async_computation | async-start | bytes 3538944 | tf_op jit(solution)/shard_map/all_to_all | solution.py:283
  10.7 3.2 %collective-permute-start = (bf16[288,1152]{1,0:T(8,128)(2,1)S(1)}, bf16[288,1152]{1,0:T(8,128)(2,1)S(1)}, u32[]{:S(2)}, u32[]{:S(2)}) collective-permute-start(bf16[288,1152]{1,0:T(8,128)(2,1)S(1)} %copy-done.1), channel_id=1, source_target_pairs={{0,2},{2,0},{1,3},{3,1},{4,6},{6,4},{5,7},{7,5},{8,10},{10,8},{9,1... | collective-permute-start | bytes 1990664 | tf_op jit(solution)/shard_map/ppermute | solution.py:285
  13.9 6.0 %collective-permute-start.1 = (bf16[288,1152]{1,0:T(8,128)(2,1)S(1)}, bf16[288,1152]{1,0:T(8,128)(2,1)}, u32[]{:S(2)}, u32[]{:S(2)}) collective-permute-start(bf16[288,1152]{1,0:T(8,128)(2,1)S(1)} %copy-done.1), channel_id=1, source_target_pairs={{0,1},{1,0},{2,3},{3,2},{4,5},{5,4},{6,7},{7,6},{8,9},{9,8},{10,11... | collective-permute-start | bytes 1990664 | tf_op jit(solution)/shard_map/ppermute | solution.py:39
  20.0 0.1 shard_map.78
  20.1 32.8 %all_gather.6.refs_1_.refs_0_ = bf16[384,1152]{1,0:T(8,128)(2,1)S(1)} all-gather(bf16[48,1152]{1,0:T(8,128)(2,1)S(1)} %shard_map.78), channel_id=1, replica_groups=mesh['xh'=2,'zh'=8,'zl'=2,'y'=4,'xl'=2,'c'=2] {'zh'}, dimensions={0}, use_global_device_ids=true | all-gather | bytes 995328 | tf_op jit(solution)/shard_map/all_gather | solution.py:291
  52.9 0.0 collective-permute-done.refs_4_
  52.9 6.5 %collective-permute-start.2 = (bf16[288,1152]{1,0:T(8,128)(2,1)S(1)}, bf16[288,1152]{1,0:T(8,128)(2,1)}, u32[]{:S(2)}, u32[]{:S(2)}) collective-permute-start(bf16[288,1152]{1,0:T(8,128)(2,1)S(1)} %collective-permute-done.refs_4_), channel_id=1, source_target_pairs={{0,1},{1,0},{2,3},{3,2},{4,5},{5,4},{6,7},{7,6},{8,9},{9,8},{10,11... | collective-permute-start | bytes 1990664 | tf_op jit(solution)/shard_map/ppermute | solution.py:39
  59.4 1.0 fusion
  60.4 3.3 %collective-permute-start.4 = (bf16[192,1152]{1,0:T(8,128)(2,1)}, bf16[192,1152]{1,0:T(8,128)(2,1)S(1)}, u32[]{:S(2)}, u32[]{:S(2)}) collective-permute-start(bf16[192,1152]{1,0:T(8,128)(2,1)} %get-tuple-element.15), channel_id=1, source_target_pairs={{0,16},{16,32},{32,48},{48,64},{64,80},{80,96},{96,112},{112,128},... | collective-permute-start | bytes 1327112 | tf_op jit(solution)/shard_map/ppermute | solution.py:35
  63.7 3.2 %collective-permute-start.5 = (bf16[192,1152]{1,0:T(8,128)(2,1)}, bf16[192,1152]{1,0:T(8,128)(2,1)S(1)}, u32[]{:S(2)}, u32[]{:S(2)}) collective-permute-start(bf16[192,1152]{1,0:T(8,128)(2,1)} %get-tuple-element.14), channel_id=1, source_target_pairs={{0,240},{16,0},{32,16},{48,32},{64,48},{80,64},{96,80},{112,96},{1... | collective-permute-start | bytes 1327112 | tf_op jit(solution)/shard_map/ppermute | solution.py:35
  68.9 0.1 stack.34.place_ref
  68.9 0.0 collective-permute-done.1.refs_5_
  68.9 0.0 collective-permute-done.2.refs_6_
  69.0 5.4 %shard_map.77 = (bf16[768,1152]{1,0:T(8,128)(2,1)S(1)}, bf16[1152,1152]{1,0:T(8,128)(2,1)}, bf16[96,1152]{1,0:T(8,128)(2,1)S(1)}, f32[8,128]{1,0:T(8,128)S(1)}) custom-call(s32[7]{0:T(128)S(1)} %stack.34.place_ref, bf16[768,1152]{1,0:T(8,128)(2,1)} %bitcast.7.from_ref.refs_3_, f32[1,1]{1,0:T(1,128)} %bitcast.24.refs_0_, f32[1,1]{1,0:T(1,128)} %bitcast.25.refs_1_, ...), custom_call_target="tpu_custom_call" | custom-call | tf_op jit(solution)/shard_map/pallas_call | solution.py:96
  74.4 3.6 %shard_map.79.refs_3_ = f32[768,1152]{1,0:T(8,128)S(1)} custom-call(s32[7]{0:T(128)S(1)} %stack.34.place_ref, bf16[768,1152]{1,0:T(8,128)(2,1)S(1)} %get-tuple-element.9.text_ref, f32[8,128]{1,0:T(8,128)S(1)} %get-tuple-element.10.refs_0_, bf16[384,1152]{1,0:T(8,128)(2,1)S(1)} %all_gather.6.refs_1_.refs_0_), custom_call_target="tpu_custom_call" | custom-call | flops 1358954496 | bytes 6193152 | tf_op jit(solution)/shard_map/pallas_call | solution.py:167
  78.0 0.0 collective-permute-done.5.refs_2_
  78.0 0.7 shard_map.80
  78.7 2.5 %collective-permute-start.6 = (bf16[768,1152]{1,0:T(8,128)(2,1)S(1)}, bf16[768,1152]{1,0:T(8,128)(2,1)S(1)}, u32[]{:S(2)}, u32[]{:S(2)}) collective-permute-start(bf16[768,1152]{1,0:T(8,128)(2,1)S(1)} %shard_map.80), channel_id=1, source_target_pairs={{0,1},{1,0},{2,3},{3,2},{4,5},{5,4},{6,7},{7,6},{8,9},{9,8},{10,11... | collective-permute-start | bytes 5308424 | tf_op jit(solution)/shard_map/ppermute | solution.py:39
  81.2 3.7 %shard_map.81.refs_2_ = f32[768,1152]{1,0:T(8,128)S(1)} custom-call(s32[7]{0:T(128)S(1)} %stack.34.place_ref, bf16[768,1152]{1,0:T(8,128)(2,1)S(1)} %get-tuple-element.9.text_ref, f32[8,128]{1,0:T(8,128)S(1)} %get-tuple-element.10.refs_0_, bf16[192,1152]{1,0:T(8,128)(2,1)S(1)} %collective-permute-done.4.refs_1_, ...), custom_call_target="tpu_custom_call" | custom-call | flops 1358954496 | bytes 6193152 | tf_op jit(solution)/shard_map/pallas_call | solution.py:167
  84.9 0.0 collective-permute-done.6.refs_1_
  84.9 6.1 %shard_map.82 = bf16[768,1152]{1,0:T(8,128)(2,1)} custom-call(s32[7]{0:T(128)S(1)} %stack.34.place_ref, bf16[768,1152]{1,0:T(8,128)(2,1)S(1)} %get-tuple-element.9.text_ref, f32[8,128]{1,0:T(8,128)S(1)} %get-tuple-element.10.refs_0_, bf16[768,1152]{1,0:T(8,128)(2,1)S(1)} %collective-permute-done.6.refs_1_, ...), custom_call_target="tpu_custom_call", output_to_operand_aliasing={{}: (5, {})} | custom-call | flops 2717908992 | bytes 7077888 | tf_op jit(solution)/shard_map/pallas_call | solution.py:167
  91.0 0.0 copy-start.3
  91.1 6.5 %all-to-all-start.1 = ((bf16[16,48,1152]{2,1,0:T(8,128)(2,1)}), bf16[16,48,1152]{2,1,0:T(8,128)(2,1)}, u32[]{:S(2)}, u32[]{:S(2)}) async-start(bf16[16,48,1152]{2,1,0:T(8,128)(2,1)} %bitcast.16), calls=%async_computation.1 | async-start | bytes 3538944 | tf_op jit(solution)/shard_map/all_to_all | solution.py:303
  97.5 2.2 %collective-permute-start.3 = (bf16[96,1152]{1,0:T(8,128)(2,1)S(1)}, bf16[96,1152]{1,0:T(8,128)(2,1)S(1)}, u32[]{:S(2)}, u32[]{:S(2)}) collective-permute-start(bf16[96,1152]{1,0:T(8,128)(2,1)S(1)} %get-tuple-element.8), channel_id=1, source_target_pairs={{0,1},{1,0},{2,3},{3,2},{4,5},{5,4},{6,7},{7,6},{8,9},{9,8},{10,11... | collective-permute-start | bytes 663560 | tf_op jit(solution)/shard_map/ppermute | solution.py:39
  99.8 0.6 convolution_bitcast_fusion.projected_ref
  100.3 0.6 collective-permute-done.3
  101.0 0.1 constant_dynamic-slice_fusion.columns_ref
  101.1 23.2 %all-to-all-done.1.from_ref = bf16[16,48,1152]{2,1,0:T(8,128)(2,1)} async-done(((bf16[16,48,1152]{2,1,0:T(8,128)(2,1)}), bf16[16,48,1152]{2,1,0:T(8,128)(2,1)}, u32[]{:S(2)}, u32[]{:S(2)}) %all-to-all-start.1) | async-done | bytes 1769504 | tf_op jit(solution)/shard_map/all_to_all | solution.py:303
  124.3 1.8 %shard_map.83.own_ref = bf16[48,1152]{1,0:T(8,128)(2,1)S(1)} custom-call(bf16[16,48,1152]{2,1,0:T(8,128)(2,1)} %all-to-all-done.1.from_ref, f32[48,1152]{1,0:T(8,128)S(1)} %convolution_bitcast_fusion.projected_ref), custom_call_target="tpu_custom_call" | custom-call | tf_op jit(solution)/shard_map/pallas_call | solution.py:229
  126.1 8.4 %all_gather.7.group_ref = bf16[192,1152]{1,0:T(8,128)(2,1)S(1)} all-gather(bf16[48,1152]{1,0:T(8,128)(2,1)S(1)} %shard_map.83.own_ref), channel_id=1, replica_groups=mesh['xh'=2,'zh'=8,'zl'=2,'y'=4,'xl'=2,'c'=2] {'xl','c'}, dimensions={0}, use_global_device_ids=true | all-gather | bytes 552960 | tf_op jit(solution)/shard_map/all_gather | solution.py:314
  134.5 2.4 %shard_map.84 = (bf16[48,1152]{1,0:T(8,128)(2,1)}, f32[288,1152]{1,0:T(8,128)}) custom-call(bf16[192,288]{1,0:T(8,128)(2,1)S(1)} %constant_dynamic-slice_fusion.columns_ref, bf16[192,1152]{1,0:T(8,128)(2,1)S(1)} %all_gather.7.group_ref, bf16[48,1152]{1,0:T(8,128)(2,1)S(1)} %shard_map.83.own_ref, bf16[1152,1152]{1,0:T(8,128)(2,1)S(1)} %copy-done), custom_call_target="tpu_custom_call" | custom-call | tf_op jit(solution)/shard_map/pallas_call | solution.py:259
  (11 shorter events, 0.1 us)
Async XLA Ops:
  2.9 7.8 %copy-start.1 = (bf16[288,1152]{1,0:T(8,128)(2,1)S(1)}, bf16[288,1152]{1,0:T(8,128)(2,1)}, u32[]{:S(2)}) copy-start(bf16[288,1152]{1,0:T(8,128)(2,1)} %refs_3_.1) | copy-start | bytes 1990660
  2.9 17.0 %copy-start.2 = (bf16[48,1152]{1,0:T(8,128)(2,1)S(1)}, bf16[48,1152]{1,0:T(8,128)(2,1)}, u32[]{:S(2)}) copy-start(bf16[48,1152]{1,0:T(8,128)(2,1)} %rows_ref.1) | copy-start | bytes 331780
  2.9 66.0 %all-to-all-start = ((bf16[16,48,1152]{2,1,0:T(8,128)(2,1)}), bf16[16,48,1152]{2,1,0:T(8,128)(2,1)}, u32[]{:S(2)}, u32[]{:S(2)}) async-start(bf16[16,48,1152]{2,1,0:T(8,128)(2,1)} %tile.2), calls=%async_computation | async-start | bytes 3538944 | tf_op jit(solution)/shard_map/all_to_all | solution.py:283
  10.7 42.2 %collective-permute-start = (bf16[288,1152]{1,0:T(8,128)(2,1)S(1)}, bf16[288,1152]{1,0:T(8,128)(2,1)S(1)}, u32[]{:S(2)}, u32[]{:S(2)}) collective-permute-start(bf16[288,1152]{1,0:T(8,128)(2,1)S(1)} %copy-done.1), channel_id=1, source_target_pairs={{0,2},{2,0},{1,3},{3,1},{4,6},{6,4},{5,7},{7,5},{8,10},{10,8},{9,1... | collective-permute-start | bytes 1990664 | tf_op jit(solution)/shard_map/ppermute | solution.py:285
  13.9 55.0 %collective-permute-start.1 = (bf16[288,1152]{1,0:T(8,128)(2,1)S(1)}, bf16[288,1152]{1,0:T(8,128)(2,1)}, u32[]{:S(2)}, u32[]{:S(2)}) collective-permute-start(bf16[288,1152]{1,0:T(8,128)(2,1)S(1)} %copy-done.1), channel_id=1, source_target_pairs={{0,1},{1,0},{2,3},{3,2},{4,5},{5,4},{6,7},{7,6},{8,9},{9,8},{10,11... | collective-permute-start | bytes 1990664 | tf_op jit(solution)/shard_map/ppermute | solution.py:39
  52.9 16.0 %collective-permute-start.2 = (bf16[288,1152]{1,0:T(8,128)(2,1)S(1)}, bf16[288,1152]{1,0:T(8,128)(2,1)}, u32[]{:S(2)}, u32[]{:S(2)}) collective-permute-start(bf16[288,1152]{1,0:T(8,128)(2,1)S(1)} %collective-permute-done.refs_4_), channel_id=1, source_target_pairs={{0,1},{1,0},{2,3},{3,2},{4,5},{5,4},{6,7},{7,6},{8,9},{9,8},{10,11... | collective-permute-start | bytes 1990664 | tf_op jit(solution)/shard_map/ppermute | solution.py:39
  60.4 17.6 %collective-permute-start.4 = (bf16[192,1152]{1,0:T(8,128)(2,1)}, bf16[192,1152]{1,0:T(8,128)(2,1)S(1)}, u32[]{:S(2)}, u32[]{:S(2)}) collective-permute-start(bf16[192,1152]{1,0:T(8,128)(2,1)} %get-tuple-element.15), channel_id=1, source_target_pairs={{0,16},{16,32},{32,48},{48,64},{64,80},{80,96},{96,112},{112,128},... | collective-permute-start | bytes 1327112 | tf_op jit(solution)/shard_map/ppermute | solution.py:35
  63.7 14.3 %collective-permute-start.5 = (bf16[192,1152]{1,0:T(8,128)(2,1)}, bf16[192,1152]{1,0:T(8,128)(2,1)S(1)}, u32[]{:S(2)}, u32[]{:S(2)}) collective-permute-start(bf16[192,1152]{1,0:T(8,128)(2,1)} %get-tuple-element.14), channel_id=1, source_target_pairs={{0,240},{16,0},{32,16},{48,32},{64,48},{80,64},{96,80},{112,96},{1... | collective-permute-start | bytes 1327112 | tf_op jit(solution)/shard_map/ppermute | solution.py:35
  78.7 6.2 %collective-permute-start.6 = (bf16[768,1152]{1,0:T(8,128)(2,1)S(1)}, bf16[768,1152]{1,0:T(8,128)(2,1)S(1)}, u32[]{:S(2)}, u32[]{:S(2)}) collective-permute-start(bf16[768,1152]{1,0:T(8,128)(2,1)S(1)} %shard_map.80), channel_id=1, source_target_pairs={{0,1},{1,0},{2,3},{3,2},{4,5},{5,4},{6,7},{7,6},{8,9},{9,8},{10,11... | collective-permute-start | bytes 5308424 | tf_op jit(solution)/shard_map/ppermute | solution.py:39
  91.0 8.7 %copy-start = (bf16[1152,1152]{1,0:T(8,128)(2,1)S(1)}, bf16[1152,1152]{1,0:T(8,128)(2,1)}, u32[]{:S(2)}) copy-start(bf16[1152,1152]{1,0:T(8,128)(2,1)} %get-tuple-element.11.from_ref) | copy-start | bytes 7962628
  91.0 8.7 %copy-start.3 = (bf16[48,1152]{1,0:T(8,128)(2,1)S(1)}, bf16[48,1152]{1,0:T(8,128)(2,1)}, u32[]{:S(2)}) copy-start(bf16[48,1152]{1,0:T(8,128)(2,1)} %param.6) | copy-start | bytes 331780
  91.1 33.3 %all-to-all-start.1 = ((bf16[16,48,1152]{2,1,0:T(8,128)(2,1)}), bf16[16,48,1152]{2,1,0:T(8,128)(2,1)}, u32[]{:S(2)}, u32[]{:S(2)}) async-start(bf16[16,48,1152]{2,1,0:T(8,128)(2,1)} %bitcast.16), calls=%async_computation.1 | async-start | bytes 3538944 | tf_op jit(solution)/shard_map/all_to_all | solution.py:303
  97.5 3.4 %collective-permute-start.3 = (bf16[96,1152]{1,0:T(8,128)(2,1)S(1)}, bf16[96,1152]{1,0:T(8,128)(2,1)S(1)}, u32[]{:S(2)}, u32[]{:S(2)}) collective-permute-start(bf16[96,1152]{1,0:T(8,128)(2,1)S(1)} %get-tuple-element.8), channel_id=1, source_target_pairs={{0,1},{1,0},{2,3},{3,2},{4,5},{5,4},{6,7},{7,6},{8,9},{9,8},{10,11... | collective-permute-start | bytes 663560 | tf_op jit(solution)/shard_map/ppermute | solution.py:39

commit v6 on v5

--- a/solution.py
+++ b/solution.py
@@ -165,7 +165,7 @@
     last = into is not None
     given = [a for a in (total, into) if a is not None]
     return pl.pallas_call(
-        functools.partial(meet_kernel, count // 2, own_rows, last),
+        functools.partial(meet_kernel, count // 2 if last else count, own_rows, last),
         out_shape=jax.ShapeDtypeStruct((count, width), jnp.bfloat16 if last else jnp.float32),
         in_specs=[IN_SMEM, IN_VMEM]
         + [IN_VMEM]

time: 137 us -> 136 us (level)
  no operation moved by 1% of the time
where the time goes in v6:
time: 136 us; the launch traced here: 135 us
  starting transfers between devices  41.8 us (31%)
  blocking collectives  40.4 us (30%)
  waiting for transfers between devices  23.2 us (17%)
  Pallas kernels  22.8 us (17%)
  local copies, waits for them, and re-layouts  3.49 us (3%)
  between operations  2.83 us (2%)
    all_gather x1, blocking collectives, body(): even = lax.all_gather(own, 'zh', axis=0, tiled=True)  32.8 us
    all_to_all x1, waiting for transfers between devices, body(): lax.all_to_all(partial, PLANE, 0, 0, tiled=True).reshape(plane, rows, width)  22.7 us
    ppermute x4, starting transfers between devices, other_core(): return lax.ppermute(array, 'c', shift(1, 2))  17.8 us
    pallas_call x3, Pallas kernels, meet(): pl.pallas_call(functools.partial(meet_kernel, count // 2 if last else cou...  12.4 us
    all_to_all x1, starting transfers between devices, body(): lax.all_to_all(jnp.tile(features, (plane, 1)), PLANE, 0, 0, tiled=True)  7.76 us
    all_gather x1, blocking collectives, body(): group_grad = lax.all_gather(proj_grad, FSDP, axis=0, tiled=True)  7.54 us
    all_to_all x1, starting transfers between devices, body(): lax.all_to_all(partial, PLANE, 0, 0, tiled=True).reshape(plane, rows, width)  6.53 us
    ppermute x2, starting transfers between devices, along_z(): return lax.ppermute(array, LINE, shift(step % 16, 16))  6.48 us
  transfers between devices with their start and end apart: 9, of which 2 were waited for; matrix products, arithmetic and copies ran while one was open for 1% of the time, Pallas kernels for 9%

profile of v6, /device:TPU:1, one launch (start us, length us, event | category | flops | bytes accessed | tf_op | source)
XLA Modules:
  0.0 135.2 jit_solution(17898312326093517200)
XLA Ops:
  0.6 2.3 %tile.2 = bf16[16,48,1152]{2,1,0:T(8,128)(2,1)} broadcast(bf16[48,1152]{1,0:T(8,128)(2,1)} %param.6), dimensions={1,2} | broadcast | bytes 1880064 | tf_op jit(solution)/shard_map/tile | solution.py:283
  2.9 7.8 %all-to-all-start = ((bf16[16,48,1152]{2,1,0:T(8,128)(2,1)}), bf16[16,48,1152]{2,1,0:T(8,128)(2,1)}, u32[]{:S(2)}, u32[]{:S(2)}) async-start(bf16[16,48,1152]{2,1,0:T(8,128)(2,1)} %tile.2), calls=%async_computation | async-start | bytes 3538944 | tf_op jit(solution)/shard_map/all_to_all | solution.py:283
  10.7 3.2 %collective-permute-start = (bf16[288,1152]{1,0:T(8,128)(2,1)S(1)}, bf16[288,1152]{1,0:T(8,128)(2,1)S(1)}, u32[]{:S(2)}, u32[]{:S(2)}) collective-permute-start(bf16[288,1152]{1,0:T(8,128)(2,1)S(1)} %copy-done.1), channel_id=1, source_target_pairs={{0,2},{2,0},{1,3},{3,1},{4,6},{6,4},{5,7},{7,5},{8,10},{10,8},{9,1... | collective-permute-start | bytes 1990664 | tf_op jit(solution)/shard_map/ppermute | solution.py:285
  13.9 6.0 %collective-permute-start.1 = (bf16[288,1152]{1,0:T(8,128)(2,1)S(1)}, bf16[288,1152]{1,0:T(8,128)(2,1)}, u32[]{:S(2)}, u32[]{:S(2)}) collective-permute-start(bf16[288,1152]{1,0:T(8,128)(2,1)S(1)} %copy-done.1), channel_id=1, source_target_pairs={{0,1},{1,0},{2,3},{3,2},{4,5},{5,4},{6,7},{7,6},{8,9},{9,8},{10,11... | collective-permute-start | bytes 1990664 | tf_op jit(solution)/shard_map/ppermute | solution.py:39
  20.0 0.1 shard_map.78
  20.1 32.8 %all_gather.6.refs_1_.refs_0_ = bf16[384,1152]{1,0:T(8,128)(2,1)S(1)} all-gather(bf16[48,1152]{1,0:T(8,128)(2,1)S(1)} %shard_map.78), channel_id=1, replica_groups=mesh['xh'=2,'zh'=8,'zl'=2,'y'=4,'xl'=2,'c'=2] {'zh'}, dimensions={0}, use_global_device_ids=true | all-gather | bytes 995328 | tf_op jit(solution)/shard_map/all_gather | solution.py:291
  52.9 0.0 collective-permute-done.refs_4_
  52.9 6.5 %collective-permute-start.2 = (bf16[288,1152]{1,0:T(8,128)(2,1)S(1)}, bf16[288,1152]{1,0:T(8,128)(2,1)}, u32[]{:S(2)}, u32[]{:S(2)}) collective-permute-start(bf16[288,1152]{1,0:T(8,128)(2,1)S(1)} %collective-permute-done.refs_4_), channel_id=1, source_target_pairs={{0,1},{1,0},{2,3},{3,2},{4,5},{5,4},{6,7},{7,6},{8,9},{9,8},{10,11... | collective-permute-start | bytes 1990664 | tf_op jit(solution)/shard_map/ppermute | solution.py:39
  59.4 1.0 fusion
  60.4 3.3 %collective-permute-start.4 = (bf16[192,1152]{1,0:T(8,128)(2,1)}, bf16[192,1152]{1,0:T(8,128)(2,1)S(1)}, u32[]{:S(2)}, u32[]{:S(2)}) collective-permute-start(bf16[192,1152]{1,0:T(8,128)(2,1)} %get-tuple-element.15), channel_id=1, source_target_pairs={{0,16},{16,32},{32,48},{48,64},{64,80},{80,96},{96,112},{112,128},... | collective-permute-start | bytes 1327112 | tf_op jit(solution)/shard_map/ppermute | solution.py:35
  63.7 3.2 %collective-permute-start.5 = (bf16[192,1152]{1,0:T(8,128)(2,1)}, bf16[192,1152]{1,0:T(8,128)(2,1)S(1)}, u32[]{:S(2)}, u32[]{:S(2)}) collective-permute-start(bf16[192,1152]{1,0:T(8,128)(2,1)} %get-tuple-element.14), channel_id=1, source_target_pairs={{0,240},{16,0},{32,16},{48,32},{64,48},{80,64},{96,80},{112,96},{1... | collective-permute-start | bytes 1327112 | tf_op jit(solution)/shard_map/ppermute | solution.py:35
  68.9 0.1 stack.34.place_ref
  68.9 0.0 collective-permute-done.1.refs_5_
  68.9 0.0 collective-permute-done.2.refs_6_
  69.0 5.4 %shard_map.77 = (bf16[768,1152]{1,0:T(8,128)(2,1)S(1)}, bf16[1152,1152]{1,0:T(8,128)(2,1)}, bf16[96,1152]{1,0:T(8,128)(2,1)S(1)}, f32[8,128]{1,0:T(8,128)S(1)}) custom-call(s32[7]{0:T(128)S(1)} %stack.34.place_ref, bf16[768,1152]{1,0:T(8,128)(2,1)} %bitcast.7.from_ref.refs_3_, f32[1,1]{1,0:T(1,128)} %bitcast.24.refs_0_, f32[1,1]{1,0:T(1,128)} %bitcast.25.refs_1_, ...), custom_call_target="tpu_custom_call" | custom-call | tf_op jit(solution)/shard_map/pallas_call | solution.py:96
  74.4 3.0 %shard_map.79.refs_3_ = f32[768,1152]{1,0:T(8,128)S(1)} custom-call(s32[7]{0:T(128)S(1)} %stack.34.place_ref, bf16[768,1152]{1,0:T(8,128)(2,1)S(1)} %get-tuple-element.9.text_ref, f32[8,128]{1,0:T(8,128)S(1)} %get-tuple-element.10.refs_0_, bf16[384,1152]{1,0:T(8,128)(2,1)S(1)} %all_gather.6.refs_1_.refs_0_), custom_call_target="tpu_custom_call" | custom-call | flops 1358954496 | bytes 6193152 | tf_op jit(solution)/shard_map/pallas_call | solution.py:167
  77.4 0.0 collective-permute-done.5.refs_2_
  77.4 0.7 shard_map.80
  78.1 2.8 %collective-permute-start.6 = (bf16[768,1152]{1,0:T(8,128)(2,1)S(1)}, bf16[768,1152]{1,0:T(8,128)(2,1)S(1)}, u32[]{:S(2)}, u32[]{:S(2)}) collective-permute-start(bf16[768,1152]{1,0:T(8,128)(2,1)S(1)} %shard_map.80), channel_id=1, source_target_pairs={{0,1},{1,0},{2,3},{3,2},{4,5},{5,4},{6,7},{7,6},{8,9},{9,8},{10,11... | collective-permute-start | bytes 5308424 | tf_op jit(solution)/shard_map/ppermute | solution.py:39
  81.0 3.3 %shard_map.81.refs_2_ = f32[768,1152]{1,0:T(8,128)S(1)} custom-call(s32[7]{0:T(128)S(1)} %stack.34.place_ref, bf16[768,1152]{1,0:T(8,128)(2,1)S(1)} %get-tuple-element.9.text_ref, f32[8,128]{1,0:T(8,128)S(1)} %get-tuple-element.10.refs_0_, bf16[192,1152]{1,0:T(8,128)(2,1)S(1)} %collective-permute-done.4.refs_1_, ...), custom_call_target="tpu_custom_call" | custom-call | flops 1358954496 | bytes 6193152 | tf_op jit(solution)/shard_map/pallas_call | solution.py:167
  84.3 0.0 collective-permute-done.6.refs_1_
  84.3 6.1 %shard_map.82 = bf16[768,1152]{1,0:T(8,128)(2,1)} custom-call(s32[7]{0:T(128)S(1)} %stack.34.place_ref, bf16[768,1152]{1,0:T(8,128)(2,1)S(1)} %get-tuple-element.9.text_ref, f32[8,128]{1,0:T(8,128)S(1)} %get-tuple-element.10.refs_0_, bf16[768,1152]{1,0:T(8,128)(2,1)S(1)} %collective-permute-done.6.refs_1_, ...), custom_call_target="tpu_custom_call", output_to_operand_aliasing={{}: (5, {})} | custom-call | flops 2717908992 | bytes 7077888 | tf_op jit(solution)/shard_map/pallas_call | solution.py:167
  90.4 0.0 copy-start.3
  90.4 6.5 %all-to-all-start.1 = ((bf16[16,48,1152]{2,1,0:T(8,128)(2,1)}), bf16[16,48,1152]{2,1,0:T(8,128)(2,1)}, u32[]{:S(2)}, u32[]{:S(2)}) async-start(bf16[16,48,1152]{2,1,0:T(8,128)(2,1)} %bitcast.16), calls=%async_computation.1 | async-start | bytes 3538944 | tf_op jit(solution)/shard_map/all_to_all | solution.py:303
  97.0 2.5 %collective-permute-start.3 = (bf16[96,1152]{1,0:T(8,128)(2,1)S(1)}, bf16[96,1152]{1,0:T(8,128)(2,1)S(1)}, u32[]{:S(2)}, u32[]{:S(2)}) collective-permute-start(bf16[96,1152]{1,0:T(8,128)(2,1)S(1)} %get-tuple-element.8), channel_id=1, source_target_pairs={{0,1},{1,0},{2,3},{3,2},{4,5},{5,4},{6,7},{7,6},{8,9},{9,8},{10,11... | collective-permute-start | bytes 663560 | tf_op jit(solution)/shard_map/ppermute | solution.py:39
  99.5 0.6 convolution_bitcast_fusion.projected_ref
  100.1 0.5 collective-permute-done.3
  100.7 0.1 constant_dynamic-slice_fusion.columns_ref
  100.8 22.7 %all-to-all-done.1.from_ref = bf16[16,48,1152]{2,1,0:T(8,128)(2,1)} async-done(((bf16[16,48,1152]{2,1,0:T(8,128)(2,1)}), bf16[16,48,1152]{2,1,0:T(8,128)(2,1)}, u32[]{:S(2)}, u32[]{:S(2)}) %all-to-all-start.1) | async-done | bytes 1769504 | tf_op jit(solution)/shard_map/all_to_all | solution.py:303
  123.5 1.8 %shard_map.83.own_ref = bf16[48,1152]{1,0:T(8,128)(2,1)S(1)} custom-call(bf16[16,48,1152]{2,1,0:T(8,128)(2,1)} %all-to-all-done.1.from_ref, f32[48,1152]{1,0:T(8,128)S(1)} %convolution_bitcast_fusion.projected_ref), custom_call_target="tpu_custom_call" | custom-call | tf_op jit(solution)/shard_map/pallas_call | solution.py:229
  125.2 7.5 %all_gather.7.group_ref = bf16[192,1152]{1,0:T(8,128)(2,1)S(1)} all-gather(bf16[48,1152]{1,0:T(8,128)(2,1)S(1)} %shard_map.83.own_ref), channel_id=1, replica_groups=mesh['xh'=2,'zh'=8,'zl'=2,'y'=4,'xl'=2,'c'=2] {'xl','c'}, dimensions={0}, use_global_device_ids=true | all-gather | bytes 552960 | tf_op jit(solution)/shard_map/all_gather | solution.py:314
  132.8 2.4 %shard_map.84 = (bf16[48,1152]{1,0:T(8,128)(2,1)}, f32[288,1152]{1,0:T(8,128)}) custom-call(bf16[192,288]{1,0:T(8,128)(2,1)S(1)} %constant_dynamic-slice_fusion.columns_ref, bf16[192,1152]{1,0:T(8,128)(2,1)S(1)} %all_gather.7.group_ref, bf16[48,1152]{1,0:T(8,128)(2,1)S(1)} %shard_map.83.own_ref, bf16[1152,1152]{1,0:T(8,128)(2,1)S(1)} %copy-done), custom_call_target="tpu_custom_call" | custom-call | tf_op jit(solution)/shard_map/pallas_call | solution.py:259
  (11 shorter events, 0.1 us)
Async XLA Ops:
  2.9 7.8 %copy-start.1 = (bf16[288,1152]{1,0:T(8,128)(2,1)S(1)}, bf16[288,1152]{1,0:T(8,128)(2,1)}, u32[]{:S(2)}) copy-start(bf16[288,1152]{1,0:T(8,128)(2,1)} %refs_3_.1) | copy-start | bytes 1990660
  2.9 17.0 %copy-start.2 = (bf16[48,1152]{1,0:T(8,128)(2,1)S(1)}, bf16[48,1152]{1,0:T(8,128)(2,1)}, u32[]{:S(2)}) copy-start(bf16[48,1152]{1,0:T(8,128)(2,1)} %rows_ref.1) | copy-start | bytes 331780
  2.9 66.0 %all-to-all-start = ((bf16[16,48,1152]{2,1,0:T(8,128)(2,1)}), bf16[16,48,1152]{2,1,0:T(8,128)(2,1)}, u32[]{:S(2)}, u32[]{:S(2)}) async-start(bf16[16,48,1152]{2,1,0:T(8,128)(2,1)} %tile.2), calls=%async_computation | async-start | bytes 3538944 | tf_op jit(solution)/shard_map/all_to_all | solution.py:283
  10.7 42.2 %collective-permute-start = (bf16[288,1152]{1,0:T(8,128)(2,1)S(1)}, bf16[288,1152]{1,0:T(8,128)(2,1)S(1)}, u32[]{:S(2)}, u32[]{:S(2)}) collective-permute-start(bf16[288,1152]{1,0:T(8,128)(2,1)S(1)} %copy-done.1), channel_id=1, source_target_pairs={{0,2},{2,0},{1,3},{3,1},{4,6},{6,4},{5,7},{7,5},{8,10},{10,8},{9,1... | collective-permute-start | bytes 1990664 | tf_op jit(solution)/shard_map/ppermute | solution.py:285
  13.9 55.0 %collective-permute-start.1 = (bf16[288,1152]{1,0:T(8,128)(2,1)S(1)}, bf16[288,1152]{1,0:T(8,128)(2,1)}, u32[]{:S(2)}, u32[]{:S(2)}) collective-permute-start(bf16[288,1152]{1,0:T(8,128)(2,1)S(1)} %copy-done.1), channel_id=1, source_target_pairs={{0,1},{1,0},{2,3},{3,2},{4,5},{5,4},{6,7},{7,6},{8,9},{9,8},{10,11... | collective-permute-start | bytes 1990664 | tf_op jit(solution)/shard_map/ppermute | solution.py:39
  52.9 16.0 %collective-permute-start.2 = (bf16[288,1152]{1,0:T(8,128)(2,1)S(1)}, bf16[288,1152]{1,0:T(8,128)(2,1)}, u32[]{:S(2)}, u32[]{:S(2)}) collective-permute-start(bf16[288,1152]{1,0:T(8,128)(2,1)S(1)} %collective-permute-done.refs_4_), channel_id=1, source_target_pairs={{0,1},{1,0},{2,3},{3,2},{4,5},{5,4},{6,7},{7,6},{8,9},{9,8},{10,11... | collective-permute-start | bytes 1990664 | tf_op jit(solution)/shard_map/ppermute | solution.py:39
  60.4 17.0 %collective-permute-start.4 = (bf16[192,1152]{1,0:T(8,128)(2,1)}, bf16[192,1152]{1,0:T(8,128)(2,1)S(1)}, u32[]{:S(2)}, u32[]{:S(2)}) collective-permute-start(bf16[192,1152]{1,0:T(8,128)(2,1)} %get-tuple-element.15), channel_id=1, source_target_pairs={{0,16},{16,32},{32,48},{48,64},{64,80},{80,96},{96,112},{112,128},... | collective-permute-start | bytes 1327112 | tf_op jit(solution)/shard_map/ppermute | solution.py:35
  63.7 13.8 %collective-permute-start.5 = (bf16[192,1152]{1,0:T(8,128)(2,1)}, bf16[192,1152]{1,0:T(8,128)(2,1)S(1)}, u32[]{:S(2)}, u32[]{:S(2)}) collective-permute-start(bf16[192,1152]{1,0:T(8,128)(2,1)} %get-tuple-element.14), channel_id=1, source_target_pairs={{0,240},{16,0},{32,16},{48,32},{64,48},{80,64},{96,80},{112,96},{1... | collective-permute-start | bytes 1327112 | tf_op jit(solution)/shard_map/ppermute | solution.py:35
  78.1 6.2 %collective-permute-start.6 = (bf16[768,1152]{1,0:T(8,128)(2,1)S(1)}, bf16[768,1152]{1,0:T(8,128)(2,1)S(1)}, u32[]{:S(2)}, u32[]{:S(2)}) collective-permute-start(bf16[768,1152]{1,0:T(8,128)(2,1)S(1)} %shard_map.80), channel_id=1, source_target_pairs={{0,1},{1,0},{2,3},{3,2},{4,5},{5,4},{6,7},{7,6},{8,9},{9,8},{10,11... | collective-permute-start | bytes 5308424 | tf_op jit(solution)/shard_map/ppermute | solution.py:39
  90.4 9.1 %copy-start = (bf16[1152,1152]{1,0:T(8,128)(2,1)S(1)}, bf16[1152,1152]{1,0:T(8,128)(2,1)}, u32[]{:S(2)}) copy-start(bf16[1152,1152]{1,0:T(8,128)(2,1)} %get-tuple-element.11.from_ref) | copy-start | bytes 7962628
  90.4 9.1 %copy-start.3 = (bf16[48,1152]{1,0:T(8,128)(2,1)S(1)}, bf16[48,1152]{1,0:T(8,128)(2,1)}, u32[]{:S(2)}) copy-start(bf16[48,1152]{1,0:T(8,128)(2,1)} %param.6) | copy-start | bytes 331780
  90.4 33.0 %all-to-all-start.1 = ((bf16[16,48,1152]{2,1,0:T(8,128)(2,1)}), bf16[16,48,1152]{2,1,0:T(8,128)(2,1)}, u32[]{:S(2)}, u32[]{:S(2)}) async-start(bf16[16,48,1152]{2,1,0:T(8,128)(2,1)} %bitcast.16), calls=%async_computation.1 | async-start | bytes 3538944 | tf_op jit(solution)/shard_map/all_to_all | solution.py:303
  97.0 3.6 %collective-permute-start.3 = (bf16[96,1152]{1,0:T(8,128)(2,1)S(1)}, bf16[96,1152]{1,0:T(8,128)(2,1)S(1)}, u32[]{:S(2)}, u32[]{:S(2)}) collective-permute-start(bf16[96,1152]{1,0:T(8,128)(2,1)S(1)} %get-tuple-element.8), channel_id=1, source_target_pairs={{0,1},{1,0},{2,3},{3,2},{4,5},{5,4},{6,7},{7,6},{8,9},{9,8},{10,11... | collective-permute-start | bytes 663560 | tf_op jit(solution)/shard_map/ppermute | solution.py:39

commit v7 on v6

--- a/solution.py
+++ b/solution.py
@@ -144,7 +144,7 @@
         return 0
 
     steps = text_ref.shape[0] // block
-    lax.fori_loop(0, steps, step, 0)
+    lax.fori_loop(0, steps, step, 0, unroll=True)
     if own_rows:
         own = pl.ds(pl.multiple_of(place_ref[5], 16), own_rows)
         image = images_ref[pl.ds(pl.multiple_of(place_ref[6], 16), own_rows)].astype(jnp.float32)

time: 136 us -> 135 us (level)
  no operation moved by 1% of the time
where the time goes in v7:
time: 135 us
  starting transfers between devices  41.8 us (31%)
  blocking collectives  40.4 us (30%)
  waiting for transfers between devices  23.2 us (17%)
  Pallas kernels  22.3 us (17%)
  local copies, waits for them, and re-layouts  3.49 us (3%)
  between operations  2.83 us (2%)
    all_gather x1, blocking collectives, body(): even = lax.all_gather(own, 'zh', axis=0, tiled=True)  32.8 us
    all_to_all x1, waiting for transfers between devices, body(): lax.all_to_all(partial, PLANE, 0, 0, tiled=True).reshape(plane, rows, width)  22.7 us
    ppermute x4, starting transfers between devices, other_core(): return lax.ppermute(array, 'c', shift(1, 2))  17.8 us
    pallas_call x3, Pallas kernels, meet(): pl.pallas_call(functools.partial(meet_kernel, count // 2 if last else cou...  11.9 us
    all_to_all x1, starting transfers between devices, body(): lax.all_to_all(jnp.tile(features, (plane, 1)), PLANE, 0, 0, tiled=True)  7.76 us
    all_gather x1, blocking collectives, body(): group_grad = lax.all_gather(proj_grad, FSDP, axis=0, tiled=True)  7.54 us
    all_to_all x1, starting transfers between devices, body(): lax.all_to_all(partial, PLANE, 0, 0, tiled=True).reshape(plane, rows, width)  6.53 us
    ppermute x2, starting transfers between devices, along_z(): return lax.ppermute(array, LINE, shift(step % 16, 16))  6.48 us
  transfers between devices with their start and end apart: 9, of which 2 were waited for; matrix products, arithmetic and copies ran while one was open for 1% of the time, Pallas kernels for 9%

profile of v7, /device:TPU:1, one launch (start us, length us, event | category | flops | bytes accessed | tf_op | source)
XLA Modules:
  0.0 134.6 jit_solution(7912248842673322747)
XLA Ops:
  0.6 2.3 %tile.2 = bf16[16,48,1152]{2,1,0:T(8,128)(2,1)} broadcast(bf16[48,1152]{1,0:T(8,128)(2,1)} %param.6), dimensions={1,2} | broadcast | bytes 1880064 | tf_op jit(solution)/shard_map/tile | solution.py:283
  2.9 7.8 %all-to-all-start = ((bf16[16,48,1152]{2,1,0:T(8,128)(2,1)}), bf16[16,48,1152]{2,1,0:T(8,128)(2,1)}, u32[]{:S(2)}, u32[]{:S(2)}) async-start(bf16[16,48,1152]{2,1,0:T(8,128)(2,1)} %tile.2), calls=%async_computation | async-start | bytes 3538944 | tf_op jit(solution)/shard_map/all_to_all | solution.py:283
  10.7 3.2 %collective-permute-start = (bf16[288,1152]{1,0:T(8,128)(2,1)S(1)}, bf16[288,1152]{1,0:T(8,128)(2,1)S(1)}, u32[]{:S(2)}, u32[]{:S(2)}) collective-permute-start(bf16[288,1152]{1,0:T(8,128)(2,1)S(1)} %copy-done.1), channel_id=1, source_target_pairs={{0,2},{2,0},{1,3},{3,1},{4,6},{6,4},{5,7},{7,5},{8,10},{10,8},{9,1... | collective-permute-start | bytes 1990664 | tf_op jit(solution)/shard_map/ppermute | solution.py:285
  13.9 6.0 %collective-permute-start.1 = (bf16[288,1152]{1,0:T(8,128)(2,1)S(1)}, bf16[288,1152]{1,0:T(8,128)(2,1)}, u32[]{:S(2)}, u32[]{:S(2)}) collective-permute-start(bf16[288,1152]{1,0:T(8,128)(2,1)S(1)} %copy-done.1), channel_id=1, source_target_pairs={{0,1},{1,0},{2,3},{3,2},{4,5},{5,4},{6,7},{7,6},{8,9},{9,8},{10,11... | collective-permute-start | bytes 1990664 | tf_op jit(solution)/shard_map/ppermute | solution.py:39
  20.0 0.1 shard_map.78
  20.1 32.8 %all_gather.6.refs_1_.refs_0_ = bf16[384,1152]{1,0:T(8,128)(2,1)S(1)} all-gather(bf16[48,1152]{1,0:T(8,128)(2,1)S(1)} %shard_map.78), channel_id=1, replica_groups=mesh['xh'=2,'zh'=8,'zl'=2,'y'=4,'xl'=2,'c'=2] {'zh'}, dimensions={0}, use_global_device_ids=true | all-gather | bytes 995328 | tf_op jit(solution)/shard_map/all_gather | solution.py:291
  52.9 0.0 collective-permute-done.refs_4_
  52.9 6.5 %collective-permute-start.2 = (bf16[288,1152]{1,0:T(8,128)(2,1)S(1)}, bf16[288,1152]{1,0:T(8,128)(2,1)}, u32[]{:S(2)}, u32[]{:S(2)}) collective-permute-start(bf16[288,1152]{1,0:T(8,128)(2,1)S(1)} %collective-permute-done.refs_4_), channel_id=1, source_target_pairs={{0,1},{1,0},{2,3},{3,2},{4,5},{5,4},{6,7},{7,6},{8,9},{9,8},{10,11... | collective-permute-start | bytes 1990664 | tf_op jit(solution)/shard_map/ppermute | solution.py:39
  59.4 1.0 fusion
  60.4 3.3 %collective-permute-start.4 = (bf16[192,1152]{1,0:T(8,128)(2,1)}, bf16[192,1152]{1,0:T(8,128)(2,1)S(1)}, u32[]{:S(2)}, u32[]{:S(2)}) collective-permute-start(bf16[192,1152]{1,0:T(8,128)(2,1)} %get-tuple-element.15), channel_id=1, source_target_pairs={{0,16},{16,32},{32,48},{48,64},{64,80},{80,96},{96,112},{112,128},... | collective-permute-start | bytes 1327112 | tf_op jit(solution)/shard_map/ppermute | solution.py:35
  63.7 3.2 %collective-permute-start.5 = (bf16[192,1152]{1,0:T(8,128)(2,1)}, bf16[192,1152]{1,0:T(8,128)(2,1)S(1)}, u32[]{:S(2)}, u32[]{:S(2)}) collective-permute-start(bf16[192,1152]{1,0:T(8,128)(2,1)} %get-tuple-element.14), channel_id=1, source_target_pairs={{0,240},{16,0},{32,16},{48,32},{64,48},{80,64},{96,80},{112,96},{1... | collective-permute-start | bytes 1327112 | tf_op jit(solution)/shard_map/ppermute | solution.py:35
  68.9 0.1 stack.34.place_ref
  68.9 0.0 collective-permute-done.1.refs_5_
  68.9 0.0 collective-permute-done.2.refs_6_
  68.9 0.0 all-to-all-done
  69.0 5.4 %shard_map.77 = (bf16[768,1152]{1,0:T(8,128)(2,1)S(1)}, bf16[1152,1152]{1,0:T(8,128)(2,1)}, bf16[96,1152]{1,0:T(8,128)(2,1)S(1)}, f32[8,128]{1,0:T(8,128)S(1)}) custom-call(s32[7]{0:T(128)S(1)} %stack.34.place_ref, bf16[768,1152]{1,0:T(8,128)(2,1)} %bitcast.7.from_ref.refs_3_, f32[1,1]{1,0:T(1,128)} %bitcast.24.refs_0_, f32[1,1]{1,0:T(1,128)} %bitcast.25.refs_1_, ...), custom_call_target="tpu_custom_call" | custom-call | tf_op jit(solution)/shard_map/pallas_call | solution.py:96
  74.4 3.0 %shard_map.79.refs_3_ = f32[768,1152]{1,0:T(8,128)S(1)} custom-call(s32[7]{0:T(128)S(1)} %stack.34.place_ref, bf16[768,1152]{1,0:T(8,128)(2,1)S(1)} %get-tuple-element.9.text_ref, f32[8,128]{1,0:T(8,128)S(1)} %get-tuple-element.10.refs_0_, bf16[384,1152]{1,0:T(8,128)(2,1)S(1)} %all_gather.6.refs_1_.refs_0_), custom_call_target="tpu_custom_call" | custom-call | flops 1358954496 | bytes 6193152 | tf_op jit(solution)/shard_map/pallas_call | solution.py:167
  77.4 0.0 collective-permute-done.4.refs_1_
  77.4 0.7 shard_map.80
  78.1 2.8 %collective-permute-start.6 = (bf16[768,1152]{1,0:T(8,128)(2,1)S(1)}, bf16[768,1152]{1,0:T(8,128)(2,1)S(1)}, u32[]{:S(2)}, u32[]{:S(2)}) collective-permute-start(bf16[768,1152]{1,0:T(8,128)(2,1)S(1)} %shard_map.80), channel_id=1, source_target_pairs={{0,1},{1,0},{2,3},{3,2},{4,5},{5,4},{6,7},{7,6},{8,9},{9,8},{10,11... | collective-permute-start | bytes 5308424 | tf_op jit(solution)/shard_map/ppermute | solution.py:39
  81.0 3.3 %shard_map.81.refs_2_ = f32[768,1152]{1,0:T(8,128)S(1)} custom-call(s32[7]{0:T(128)S(1)} %stack.34.place_ref, bf16[768,1152]{1,0:T(8,128)(2,1)S(1)} %get-tuple-element.9.text_ref, f32[8,128]{1,0:T(8,128)S(1)} %get-tuple-element.10.refs_0_, bf16[192,1152]{1,0:T(8,128)(2,1)S(1)} %collective-permute-done.4.refs_1_, ...), custom_call_target="tpu_custom_call" | custom-call | flops 1358954496 | bytes 6193152 | tf_op jit(solution)/shard_map/pallas_call | solution.py:167
  84.3 5.5 %shard_map.82 = bf16[768,1152]{1,0:T(8,128)(2,1)} custom-call(s32[7]{0:T(128)S(1)} %stack.34.place_ref, bf16[768,1152]{1,0:T(8,128)(2,1)S(1)} %get-tuple-element.9.text_ref, f32[8,128]{1,0:T(8,128)S(1)} %get-tuple-element.10.refs_0_, bf16[768,1152]{1,0:T(8,128)(2,1)S(1)} %collective-permute-done.6.refs_1_, ...), custom_call_target="tpu_custom_call", output_to_operand_aliasing={{}: (5, {})} | custom-call | flops 2717908992 | bytes 7077888 | tf_op jit(solution)/shard_map/pallas_call | solution.py:167
  89.9 0.0 copy-start.3
  89.9 6.5 %all-to-all-start.1 = ((bf16[16,48,1152]{2,1,0:T(8,128)(2,1)}), bf16[16,48,1152]{2,1,0:T(8,128)(2,1)}, u32[]{:S(2)}, u32[]{:S(2)}) async-start(bf16[16,48,1152]{2,1,0:T(8,128)(2,1)} %bitcast.16), calls=%async_computation.1 | async-start | bytes 3538944 | tf_op jit(solution)/shard_map/all_to_all | solution.py:303
  96.4 2.5 %collective-permute-start.3 = (bf16[96,1152]{1,0:T(8,128)(2,1)S(1)}, bf16[96,1152]{1,0:T(8,128)(2,1)S(1)}, u32[]{:S(2)}, u32[]{:S(2)}) collective-permute-start(bf16[96,1152]{1,0:T(8,128)(2,1)S(1)} %get-tuple-element.8), channel_id=1, source_target_pairs={{0,1},{1,0},{2,3},{3,2},{4,5},{5,4},{6,7},{7,6},{8,9},{9,8},{10,11... | collective-permute-start | bytes 663560 | tf_op jit(solution)/shard_map/ppermute | solution.py:39
  99.0 0.6 convolution_bitcast_fusion.projected_ref
  99.6 0.5 collective-permute-done.3
  100.1 0.1 constant_dynamic-slice_fusion.columns_ref
  100.3 22.7 %all-to-all-done.1.from_ref = bf16[16,48,1152]{2,1,0:T(8,128)(2,1)} async-done(((bf16[16,48,1152]{2,1,0:T(8,128)(2,1)}), bf16[16,48,1152]{2,1,0:T(8,128)(2,1)}, u32[]{:S(2)}, u32[]{:S(2)}) %all-to-all-start.1) | async-done | bytes 1769504 | tf_op jit(solution)/shard_map/all_to_all | solution.py:303
  122.9 1.8 %shard_map.83.own_ref = bf16[48,1152]{1,0:T(8,128)(2,1)S(1)} custom-call(bf16[16,48,1152]{2,1,0:T(8,128)(2,1)} %all-to-all-done.1.from_ref, f32[48,1152]{1,0:T(8,128)S(1)} %convolution_bitcast_fusion.projected_ref), custom_call_target="tpu_custom_call" | custom-call | tf_op jit(solution)/shard_map/pallas_call | solution.py:229
  124.7 7.5 %all_gather.7.group_ref = bf16[192,1152]{1,0:T(8,128)(2,1)S(1)} all-gather(bf16[48,1152]{1,0:T(8,128)(2,1)S(1)} %shard_map.83.own_ref), channel_id=1, replica_groups=mesh['xh'=2,'zh'=8,'zl'=2,'y'=4,'xl'=2,'c'=2] {'xl','c'}, dimensions={0}, use_global_device_ids=true | all-gather | bytes 552960 | tf_op jit(solution)/shard_map/all_gather | solution.py:314
  132.2 2.4 %shard_map.84 = (bf16[48,1152]{1,0:T(8,128)(2,1)}, f32[288,1152]{1,0:T(8,128)}) custom-call(bf16[192,288]{1,0:T(8,128)(2,1)S(1)} %constant_dynamic-slice_fusion.columns_ref, bf16[192,1152]{1,0:T(8,128)(2,1)S(1)} %all_gather.7.group_ref, bf16[48,1152]{1,0:T(8,128)(2,1)S(1)} %shard_map.83.own_ref, bf16[1152,1152]{1,0:T(8,128)(2,1)S(1)} %copy-done), custom_call_target="tpu_custom_call" | custom-call | tf_op jit(solution)/shard_map/pallas_call | solution.py:259
  (11 shorter events, 0.1 us)
Async XLA Ops:
  2.9 7.8 %copy-start.1 = (bf16[288,1152]{1,0:T(8,128)(2,1)S(1)}, bf16[288,1152]{1,0:T(8,128)(2,1)}, u32[]{:S(2)}) copy-start(bf16[288,1152]{1,0:T(8,128)(2,1)} %refs_3_.1) | copy-start | bytes 1990660
  2.9 17.0 %copy-start.2 = (bf16[48,1152]{1,0:T(8,128)(2,1)S(1)}, bf16[48,1152]{1,0:T(8,128)(2,1)}, u32[]{:S(2)}) copy-start(bf16[48,1152]{1,0:T(8,128)(2,1)} %rows_ref.1) | copy-start | bytes 331780
  2.9 66.0 %all-to-all-start = ((bf16[16,48,1152]{2,1,0:T(8,128)(2,1)}), bf16[16,48,1152]{2,1,0:T(8,128)(2,1)}, u32[]{:S(2)}, u32[]{:S(2)}) async-start(bf16[16,48,1152]{2,1,0:T(8,128)(2,1)} %tile.2), calls=%async_computation | async-start | bytes 3538944 | tf_op jit(solution)/shard_map/all_to_all | solution.py:283
  10.7 42.2 %collective-permute-start = (bf16[288,1152]{1,0:T(8,128)(2,1)S(1)}, bf16[288,1152]{1,0:T(8,128)(2,1)S(1)}, u32[]{:S(2)}, u32[]{:S(2)}) collective-permute-start(bf16[288,1152]{1,0:T(8,128)(2,1)S(1)} %copy-done.1), channel_id=1, source_target_pairs={{0,2},{2,0},{1,3},{3,1},{4,6},{6,4},{5,7},{7,5},{8,10},{10,8},{9,1... | collective-permute-start | bytes 1990664 | tf_op jit(solution)/shard_map/ppermute | solution.py:285
  13.9 55.0 %collective-permute-start.1 = (bf16[288,1152]{1,0:T(8,128)(2,1)S(1)}, bf16[288,1152]{1,0:T(8,128)(2,1)}, u32[]{:S(2)}, u32[]{:S(2)}) collective-permute-start(bf16[288,1152]{1,0:T(8,128)(2,1)S(1)} %copy-done.1), channel_id=1, source_target_pairs={{0,1},{1,0},{2,3},{3,2},{4,5},{5,4},{6,7},{7,6},{8,9},{9,8},{10,11... | collective-permute-start | bytes 1990664 | tf_op jit(solution)/shard_map/ppermute | solution.py:39
  52.9 16.0 %collective-permute-start.2 = (bf16[288,1152]{1,0:T(8,128)(2,1)S(1)}, bf16[288,1152]{1,0:T(8,128)(2,1)}, u32[]{:S(2)}, u32[]{:S(2)}) collective-permute-start(bf16[288,1152]{1,0:T(8,128)(2,1)S(1)} %collective-permute-done.refs_4_), channel_id=1, source_target_pairs={{0,1},{1,0},{2,3},{3,2},{4,5},{5,4},{6,7},{7,6},{8,9},{9,8},{10,11... | collective-permute-start | bytes 1990664 | tf_op jit(solution)/shard_map/ppermute | solution.py:39
  60.4 17.0 %collective-permute-start.4 = (bf16[192,1152]{1,0:T(8,128)(2,1)}, bf16[192,1152]{1,0:T(8,128)(2,1)S(1)}, u32[]{:S(2)}, u32[]{:S(2)}) collective-permute-start(bf16[192,1152]{1,0:T(8,128)(2,1)} %get-tuple-element.15), channel_id=1, source_target_pairs={{0,16},{16,32},{32,48},{48,64},{64,80},{80,96},{96,112},{112,128},... | collective-permute-start | bytes 1327112 | tf_op jit(solution)/shard_map/ppermute | solution.py:35
  63.7 13.8 %collective-permute-start.5 = (bf16[192,1152]{1,0:T(8,128)(2,1)}, bf16[192,1152]{1,0:T(8,128)(2,1)S(1)}, u32[]{:S(2)}, u32[]{:S(2)}) collective-permute-start(bf16[192,1152]{1,0:T(8,128)(2,1)} %get-tuple-element.14), channel_id=1, source_target_pairs={{0,240},{16,0},{32,16},{48,32},{64,48},{80,64},{96,80},{112,96},{1... | collective-permute-start | bytes 1327112 | tf_op jit(solution)/shard_map/ppermute | solution.py:35
  78.1 6.2 %collective-permute-start.6 = (bf16[768,1152]{1,0:T(8,128)(2,1)S(1)}, bf16[768,1152]{1,0:T(8,128)(2,1)S(1)}, u32[]{:S(2)}, u32[]{:S(2)}) collective-permute-start(bf16[768,1152]{1,0:T(8,128)(2,1)S(1)} %shard_map.80), channel_id=1, source_target_pairs={{0,1},{1,0},{2,3},{3,2},{4,5},{5,4},{6,7},{7,6},{8,9},{9,8},{10,11... | collective-permute-start | bytes 5308424 | tf_op jit(solution)/shard_map/ppermute | solution.py:39
  89.9 9.1 %copy-start = (bf16[1152,1152]{1,0:T(8,128)(2,1)S(1)}, bf16[1152,1152]{1,0:T(8,128)(2,1)}, u32[]{:S(2)}) copy-start(bf16[1152,1152]{1,0:T(8,128)(2,1)} %get-tuple-element.11.from_ref) | copy-start | bytes 7962628
  89.9 9.1 %copy-start.3 = (bf16[48,1152]{1,0:T(8,128)(2,1)S(1)}, bf16[48,1152]{1,0:T(8,128)(2,1)}, u32[]{:S(2)}) copy-start(bf16[48,1152]{1,0:T(8,128)(2,1)} %param.6) | copy-start | bytes 331780
  89.9 33.0 %all-to-all-start.1 = ((bf16[16,48,1152]{2,1,0:T(8,128)(2,1)}), bf16[16,48,1152]{2,1,0:T(8,128)(2,1)}, u32[]{:S(2)}, u32[]{:S(2)}) async-start(bf16[16,48,1152]{2,1,0:T(8,128)(2,1)} %bitcast.16), calls=%async_computation.1 | async-start | bytes 3538944 | tf_op jit(solution)/shard_map/all_to_all | solution.py:303
  96.4 3.6 %collective-permute-start.3 = (bf16[96,1152]{1,0:T(8,128)(2,1)S(1)}, bf16[96,1152]{1,0:T(8,128)(2,1)S(1)}, u32[]{:S(2)}, u32[]{:S(2)}) collective-permute-start(bf16[96,1152]{1,0:T(8,128)(2,1)S(1)} %get-tuple-element.8), channel_id=1, source_target_pairs={{0,1},{1,0},{2,3},{3,2},{4,5},{5,4},{6,7},{7,6},{8,9},{9,8},{10,11... | collective-permute-start | bytes 663560 | tf_op jit(solution)/shard_map/ppermute | solution.py:39
